TPU v7x, 128 devices: a whole 4x4x4 slice. The times are simulated.
128 devices in a mesh: ctx: 16 (over x, y), head: 8 (over z, core).
Axes of the slice: x: 4, y: 4, z: 4, core: 2. Of those that a mesh axis runs over, the one named last changes fastest.
Arguments:
- x_rows: bfloat16 [32768, 8192], P(('ctx', 'head')), may hold values from -6 to 6
- b_rows: bfloat16 [32768, 1024], P(('ctx', 'head')), may hold values from -0.5 to 0.5
- c_rows: bfloat16 [32768, 1024], P(('ctx', 'head')), may hold values from -6 to 6
- dt_rows: bfloat16 [32768, 128], P(('ctx', 'head')), may hold values from -3 to 3
- destination: int32 [256], P('ctx'), may hold values from 0 to 255, as said below
- doc_start: int32 [32768], P('ctx'), may hold values 0 or 1
- a_log: float32 [128], P('head'), may hold values from -9 to -1
- dt_bias: float32 [128], P('head'), may hold values from -8 to 0
- d_skip: float32 [128], P('head'), may hold values from 0.5 to 1.5
- cotangent: bfloat16 [32768, 8192], P('ctx', 'head'), may hold values from -6 to 6
Outputs:
- ssd_output: bfloat16 [32768, 8192], P('ctx', 'head')
- input_grad: bfloat16 [32768, 8192], P('ctx', 'head')
Inputs may be any that keep to these rules, and one draw needn't show every extreme that they name: Entry p names the packed block of loader block p, and every packed block is named once. The owner of a block is destination // 16; of the 16 blocks of one loader shard at most 2 go to one owner, and in every draw some loader shard sends 2 to one owner.
All inputs are finite; a program needn't handle non-finite values. No bound on the sum of `doc_start` on one device may be relied on, other than what follows from the above.
Results may differ from a plain program's by a relative error of at most 0.004.
Values may be sent and summed in bfloat16 or wider, within the bound.
No kernel may reach another device: no remote copies, remote signals or barrier semaphores. Data moves between devices by JAX's collectives and lax.ppermute only.
A program may use at most 192 MiB of HBM per device.

v0:
```python
from functools import partial

import jax
import jax.numpy as jnp
from jax import lax
from jax.sharding import PartitionSpec as P

STATE = 128
BLOCK = 256


def entering(shard, axis, combine, identity, reverse):
    peers, here = (lax.axis_size(axis), lax.axis_index(axis))
    everything = jax.tree.map(lambda part: lax.all_gather(part, axis), shard)
    start = jax.tree.map(
        lambda part, zero: jnp.broadcast_to(jnp.asarray(zero, part.dtype), part.shape),
        shard,
        identity,
    )

    def hop(k, before):
        at = peers - 1 - k if reverse else k
        reached = at > here if reverse else at < here
        new = combine(before, jax.tree.map(lambda part: part[at], everything))
        return jax.tree.map(lambda a, b: jnp.where(reached, a, b), new, before)

    return lax.fori_loop(0, peers, hop, start)


def combine_states(earlier, later):
    return (earlier[0] * later[0], later[0][:, None, None] * earlier[1] + later[1])


def block_local(blocks, skip_gain, groups, head_dim):
    x_blk, b_blk, c_blk, rate_blk, step_blk, start_blk, cot_blk = blocks
    block_size, head_count = rate_blk.shape
    per_group = head_count // groups
    state_size = b_blk.shape[1] // groups
    log_decay = jnp.cumsum(rate_blk, axis=0)
    segment = jnp.cumsum(start_blk)
    row_index = lax.broadcasted_iota(jnp.int32, (block_size, block_size), 0)
    col_index = lax.broadcasted_iota(jnp.int32, (block_size, block_size), 1)
    causal = (col_index <= row_index) & (segment[:, None] == segment[None, :])
    decay_rows = log_decay.T
    log_gap = decay_rows[:, :, None] - decay_rows[:, None, :]
    decay = jnp.exp(jnp.where(causal[None], log_gap, -jnp.inf))
    b_three = b_blk.reshape(block_size, groups, state_size)
    c_three = c_blk.reshape(block_size, groups, state_size)
    scores = jnp.einsum("tgs,ugs->gtu", c_three, b_three, preferred_element_type=jnp.float32)
    masked = scores[:, None] * decay.reshape(groups, per_group, block_size, block_size)
    forward_weights = (masked * step_blk.T.reshape(groups, per_group, 1, block_size)).astype(
        jnp.bfloat16
    )
    backward_weights = masked.astype(jnp.bfloat16)
    x_four = x_blk.reshape(block_size, groups, per_group, head_dim)
    cot_four = cot_blk.reshape(block_size, groups, per_group, head_dim)
    step_four = step_blk.reshape(block_size, groups, per_group, 1)
    y_local = (
        jnp.einsum("gjtu,ugjp->tgjp", forward_weights, x_four, preferred_element_type=jnp.float32)
        + skip_gain * x_four
    )
    grad_diag = jnp.einsum(
        "gjut,ugjp->tgjp", backward_weights, cot_four, preferred_element_type=jnp.float32
    )
    grad_local = step_four * grad_diag + skip_gain * cot_four
    entry_scale = jnp.exp(log_decay) * (segment == 0)[:, None].astype(jnp.float32)
    exit_scale = jnp.exp(log_decay[-1][None, :] - log_decay) * (segment == segment[-1])[
        :, None
    ].astype(jnp.float32)
    block_decay = jnp.exp(log_decay[-1]) * (segment[-1] == 0).astype(jnp.float32)
    step_exit = step_blk * exit_scale
    x_scaled = (x_four * step_exit.reshape(block_size, groups, per_group, 1)).astype(jnp.bfloat16)
    state_part = jnp.einsum("ugjp,ugs->gjps", x_scaled, b_three, preferred_element_type=jnp.float32)
    cot_scaled = (cot_four * entry_scale.reshape(block_size, groups, per_group, 1)).astype(
        jnp.bfloat16
    )
    grad_part = jnp.einsum(
        "ugjp,ugs->gjps", cot_scaled, c_three, preferred_element_type=jnp.float32
    )
    state_part = state_part.reshape(head_count, head_dim, state_size)
    grad_part = grad_part.reshape(head_count, head_dim, state_size)
    return (y_local, grad_local, state_part, grad_part, block_decay, entry_scale, step_exit)


def run_states(carry, block_parts):
    decay_acc, state_acc = carry
    part_decay, part_state = block_parts
    updated = (decay_acc * part_decay, part_decay[:, None, None] * state_acc + part_state)
    return (updated, (decay_acc, state_acc))


def body(
    x_rows, b_rows, c_rows, dt_rows, destination, doc_start, a_log, dt_bias, d_skip, cotangent
):
    x_heads, b_heads, c_heads, dt_heads = (
        lax.all_to_all(x_rows, "head", split_axis=1, concat_axis=0, tiled=True),
        lax.all_to_all(b_rows, "head", split_axis=1, concat_axis=0, tiled=True),
        lax.all_to_all(c_rows, "head", split_axis=1, concat_axis=0, tiled=True),
        lax.all_to_all(dt_rows, "head", split_axis=1, concat_axis=0, tiled=True),
    )
    owners = lax.axis_size("ctx")
    tok_rows = x_heads.shape[0]
    piece_rows = tok_rows // owners
    owner_of = destination // owners
    position = destination % owners
    row_index = lax.broadcasted_iota(jnp.int32, (owners, owners), 0)
    col_index = lax.broadcasted_iota(jnp.int32, (owners, owners), 1)
    earlier_same = (owner_of[None, :] == owner_of[:, None]) & (col_index < row_index)
    rank_among = jnp.sum(earlier_same.astype(jnp.int32), axis=1)
    send_slot = owner_of * 2 + rank_among

    def pack_slots(source):
        col_count = source.shape[1]
        pieces = source.reshape(owners, piece_rows, col_count)
        filled = (
            jnp.zeros((owners * 2, piece_rows, col_count), source.dtype).at[send_slot].set(pieces)
        )
        return filled.reshape(owners, 2, piece_rows, col_count)

    labels = jnp.full((owners * 2,), -1, jnp.int32).at[send_slot].set(position).reshape(owners, 2)
    arrived = (
        lax.all_to_all(pack_slots(x_heads), "ctx", split_axis=0, concat_axis=0, tiled=True),
        lax.all_to_all(pack_slots(b_heads), "ctx", split_axis=0, concat_axis=0, tiled=True),
        lax.all_to_all(pack_slots(c_heads), "ctx", split_axis=0, concat_axis=0, tiled=True),
        lax.all_to_all(pack_slots(dt_heads), "ctx", split_axis=0, concat_axis=0, tiled=True),
        lax.all_to_all(labels, "ctx", split_axis=0, concat_axis=0, tiled=True),
    )
    target = arrived[4].reshape(owners * 2)
    target = jnp.where(target >= 0, target, owners)

    def unpack(received):
        col_count = received.shape[3]
        flat_rows = received.reshape(owners * 2, piece_rows, col_count)
        placed = (
            jnp.zeros((owners, piece_rows, col_count), received.dtype)
            .at[target]
            .set(flat_rows, mode="drop")
        )
        return placed.reshape(tok_rows, col_count)

    x_pack = unpack(arrived[0])
    b_pack = unpack(arrived[1])
    c_pack = unpack(arrived[2])
    dt_pack = unpack(arrived[3])
    head_count = a_log.shape[0]
    head_dim = x_pack.shape[1] // head_count
    groups = b_pack.shape[1] // STATE
    per_group = head_count // groups
    block_count = tok_rows // BLOCK
    step_size = jax.nn.softplus(dt_pack.astype(jnp.float32) + dt_bias)
    rate_log = -step_size * jnp.exp(a_log)
    skip_gain = d_skip.reshape(1, groups, per_group, 1)
    blocks = (
        x_pack.reshape(block_count, BLOCK, x_pack.shape[1]),
        b_pack.reshape(block_count, BLOCK, b_pack.shape[1]),
        c_pack.reshape(block_count, BLOCK, c_pack.shape[1]),
        rate_log.reshape(block_count, BLOCK, head_count),
        step_size.reshape(block_count, BLOCK, head_count),
        doc_start.reshape(block_count, BLOCK),
        cotangent.reshape(block_count, BLOCK, cotangent.shape[1]),
    )
    y_local, grad_local, state_parts, grad_parts, block_decay, entry_scale, step_exit = lax.map(
        partial(block_local, skip_gain=skip_gain, groups=groups, head_dim=head_dim), blocks
    )
    unit_decay = jnp.ones((head_count,), jnp.float32)
    zero_state = jnp.zeros(state_parts.shape[1:], jnp.float32)
    (own_decay, own_state), (decay_before, state_before) = lax.scan(
        run_states, (unit_decay, zero_state), (block_decay, state_parts)
    )
    (unused, own_grad), (decay_after, grad_after) = lax.scan(
        run_states, (unit_decay, zero_state), (block_decay, grad_parts), reverse=True
    )
    from_left = entering(
        (own_decay, own_state), "ctx", combine_states, (unit_decay, zero_state), False
    )[1]
    from_right = entering(
        (own_decay, own_grad), "ctx", combine_states, (unit_decay, zero_state), True
    )[1]
    state_in = state_before + decay_before[:, :, None, None] * from_left
    grad_in = grad_after + decay_after[:, :, None, None] * from_right
    state_round = state_in.astype(jnp.bfloat16).reshape(
        block_count, groups, per_group, head_dim, STATE
    )
    grad_round = grad_in.astype(jnp.bfloat16).reshape(
        block_count, groups, per_group, head_dim, STATE
    )
    c_all = c_pack.reshape(block_count, BLOCK, groups, STATE)
    b_all = b_pack.reshape(block_count, BLOCK, groups, STATE)
    y_off = jnp.einsum("ctgs,cgjps->ctgjp", c_all, state_round, preferred_element_type=jnp.float32)
    y_off = y_off * entry_scale.reshape(block_count, BLOCK, groups, per_group, 1)
    grad_off = jnp.einsum(
        "ctgs,cgjps->ctgjp", b_all, grad_round, preferred_element_type=jnp.float32
    )
    grad_off = grad_off * step_exit.reshape(block_count, BLOCK, groups, per_group, 1)
    ssd_output = (y_local + y_off).astype(jnp.bfloat16).reshape(tok_rows, x_pack.shape[1])
    input_grad = (grad_local + grad_off).astype(jnp.bfloat16).reshape(tok_rows, x_pack.shape[1])
    return (ssd_output, input_grad)


def solution(mesh):
    in_specs = (
        P(("ctx", "head"), None),
        P(("ctx", "head"), None),
        P(("ctx", "head"), None),
        P(("ctx", "head"), None),
        P("ctx"),
        P("ctx"),
        P("head"),
        P("head"),
        P("head"),
        P("ctx", "head"),
    )
    out_specs = (P("ctx", "head"), P("ctx", "head"))
    return jax.shard_map(body, mesh=mesh, in_specs=in_specs, out_specs=out_specs, check_vma=False)
```

profile of v0, /device:TPU:98, one launch (start us, length us, event | category | flops | bytes accessed | tf_op | source)
XLA Modules:
  0.0 715.5 jit_solution(9166548813326513781)
XLA Ops:
  16.9 7.5 %all-to-all-start = ((s32[16,1,2]{2,1,0:T(1,128)}), s32[16,1,2]{2,1,0:T(1,128)S(1)}, u32[]{:S(2)}, u32[]{:S(2)}) async-start(s32[16,1,2]{2,1,0:T(1,128)} %bitcast.31), calls=%async_computation | async-start | bytes 16384 | tf_op jit(solution)/shard_map/all_to_all | solution.py:126
  48.3 7.3 %all-to-all-done.3 = bf16[256,8,128]{0,2,1:T(8,128)(2,1)S(1)} async-done(((bf16[256,8,128]{0,2,1:T(8,128)(2,1)}), bf16[256,8,128]{0,2,1:T(8,128)(2,1)S(1)}, u32[]{:S(2)}, u32[]{:S(2)}) %all-to-all-start.3) | async-done | bytes 524320 | tf_op jit(solution)/shard_map/all_to_all | solution.py:98
  80.7 8.7 %all-to-all-done.4 = bf16[16,2,128,128]{3,2,1,0:T(8,128)(2,1)S(1)} async-done(((bf16[16,2,128,128]{3,2,1,0:T(8,128)(2,1)}), bf16[16,2,128,128]{3,2,1,0:T(8,128)(2,1)S(1)}, u32[]{:S(2)}, u32[]{:S(2)}) %all-to-all-start.4) | async-done | bytes 1048608 | tf_op jit(solution)/shard_map/all_to_all | solution.py:124
  89.4 6.5 all-to-all-start.1
  100.0 43.6 %all-to-all-done.1 = bf16[256,8,1024]{0,2,1:T(8,128)(2,1)} async-done(((bf16[256,8,1024]{0,2,1:T(8,128)(2,1)}), bf16[256,8,1024]{0,2,1:T(8,128)(2,1)}, u32[]{:S(2)}, u32[]{:S(2)}) %all-to-all-start.1) | async-done | bytes 4194336 | tf_op jit(solution)/shard_map/all_to_all | solution.py:96
  149.9 6.4 copy.103
  160.6 11.0 %scatter_fusion = bf16[32,128,1024]{2,1,0:T(8,128)(2,1)} fusion(bf16[32,128,1024]{2,1,0:T(8,128)(2,1)} %broadcast_in_dim.110, s32[16]{0:T(128)S(1)} %compare_select_fusion.3, bf16[16,128,1024]{2,1,0:T(8,128)(2,1)} %bitcast.307), kind=kCustom, calls=%fused_computation.1 | custom fusion | bytes 12582976 | tf_op jit(solution)/shard_map/scatter | solution.py:116
  172.6 7.2 %all-to-all-start.2 = ((bf16[16,2,128,1024]{3,2,1,0:T(8,128)(2,1)}), bf16[16,2,128,1024]{3,2,1,0:T(8,128)(2,1)}, u32[]{:S(2)}, u32[]{:S(2)}) async-start(bf16[16,2,128,1024]{3,2,1,0:T(8,128)(2,1)} %bitcast.299), calls=%async_computation.2 | async-start | bytes 16777216 | tf_op jit(solution)/shard_map/all_to_all | solution.py:122
  189.5 94.4 %all-to-all-done.2 = bf16[16,2,128,1024]{3,2,1,0:T(8,128)(2,1)} async-done(((bf16[16,2,128,1024]{3,2,1,0:T(8,128)(2,1)}), bf16[16,2,128,1024]{3,2,1,0:T(8,128)(2,1)}, u32[]{:S(2)}, u32[]{:S(2)}) %all-to-all-start.2) | async-done | bytes 8388640 | tf_op jit(solution)/shard_map/all_to_all | solution.py:122
  286.4 20.1 %scatter_fusion.1 = bf16[16,128,1024]{2,1,0:T(8,128)(2,1)} fusion(bf16[16,128,1024]{2,1,0:T(8,128)(2,1)} %broadcast_in_dim.106, s32[32]{0:T(128)S(1)} %fusion.71, bf16[32,128,1024]{2,1,0:T(8,128)(2,1)} %bitcast.37), kind=kCustom, calls=%fused_computation.2 | custom fusion | bytes 25165952 | tf_op jit(solution)/shard_map/scatter | solution.py:137
  312.2 135.1 %while.90 = (s32[]{:T(128)}, f32[8,256,1,16,64]{1,4,3,2,0:T(8,128)}, f32[8,256,1,16,64]{1,4,3,2,0:T(8,128)}, f32[8,16,64,128]{3,2,1,0:T(8,128)}, f32[8,16,64,128...) while((s32[]{:T(128)}, ...), condition=%wide.region_15.16_spmd, body=%wide.region_10.15_spmd.sunk | while | flops 433050688 | bytes 14290279 | solution.py:162
  449.9 22.1 %while.93 = (s32[]{:T(128)}, f32[16]{0:T(128)S(1)}, f32[16,64,128]{2,1,0:T(8,128)S(1)}, f32[8,16]{1,0:T(8,128)S(1)}, f32[8,16,64,128]{3,2,1,0:T(8,128)}, /*index...) while((s32[]{:T(128)}, f32[16]{0:T(128)S(1)}, ...), condition=%wide.region_21.22_spmd.clone, body=%wide.region_20.21_spmd.clone.sunk | while | flops 524324 | bytes 2622093 | solution.py:170
  475.4 22.0 %while.91 = (s32[]{:T(128)}, f32[16]{0:T(128)S(1)}, f32[16,64,128]{2,1,0:T(8,128)S(1)}, f32[8,16]{1,0:T(8,128)S(1)}, f32[8,16,64,128]{3,2,1,0:T(8,128)}, /*index...) while((s32[]{:T(128)}, f32[16]{0:T(128)S(1)}, ...), condition=%wide.region_17.18_spmd.clone, body=%wide.region_16.17_spmd.clone.sunk | while | flops 524323 | bytes 2622581 | solution.py:167
  499.6 68.5 %all-reduce = f32[256]{0:T(256)S(1)} all-reduce(f32[256]{0:T(256)S(1)} %dynamic-update-slice), channel_id=2, replica_groups=mesh['ctx'=16,'head'=8] {'ctx'}, use_global_device_ids=true, to_apply=%add | all-reduce | flops 256 | bytes 2048
  568.2 17.7 %all-gather.8.cloned.1.call-done = f32[256,64,128]{2,1,0:T(8,128)} async-done(((f32[16,64,128]{2,1,0:T(8,128)}), f32[256,64,128]{2,1,0:T(8,128)}) %all-gather.8.cloned.1.call-update) | async-done | bytes 8388624 | tf_op jit(solution)/shard_map/all_gather | solution.py:14
  585.9 19.7 %while.94 = (s32[]{:T(128)}, f32[16,64,128]{2,1,0:T(8,128)S(1)}, s32[]{:T(128)}, f32[16,16]{1,0:T(8,128)S(1)}, f32[16,16,64,128]{3,2,1,0:T(8,128)}, /*index=5*/s32[]{:T(128)}, s32[]{:T(128)}, s32[]{:T(128)}, s32[]{:T(128)}) while((s32[]{:T(128)}, f32[16,64,128]{2,1,0:T(8,128)S(1)}, s32[]{:T(128)}, f32[16,16]{1,0:T(8,128)S(1)}, ...), condition=%wide.region_23.24_spmd.clone, body=%wide.region_22.23_spmd.clone.sunk | while | flops 524296 | bytes 1573223 | solution.py:27
  605.6 8.1 %fusion.63 = bf16[8,256,1,16,64]{1,4,3,0,2:T(8,128)(2,1)} fusion(f32[8,256,1,16,64]{1,4,3,2,0:T(8,128)} %get-tuple-element.508, f32[8,256,16]{1,2,0:T(8,128)} %get-tuple-element.514, bf16[8,256,128,1]{2,1,3,0:T(8,128)(2,1)S(1)} %bitcast.311, f32[8,16,64,128]{3,2,1,0:T(8,128)} %get-tuple-element.510, f32[16,64,128]{2,1,0:T(8,128)S(1)} %get-tuple-element.513, ...), kind=kOutput, calls=%fused_computation.103 | convolution fusion | flops 546308096 | bytes 17957376 | tf_op jit(solution)/shard_map/ctgs,cgjps->ctgjp/dot_general | solution.py:191
  613.7 11.0 %copy.130 = bf16[8,256,1,16,64]{4,3,1,0,2:T(8,128)(2,1)} copy(bf16[8,256,1,16,64]{1,4,3,0,2:T(8,128)(2,1)} %fusion.63) | data formatting | bytes 8388608
  624.6 11.9 %reshape.515 = bf16[2048,1024]{1,0:T(8,128)(2,1)} reshape(bf16[8,256,1,16,64]{4,3,1,0,2:T(8,128)(2,1)} %copy.130) | data formatting | bytes 8388608
  636.6 22.0 %all-gather.6.cloned.1.call-done = f32[256,64,128]{2,1,0:T(8,128)} async-done(((f32[16,64,128]{2,1,0:T(8,128)}), f32[256,64,128]{2,1,0:T(8,128)}) %all-gather.6.cloned.1.call-update) | async-done | bytes 8388624 | tf_op jit(solution)/shard_map/all_gather | solution.py:14
  658.6 19.4 %while.92 = (s32[]{:T(128)}, f32[16,64,128]{2,1,0:T(8,128)S(1)}, s32[]{:T(128)}, f32[16,16]{1,0:T(8,128)S(1)}, f32[16,16,64,128]{3,2,1,0:T(8,128)}, /*index=5*/s32[]{:T(128)}, s32[]{:T(128)}) while((s32[]{:T(128)}, f32[16,64,128]{2,1,0:T(8,128)S(1)}, s32[]{:T(128)}, f32[16,16]{1,0:T(8,128)S(1)}, f32[16,16,64,128]{3,2,1,0:T(8,128)}, ...), condition=%wide.region_19.20_spmd.clone, body=%wide.region_18.19_spmd.clone.sunk | while | flops 524292 | bytes 1573161 | solution.py:27
  678.0 7.9 %fusion.65 = bf16[8,256,1,16,64]{1,4,3,0,2:T(8,128)(2,1)} fusion(f32[8,256,1,16,64]{1,4,3,2,0:T(8,128)} %get-tuple-element.499, f32[8,256,16]{1,2,0:T(8,128)} %get-tuple-element.507, bf16[8,256,128,1]{2,1,3,0:T(8,128)(2,1)S(1)} %bitcast.309, f32[8,16,64,128]{3,2,1,0:T(8,128)} %get-tuple-element.502, f32[16,64,128]{2,1,0:T(8,128)S(1)} %get-tuple-element.506, ...), kind=kOutput, calls=%fused_computation.106 | convolution fusion | flops 546308096 | bytes 17957376 | tf_op jit(solution)/shard_map/ctgs,cgjps->ctgjp/dot_general | solution.py:189
  685.9 10.9 %copy.129 = bf16[8,256,1,16,64]{4,3,1,0,2:T(8,128)(2,1)} copy(bf16[8,256,1,16,64]{1,4,3,0,2:T(8,128)(2,1)} %fusion.65) | data formatting | bytes 8388608
  696.8 11.9 %reshape.514 = bf16[2048,1024]{1,0:T(8,128)(2,1)} reshape(bf16[8,256,1,16,64]{4,3,1,0,2:T(8,128)(2,1)} %copy.129) | data formatting | bytes 8388608
  (459 shorter events, 310.9 us)
Async XLA Ops:
  7.2 40.1 %copy-start.3 = (bf16[256,1024]{1,0:T(8,128)(2,1)S(1)}, bf16[256,1024]{1,0:T(8,128)(2,1)}, u32[]{:S(2)}) copy-start(bf16[256,1024]{1,0:T(8,128)(2,1)} %param.21) | copy-start | bytes 1572868
  8.8 8.1 %all-to-all-start.7 = ((bf16[256,8,16]{0,2,1:T(8,128)(2,1)}), bf16[256,8,16]{0,2,1:T(8,128)(2,1)S(1)}, u32[]{:S(2)}, u32[]{:S(2)}) async-start(bf16[256,8,16]{0,2,1:T(8,128)(2,1)} %bitcast.51), calls=%async_computation.7 | async-start | bytes 131072 | tf_op jit(solution)/shard_map/all_to_all | solution.py:99
  16.9 13.5 %all-to-all-start = ((s32[16,1,2]{2,1,0:T(1,128)}), s32[16,1,2]{2,1,0:T(1,128)S(1)}, u32[]{:S(2)}, u32[]{:S(2)}) async-start(s32[16,1,2]{2,1,0:T(1,128)} %bitcast.31), calls=%async_computation | async-start | bytes 16384 | tf_op jit(solution)/shard_map/all_to_all | solution.py:126
  30.4 11.4 %all-to-all-start.8 = ((bf16[16,2,128,16]{2,3,1,0:T(8,128)(2,1)}), bf16[16,2,128,16]{2,3,1,0:T(8,128)(2,1)S(1)}, u32[]{:S(2)}, u32[]{:S(2)}) async-start(bf16[16,2,128,16]{2,3,1,0:T(8,128)(2,1)} %bitcast.53), calls=%async_computation.8 | async-start | bytes 262144 | tf_op jit(solution)/shard_map/all_to_all | solution.py:125
  41.8 13.8 %all-to-all-start.3 = ((bf16[256,8,128]{0,2,1:T(8,128)(2,1)}), bf16[256,8,128]{0,2,1:T(8,128)(2,1)S(1)}, u32[]{:S(2)}, u32[]{:S(2)}) async-start(bf16[256,8,128]{0,2,1:T(8,128)(2,1)} %bitcast.39), calls=%async_computation.3 | async-start | bytes 1048576 | tf_op jit(solution)/shard_map/all_to_all | solution.py:98
  55.5 13.8 %all-to-all-start.5 = ((bf16[256,8,128]{0,2,1:T(8,128)(2,1)}), bf16[256,8,128]{0,2,1:T(8,128)(2,1)S(1)}, u32[]{:S(2)}, u32[]{:S(2)}) async-start(bf16[256,8,128]{0,2,1:T(8,128)(2,1)} %bitcast.45), calls=%async_computation.5 | async-start | bytes 1048576 | tf_op jit(solution)/shard_map/all_to_all | solution.py:97
  69.3 20.1 %all-to-all-start.4 = ((bf16[16,2,128,128]{3,2,1,0:T(8,128)(2,1)}), bf16[16,2,128,128]{3,2,1,0:T(8,128)(2,1)S(1)}, u32[]{:S(2)}, u32[]{:S(2)}) async-start(bf16[16,2,128,128]{3,2,1,0:T(8,128)(2,1)} %bitcast.42), calls=%async_computation.4 | async-start | bytes 2097152 | tf_op jit(solution)/shard_map/all_to_all | solution.py:124
  89.4 54.2 %all-to-all-start.1 = ((bf16[256,8,1024]{0,2,1:T(8,128)(2,1)}), bf16[256,8,1024]{0,2,1:T(8,128)(2,1)}, u32[]{:S(2)}, u32[]{:S(2)}) async-start(bf16[256,8,1024]{0,2,1:T(8,128)(2,1)} %bitcast.306), calls=%async_computation.1 | async-start | bytes 8388608 | tf_op jit(solution)/shard_map/all_to_all | solution.py:96
  143.6 28.0 %all-to-all-start.6 = ((bf16[16,2,128,128]{3,2,1,0:T(8,128)(2,1)}), bf16[16,2,128,128]{3,2,1,0:T(8,128)(2,1)S(1)}, u32[]{:S(2)}, u32[]{:S(2)}) async-start(bf16[16,2,128,128]{3,2,1,0:T(8,128)(2,1)} %bitcast.48), calls=%async_computation.6 | async-start | bytes 2097152 | tf_op jit(solution)/shard_map/all_to_all | solution.py:123
  171.7 1.0 copy-start.2
  171.7 8.4 %copy-start.7 = (f32[16]{0:T(128)S(1)}, f32[16]{0:T(128)}, u32[]{:S(2)}) copy-start(f32[16]{0:T(128)} %param.26) | copy-start | bytes 196
  171.7 8.4 %copy-start.5 = (s32[2048]{0:T(1024)S(1)}, s32[2048]{0:T(1024)}, u32[]{:S(2)}) copy-start(s32[2048]{0:T(1024)} %param.25) | copy-start | bytes 24580
  171.7 11.4 %copy-start.6 = (f32[16]{0:T(128)S(1)}, f32[16]{0:T(128)}, u32[]{:S(2)}) copy-start(f32[16]{0:T(128)} %param.27) | copy-start | bytes 196
  172.6 111.3 %all-to-all-start.2 = ((bf16[16,2,128,1024]{3,2,1,0:T(8,128)(2,1)}), bf16[16,2,128,1024]{3,2,1,0:T(8,128)(2,1)}, u32[]{:S(2)}, u32[]{:S(2)}) async-start(bf16[16,2,128,1024]{3,2,1,0:T(8,128)(2,1)} %bitcast.299), calls=%async_computation.2 | async-start | bytes 16777216 | tf_op jit(solution)/shard_map/all_to_all | solution.py:122
  179.8 406.1 %all-gather.8.cloned.1.call-start = ((), (), s32[]{:S(2)}) async-start(), calls=%async_computation.10 | async-start | bytes 8912896 | tf_op jit(solution)/shard_map/all_gather | solution.py:14
  447.3 2.6 copy-start.4
  472.0 0.8 copy-start
  472.8 185.8 %all-gather.6.cloned.1.call-start = ((), (), s32[]{:S(2)}) async-start(), calls=%async_computation.9 | async-start | bytes 8912896 | tf_op jit(solution)/shard_map/all_gather | solution.py:14
  475.4 22.8 %copy-start.8 = (u32[128]{0:T(128)S(1)}, u32[128]{0:T(128)}, u32[]{:S(2)}) copy-start(u32[128]{0:T(128)} %constant.212) | copy-start | bytes 1540
  497.4 0.8 copy-start.1
Sparse Core Ops, SparseCore 0:
  472.9 112.9 all-gather.7
  588.1 70.4 all-gather.5
where the time goes:
time: 724 us; the launch traced here: 715 us
  waiting for transfers between devices  207 us (29%)
  local copies, waits for them, and re-layouts  176 us (24%)
  other arithmetic  107 us (15%)
  matrix products  81.7 us (11%)
  blocking collectives  68.5 us (9%)
  starting transfers between devices  53.2 us (7%)
  between operations  15 us (2%)
    all_to_all x1, waiting for transfers between devices, body(): lax.all_to_all(pack_slots(x_heads), 'ctx', split_axis=0, concat_axis=0, t...  94.4 us
    unnamed x1, blocking collectives  68.5 us
    unnamed x29, local copies, waits for them, and re-layouts  60.1 us
    all_to_all x1, waiting for transfers between devices, body(): lax.all_to_all(x_rows, 'head', split_axis=1, concat_axis=0, tiled=True)  43.6 us
    all_gather x2, waiting for transfers between devices, entering(): everything = jax.tree.map(lambda part: lax.all_gather(part, axis), shard)  39.7 us
    select_n x32, other arithmetic, hop(): return jax.tree.map(lambda a, b: jnp.where(reached, a, b), new, before)  37.6 us
    scatter x4, local copies, waits for them, and re-layouts, unpack(): placed = jnp.zeros((owners, piece_rows, col_count), received.dtype).at[ta...  27 us
    dot_general x8, matrix products, block_local(): jnp.einsum('gjtu,ugjp->tgjp', forward_weights, x_four, preferred_element_...  23.8 us
  transfers between devices with their start and end apart: 11, of which 10 were waited for; matrix products, arithmetic and copies ran while one was open for 18% of the time, Pallas kernels for 0%

commit v1 on v0

v1 whole, which is shorter than its diff:
```python
from functools import partial

import jax
import jax.numpy as jnp
from jax import lax
from jax.experimental import pallas as pl
from jax.experimental.pallas import tpu as pltpu
from jax.sharding import PartitionSpec as P

OWNERS = 16
PEERS = 8
PIECE = 128
STATE = 128
HEADS = 16
HEAD_DIM = 64
WIDTH = HEADS * HEAD_DIM
HALF = WIDTH // 2
SMALL_ROWS = 2 * PIECE + HEADS
TAG_ROWS = 16
SENT_ROWS = SMALL_ROWS + TAG_ROWS
EXTRA = 128
LOG2E = 1.4426950408889634
F32 = jnp.float32
BF16 = jnp.bfloat16
ANY = pl.BlockSpec(memory_space=pltpu.HBM)
SMEM = pl.BlockSpec(memory_space=pltpu.SMEM)
SHIFTS = [(1, 0), (3, 0), (1, 1), (3, 1), (2, 0), (2, 1), (0, 1)]


def params(mib=48):
    return pltpu.CompilerParams(vmem_limit_bytes=mib * 1024 * 1024)


def partner(head, shift):
    return (head // 2 + shift[0]) % 4 * 2 + (head % 2 + shift[1]) % 2


def source(head, shift):
    return (head // 2 + 4 - shift[0]) % 4 * 2 + (head % 2 + shift[1]) % 2


def run_copies(copies):
    for copy in copies:
        copy.start()
    for copy in copies:
        copy.wait()


def gather_small_kernel(b_ref, c_ref, dt_ref, out_ref, turned, sems):
    copies = []
    for r in range(2):
        rows = pl.ds(r * PIECE, PIECE)
        for g in range(PEERS):
            cols = pl.ds(g * STATE, STATE)
            for kind, ref in enumerate((b_ref, c_ref)):
                copies.append(
                    pltpu.make_async_copy(
                        ref.at[rows, cols],
                        out_ref.at[g, r, pl.ds(kind * PIECE, PIECE), :],
                        sems.at[len(copies)],
                    )
                )
    for copy in copies:
        copy.start()
    last = []
    for r in range(2):
        dt_t = dt_ref[r * PIECE : (r + 1) * PIECE, :].astype(F32).T.astype(BF16)
        for g in range(PEERS):
            turned[g, r] = dt_t[g * HEADS : (g + 1) * HEADS, :]
    last = pltpu.make_async_copy(
        turned, out_ref.at[:, :, pl.ds(2 * PIECE, HEADS), :], sems.at[len(copies)]
    )
    last.start()
    for copy in copies + [last]:
        copy.wait()


def gather_small(b_rows, c_rows, dt_rows):
    return pl.pallas_call(
        gather_small_kernel,
        in_specs=[ANY, ANY, pl.BlockSpec(memory_space=pltpu.VMEM)],
        out_specs=ANY,
        out_shape=jax.ShapeDtypeStruct((PEERS, 2, SMALL_ROWS, STATE), BF16),
        scratch_shapes=[
            pltpu.VMEM((PEERS, 2, HEADS, PIECE), BF16),
            pltpu.SemaphoreType.DMA((4 * PEERS + 1,)),
        ],
        compiler_params=params(),
        name="gather_small",
    )(b_rows, c_rows, dt_rows)


def pack_small_kernel(slot_ref, place_ref, in_ref, out_ref, tags, sems):
    copies = [
        pltpu.make_async_copy(
            in_ref.at[j], out_ref.at[slot_ref[j], pl.ds(0, SMALL_ROWS), :], sems.at[j]
        )
        for j in range(OWNERS)
    ]
    for copy in copies:
        copy.start()
    tags[...] = jnp.full(tags.shape, -1.0, BF16)
    for j in range(OWNERS):
        place = place_ref[j].astype(F32)
        tags[slot_ref[j]] = jnp.full(tags.shape[1:], place, F32).astype(BF16)
    last = pltpu.make_async_copy(
        tags, out_ref.at[:, pl.ds(SMALL_ROWS, TAG_ROWS), :], sems.at[OWNERS]
    )
    last.start()
    for copy in copies + [last]:
        copy.wait()


def pack_small(slot, place, pieces):
    return pl.pallas_call(
        pack_small_kernel,
        in_specs=[SMEM, SMEM, ANY],
        out_specs=ANY,
        out_shape=jax.ShapeDtypeStruct((2 * OWNERS, SENT_ROWS, STATE), BF16),
        scratch_shapes=[
            pltpu.VMEM((2 * OWNERS, TAG_ROWS, STATE), BF16),
            pltpu.SemaphoreType.DMA((OWNERS + 1,)),
        ],
        compiler_params=params(),
        name="pack_small",
    )(slot, place, pieces)


def find_source_kernel(small_ref, out_ref, tags, sem):
    copy = pltpu.make_async_copy(
        small_ref.at[:, pl.ds(SMALL_ROWS, TAG_ROWS), :], tags, sem.at[0]
    )
    copy.start()
    copy.wait()
    slot = lax.broadcasted_iota(jnp.int32, tags.shape, 0).astype(F32)
    place = lax.broadcasted_iota(jnp.int32, tags.shape, 2).astype(F32)
    found = jnp.where(tags[...].astype(F32) == place, slot, 0.0)
    out_ref[...] = jnp.sum(found, axis=0)[0:1].astype(jnp.int32)


def find_source(small):
    return pl.pallas_call(
        find_source_kernel,
        in_specs=[ANY],
        out_specs=pl.BlockSpec(memory_space=pltpu.VMEM),
        out_shape=jax.ShapeDtypeStruct((1, STATE), jnp.int32),
        scratch_shapes=[
            pltpu.VMEM((2 * OWNERS, TAG_ROWS, STATE), BF16),
            pltpu.SemaphoreType.DMA((1,)),
        ],
        compiler_params=params(),
        name="find_source",
    )(small)


def cut_kernel(half, dest_ref, x_ref, *rest):
    outs, sems = rest[:-1], rest[-1]
    copies = []
    for i, out_ref in enumerate(outs):
        at = pl.multiple_of(dest_ref[i] * WIDTH + half * HALF, HALF)
        copies.append(pltpu.make_async_copy(x_ref.at[:, pl.ds(at, HALF)], out_ref, sems.at[i]))
    for copy in copies:
        copy.start()
    for copy in copies:
        copy.wait()


def cut(half, dest, x_rows):
    count = len(SHIFTS)
    return pl.pallas_call(
        partial(cut_kernel, half),
        in_specs=[SMEM, ANY],
        out_specs=[ANY] * count,
        out_shape=[jax.ShapeDtypeStruct((x_rows.shape[0], HALF), BF16)] * count,
        scratch_shapes=[pltpu.SemaphoreType.DMA((count,))],
        compiler_params=params(),
        name="cut",
    )(dest, x_rows)


def pack_x_kernel(half, slot_ref, from_ref, x_ref, *rest):
    arrived, out_ref, sems = rest[:-2], rest[-2], rest[-1]
    count = len(arrived)
    at = pl.multiple_of(from_ref[count] * WIDTH + half * HALF, HALF)
    copies = []
    for i in range(count + 1):
        for r in range(2):
            slot = slot_ref[from_ref[i] * 2 + r]
            rows = pl.ds(r * PIECE, PIECE)
            piece = arrived[i].at[rows, :] if i < count else x_ref.at[rows, pl.ds(at, HALF)]
            copies.append(pltpu.make_async_copy(piece, out_ref.at[slot], sems.at[2 * i + r]))
    for copy in copies:
        copy.start()
    for copy in copies:
        copy.wait()


def pack_x(half, slot, origin, x_rows, arrived):
    return pl.pallas_call(
        partial(pack_x_kernel, half),
        in_specs=[SMEM, SMEM] + [ANY] * (1 + len(arrived)),
        out_specs=ANY,
        out_shape=jax.ShapeDtypeStruct((2 * OWNERS, PIECE, HALF), BF16),
        scratch_shapes=[pltpu.SemaphoreType.DMA((2 * PEERS,))],
        compiler_params=params(),
        name="pack_x",
    )(slot, origin, x_rows, *arrived)


def split_two(value):
    high = value.astype(BF16)
    return high, (value - high.astype(F32)).astype(BF16)


def softplus(value):
    small = jnp.exp(-jnp.abs(value))
    series = small * (1.0 - small * (0.5 - small * (1.0 / 3.0 - small * 0.25)))
    return jnp.maximum(value, 0.0) + jnp.where(small < 1e-2, series, jnp.log(1.0 + small))


def decay_kernel(
    src_ref, small_ref, seg_ref, bias_ref, alog_ref, rows_ref, scale_ref, ends_ref, total_ref, dt_ref, sems
):
    pieces = seg_ref.shape[0]
    copies = [
        pltpu.make_async_copy(
            small_ref.at[src_ref[0, k], pl.ds(2 * PIECE, HEADS), :], dt_ref.at[k], sems.at[k]
        )
        for k in range(pieces)
    ]
    for copy in copies:
        copy.start()
    for copy in copies:
        copy.wait()
    step_all = softplus(dt_ref[...].astype(F32) + bias_ref[...][None])
    rate_all = -step_all * (jnp.exp(alog_ref[...]) * LOG2E)[None]
    up_to = (
        lax.broadcasted_iota(jnp.int32, (PIECE, PIECE), 0)
        <= lax.broadcasted_iota(jnp.int32, (PIECE, PIECE), 1)
    ).astype(F32)
    log_all = jnp.dot(
        rate_all.reshape(pieces * HEADS, PIECE),
        up_to,
        precision=lax.Precision.HIGHEST,
        preferred_element_type=F32,
    ).reshape(pieces, HEADS, PIECE)
    ends = [log_all[k, :, PIECE - 1 :] for k in range(pieces)]
    starts = [seg_ref[k, :, PIECE - 1 :] for k in range(pieces)]
    log_before = jnp.zeros((HEADS, 1), F32)
    starts_before = jnp.zeros((1, 1), F32)
    rows_ref[...] = jnp.zeros(rows_ref.shape, F32)
    for k in range(pieces):
        log, step, seg = log_all[k], step_all[k], seg_ref[k]
        rows_ref[k, 0:HEADS, :] = log
        rows_ref[k, HEADS : 2 * HEADS, :] = log - jnp.log(step) * LOG2E
        rows_ref[k, 2 * HEADS : 2 * HEADS + 1, :] = seg
        none_yet = (seg == 0.0).astype(F32)
        none_left = (seg == starts[k]).astype(F32)
        entry = jnp.exp2(log) * none_yet
        step_exit = step * (jnp.exp2(ends[k] - log) * none_left)
        decay = jnp.exp2(ends[k]) * (starts[k] == 0.0).astype(F32)
        before = jnp.exp2(log_before + log) * (none_yet * (starts_before == 0.0).astype(F32))
        for at, value in enumerate(
            (entry, step_exit, step, jnp.broadcast_to(decay, entry.shape))
        ):
            high, low = split_two(value)
            scale_ref[k, 2 * at * HEADS : (2 * at + 1) * HEADS, :] = high
            scale_ref[k, (2 * at + 1) * HEADS : (2 * at + 2) * HEADS, :] = low
        high, low = split_two(before)
        ends_ref[k, 0:HEADS, :] = high
        ends_ref[k, HEADS : 2 * HEADS, :] = low
        log_before = log_before + ends[k]
        starts_before = starts_before + starts[k]
    total_ref[...] = jnp.broadcast_to(
        jnp.exp2(log_before) * (starts_before == 0.0).astype(F32), total_ref.shape
    )
    log_after = jnp.zeros((HEADS, 1), F32)
    starts_after = jnp.zeros((1, 1), F32)
    for k in reversed(range(pieces)):
        log, step, seg = log_all[k], step_all[k], seg_ref[k]
        none_left = (seg == starts[k]).astype(F32) * (starts_after == 0.0).astype(F32)
        after = step * (jnp.exp2(log_after + (ends[k] - log)) * none_left)
        high, low = split_two(after)
        ends_ref[k, 2 * HEADS : 3 * HEADS, :] = high
        ends_ref[k, 3 * HEADS : 4 * HEADS, :] = low
        log_after = log_after + ends[k]
        starts_after = starts_after + starts[k]


ROW_COUNT = 40


def decays(src, small, seg, bias, alog):
    pieces = seg.shape[0]
    whole = pl.BlockSpec(memory_space=pltpu.VMEM)
    return pl.pallas_call(
        decay_kernel,
        in_specs=[SMEM, ANY, whole, whole, whole],
        out_specs=[whole] * 4,
        out_shape=[
            jax.ShapeDtypeStruct((pieces, ROW_COUNT, PIECE), F32),
            jax.ShapeDtypeStruct((pieces, 8 * HEADS, PIECE), BF16),
            jax.ShapeDtypeStruct((pieces, 4 * HEADS, PIECE), BF16),
            jax.ShapeDtypeStruct((HEADS, PIECE), F32),
        ],
        scratch_shapes=[
            pltpu.VMEM((pieces, HEADS, PIECE), BF16),
            pltpu.SemaphoreType.DMA((pieces,)),
        ],
        compiler_params=params(),
        name="decays",
    )(src, small, seg, bias, alog)


def spread(kinds):
    rows = lax.broadcasted_iota(jnp.int32, (kinds, kinds * 2 * HEADS, WIDTH), 1)
    kind = lax.broadcasted_iota(jnp.int32, (kinds, kinds * 2 * HEADS, WIDTH), 0)
    head = lax.broadcasted_iota(jnp.int32, (kinds, kinds * 2 * HEADS, WIDTH), 2) // HEAD_DIM
    return ((rows // (2 * HEADS) == kind) & (rows % HEADS == head)).astype(BF16)


def over_first(left, right):
    return lax.dot_general(left, right, (((0,), (0,)), ((), ())), preferred_element_type=F32)


def over_last(left, right):
    return lax.dot_general(left, right, (((1,), (1,)), ((), ())), preferred_element_type=F32)


def two_heads(weights, values):
    lane = lax.broadcasted_iota(jnp.int32, values.shape, 1)
    zero = jnp.zeros_like(values)
    stacked = jnp.concatenate(
        [jnp.where(lane < HEAD_DIM, values, zero), jnp.where(lane < HEAD_DIM, zero, values)], axis=0
    )
    return jnp.dot(jnp.concatenate(weights, axis=1), stacked, preferred_element_type=F32)


ENTRY, STEP_EXIT, STEP, DECAY = range(4)


def forward_kernel(
    first, src_ref, small_ref, x_ref, rows_ref, scale_ref, spread_ref, skip_ref, y_ref, out_ref, state
):
    step = pl.program_id(0)

    @pl.when(step == 0)
    def _():
        state[...] = jnp.zeros_like(state)

    b, c = small_ref[0, 0:PIECE, :], small_ref[0, PIECE : 2 * PIECE, :]
    scales = scale_ref[0]
    by_token = rows_ref[0].T
    row = lax.broadcasted_iota(jnp.int32, (PIECE, PIECE), 0)
    col = lax.broadcasted_iota(jnp.int32, (PIECE, PIECE), 1)
    same = by_token[:, 2 * HEADS : 2 * HEADS + 1] == rows_ref[0, 2 * HEADS : 2 * HEADS + 1, :]
    scores = jnp.where((col <= row) & same, over_last(c, b), 0.0)
    for pair in range(x_ref.shape[2] // (2 * HEAD_DIM)):
        cols = slice(pair * 2 * HEAD_DIM, (pair + 1) * 2 * HEAD_DIM)
        weights = []
        for head in (first + 2 * pair, first + 2 * pair + 1):
            gap = by_token[:, head : head + 1] - rows_ref[0, HEADS + head : HEADS + head + 1, :]
            weights.append((scores * jnp.exp2(jnp.minimum(gap, 8.0))).astype(BF16))
        x = x_ref[0, :, cols]
        x_wide = x.astype(F32)
        held = state[:, cols]
        y = two_heads(weights, x) + skip_ref[:, cols] * x_wide
        y += over_first(scales, spread_ref[ENTRY, :, cols]) * jnp.dot(
            c, held.astype(BF16), preferred_element_type=F32
        )
        y_ref[0, :, cols] = y
        x_scaled = (x_wide * over_first(scales, spread_ref[STEP_EXIT, :, cols])).astype(BF16)
        state[:, cols] = over_first(scales, spread_ref[DECAY, :, cols]) * held + over_first(b, x_scaled)

    @pl.when(step == pl.num_programs(0) - 1)
    def _():
        out_ref[...] = state[...].astype(BF16)


def forward_local(half, src, small, x_slots, rows, scales, spread_four, skip):
    pieces = rows.shape[0]
    return pl.pallas_call(
        partial(forward_kernel, half * HEADS // 2),
        grid_spec=pltpu.PrefetchScalarGridSpec(
            num_scalar_prefetch=1,
            grid=(pieces,),
            in_specs=[
                pl.BlockSpec((1, 2 * PIECE, STATE), lambda k, src: (src[0, k], 0, 0)),
                pl.BlockSpec((1, PIECE, HALF), lambda k, src: (src[0, k], 0, 0)),
                pl.BlockSpec((1, ROW_COUNT, PIECE), lambda k, src: (k, 0, 0)),
                pl.BlockSpec((1, 8 * HEADS, PIECE), lambda k, src: (k, 0, 0)),
                pl.BlockSpec((4, 8 * HEADS, HALF), lambda k, src: (0, 0, half)),
                pl.BlockSpec((1, HALF), lambda k, src: (0, half)),
            ],
            out_specs=[
                pl.BlockSpec((1, PIECE, HALF), lambda k, src: (k, 0, 0)),
                pl.BlockSpec((STATE, HALF), lambda k, src: (0, 0)),
            ],
            scratch_shapes=[pltpu.VMEM((STATE, HALF), F32)],
        ),
        out_shape=[
            jax.ShapeDtypeStruct((pieces, PIECE, HALF), F32),
            jax.ShapeDtypeStruct((STATE, HALF), BF16),
        ],
        compiler_params=params(),
        name="forward_local",
    )(src, small, x_slots, rows, scales, spread_four, skip)


def forward_state_kernel(half, src_ref, small_ref, x_ref, ends_ref, spread_ref, out_ref, b_all, x_all, state, sems):
    pieces = ends_ref.shape[0]
    copies = []
    for k in range(pieces):
        at = src_ref[0, k]
        copies.append(
            (
                pltpu.make_async_copy(small_ref.at[at, pl.ds(0, PIECE), :], b_all.at[k], sems.at[2 * k]),
                pltpu.make_async_copy(x_ref.at[at], x_all.at[k], sems.at[2 * k + 1]),
            )
        )
    for pair in copies:
        for copy in pair:
            copy.start()
    for k, pair in enumerate(copies):
        for copy in pair:
            copy.wait()
        after = over_first(ends_ref[k], spread_ref[1, :, half * HALF : (half + 1) * HALF])
        x_scaled = (x_all[k].astype(F32) * after).astype(BF16)
        update = over_first(b_all[k], x_scaled)
        state[...] = update if k == 0 else state[...] + update
    out_ref[...] = state[...].astype(BF16)


def forward_state(half, src, small, x_slots, ends, spread_two):
    whole = pl.BlockSpec(memory_space=pltpu.VMEM)
    pieces = ends.shape[0]
    return pl.pallas_call(
        partial(forward_state_kernel, half),
        in_specs=[SMEM, ANY, ANY, whole, whole],
        out_specs=whole,
        out_shape=jax.ShapeDtypeStruct((STATE, HALF), BF16),
        scratch_shapes=[
            pltpu.VMEM((pieces, PIECE, STATE), BF16),
            pltpu.VMEM((pieces, PIECE, HALF), BF16),
            pltpu.VMEM((STATE, HALF), F32),
            pltpu.SemaphoreType.DMA((2 * pieces,)),
        ],
        compiler_params=params(),
        name="forward_state",
    )(src, small, x_slots, ends, spread_two)


def backward_kernel(
    src_ref, small_ref, cot_ref, rows_ref, scale_ref, spread_ref, skip_ref, g_ref, out_ref, state
):
    step = pl.program_id(0)

    @pl.when(step == 0)
    def _():
        state[...] = jnp.zeros_like(state)

    b, c = small_ref[0, 0:PIECE, :], small_ref[0, PIECE : 2 * PIECE, :]
    scales = scale_ref[0]
    by_token = rows_ref[0].T
    row = lax.broadcasted_iota(jnp.int32, (PIECE, PIECE), 0)
    col = lax.broadcasted_iota(jnp.int32, (PIECE, PIECE), 1)
    same = by_token[:, 2 * HEADS : 2 * HEADS + 1] == rows_ref[0, 2 * HEADS : 2 * HEADS + 1, :]
    scores = jnp.where((col >= row) & same, over_last(b, c), 0.0)
    for pair in range(HEADS // 2):
        cols = slice(pair * 2 * HEAD_DIM, (pair + 1) * 2 * HEAD_DIM)
        weights = []
        for head in (2 * pair, 2 * pair + 1):
            gap = rows_ref[0, head : head + 1, :] - by_token[:, head : head + 1]
            weights.append((scores * jnp.exp2(jnp.minimum(gap, 1.0))).astype(BF16))
        cot = cot_ref[:, cols]
        cot_wide = cot.astype(F32)
        held = state[:, cols]
        g = over_first(scales, spread_ref[STEP, :, cols]) * two_heads(weights, cot)
        g += skip_ref[:, cols] * cot_wide
        g += over_first(scales, spread_ref[STEP_EXIT, :, cols]) * jnp.dot(
            b, held.astype(BF16), preferred_element_type=F32
        )
        g_ref[0, :, cols] = g
        cot_scaled = (cot_wide * over_first(scales, spread_ref[ENTRY, :, cols])).astype(BF16)
        state[:, cols] = over_first(scales, spread_ref[DECAY, :, cols]) * held + over_first(c, cot_scaled)

    @pl.when(step == pl.num_programs(0) - 1)
    def _():
        out_ref[...] = state[...].astype(BF16)


def backward_local(src, small, cotangent, rows, scales, spread_four, skip):
    pieces = rows.shape[0]
    last = pieces - 1
    return pl.pallas_call(
        backward_kernel,
        grid_spec=pltpu.PrefetchScalarGridSpec(
            num_scalar_prefetch=1,
            grid=(pieces,),
            in_specs=[
                pl.BlockSpec((1, 2 * PIECE, STATE), lambda k, src: (src[0, last - k], 0, 0)),
                pl.BlockSpec((PIECE, WIDTH), lambda k, src: (last - k, 0)),
                pl.BlockSpec((1, ROW_COUNT, PIECE), lambda k, src: (last - k, 0, 0)),
                pl.BlockSpec((1, 8 * HEADS, PIECE), lambda k, src: (last - k, 0, 0)),
                pl.BlockSpec((4, 8 * HEADS, WIDTH), lambda k, src: (0, 0, 0)),
                pl.BlockSpec((1, WIDTH), lambda k, src: (0, 0)),
            ],
            out_specs=[
                pl.BlockSpec((1, PIECE, WIDTH), lambda k, src: (last - k, 0, 0)),
                pl.BlockSpec((STATE, WIDTH), lambda k, src: (0, 0)),
            ],
            scratch_shapes=[pltpu.VMEM((STATE, WIDTH), F32)],
        ),
        out_shape=[
            jax.ShapeDtypeStruct((pieces, PIECE, WIDTH), F32),
            jax.ShapeDtypeStruct((STATE, WIDTH), BF16),
        ],
        compiler_params=params(),
        name="backward_local",
    )(src, small, cotangent, rows, scales, spread_four, skip)


def join_kernel(a_ref, b_ref, g_ref, total_ref, out_ref):
    high, low = split_two(total_ref[...])
    lane = lax.broadcasted_iota(jnp.int32, high.shape, 1)
    decay = jnp.where(lane == 0, high, jnp.where(lane == 1, low, jnp.zeros_like(low)))
    for part in range(OWNERS):
        rows = slice(part % 8 * 16, part % 8 * 16 + 16)
        if part < 8:
            out_ref[part, :, 0:HALF] = a_ref[rows, :]
            out_ref[part, :, HALF:WIDTH] = b_ref[rows, :]
        else:
            out_ref[part, :, 0:WIDTH] = g_ref[rows, :]
        out_ref[part, :, WIDTH:] = decay


def join_states(state_a, state_b, g_state, total):
    return pl.pallas_call(
        join_kernel,
        out_shape=jax.ShapeDtypeStruct((OWNERS, 16, WIDTH + EXTRA), BF16),
        compiler_params=params(),
        name="join_states",
    )(state_a, state_b, g_state, total)


def scan_kernel(back_ref, part_ref, out_ref):
    back = back_ref[0]
    head = lax.broadcasted_iota(jnp.int32, (HEADS, WIDTH), 0)
    lane = lax.broadcasted_iota(jnp.int32, (HEADS, WIDTH), 1)
    spread_one = (lane // HEAD_DIM == head).astype(BF16)

    def hop(k, held):
        at = jnp.where(back == 1, OWNERS - 1 - k, k)
        out_ref[at] = held.astype(BF16)
        decay = over_first(part_ref[at, :, WIDTH:], spread_one)
        return (decay[0:1] + decay[1:2]) * held + part_ref[at, :, 0:WIDTH].astype(F32)

    lax.fori_loop(0, OWNERS, hop, jnp.zeros((HEADS, WIDTH), F32), unroll=4)


def scan_owners(back, parts):
    whole = pl.BlockSpec(memory_space=pltpu.VMEM)
    return pl.pallas_call(
        scan_kernel,
        in_specs=[SMEM, whole],
        out_specs=whole,
        out_shape=jax.ShapeDtypeStruct((OWNERS, 16, WIDTH), BF16),
        compiler_params=params(),
        name="scan_owners",
    )(back, parts)


def finish_kernel(
    src_ref, small_ref, ya_ref, yb_ref, g_ref, enter_ref, ends_ref, spread_ref, y_out, g_out
):
    b, c = small_ref[0, 0:PIECE, :], small_ref[0, PIECE : 2 * PIECE, :]
    ends = ends_ref[0]
    for half, y_ref in enumerate((ya_ref, yb_ref)):
        cols = slice(half * HALF, (half + 1) * HALF)
        y_off = jnp.dot(c, enter_ref[0:STATE, cols], preferred_element_type=F32)
        y = y_ref[0] + over_first(ends, spread_ref[0, :, cols]) * y_off
        y_out[:, cols] = y.astype(BF16)
        g_off = jnp.dot(b, enter_ref[STATE:, cols], preferred_element_type=F32)
        g = g_ref[0, :, cols] + over_first(ends, spread_ref[1, :, cols]) * g_off
        g_out[:, cols] = g.astype(BF16)


def finish(src, small, y_a, y_b, g_local, enter, ends, spread_two):
    pieces = ends.shape[0]
    out = jax.ShapeDtypeStruct((pieces * PIECE, WIDTH), BF16)
    return pl.pallas_call(
        finish_kernel,
        grid_spec=pltpu.PrefetchScalarGridSpec(
            num_scalar_prefetch=1,
            grid=(pieces,),
            in_specs=[
                pl.BlockSpec((1, 2 * PIECE, STATE), lambda k, src: (src[0, k], 0, 0)),
                pl.BlockSpec((1, PIECE, HALF), lambda k, src: (k, 0, 0)),
                pl.BlockSpec((1, PIECE, HALF), lambda k, src: (k, 0, 0)),
                pl.BlockSpec((1, PIECE, WIDTH), lambda k, src: (k, 0, 0)),
                pl.BlockSpec((2 * STATE, WIDTH), lambda k, src: (0, 0)),
                pl.BlockSpec((1, 4 * HEADS, PIECE), lambda k, src: (k, 0, 0)),
                pl.BlockSpec((2, 4 * HEADS, WIDTH), lambda k, src: (0, 0, 0)),
            ],
            out_specs=[pl.BlockSpec((PIECE, WIDTH), lambda k, src: (k, 0))] * 2,
        ),
        out_shape=[out, out],
        compiler_params=params(),
        name="finish",
    )(src, small, y_a, y_b, g_local, enter, ends, spread_two)


def ranks(dest):
    owner = dest // OWNERS
    here = lax.broadcasted_iota(jnp.int32, (OWNERS, OWNERS), 0)
    other = lax.broadcasted_iota(jnp.int32, (OWNERS, OWNERS), 1)
    same = (owner[..., None, :] == owner[..., :, None]) & (other < here)
    return jnp.sum(same.astype(jnp.int32), axis=-1)


def to_owners(value):
    return lax.all_to_all(value, "ctx", split_axis=0, concat_axis=0, tiled=True)


def body(
    x_rows, b_rows, c_rows, dt_rows, destination, doc_start, a_log, dt_bias, d_skip, cotangent
):
    head = lax.axis_index("head")
    me = lax.axis_index("ctx")
    dest_heads = jnp.stack([partner(head, s) for s in SHIFTS]).astype(jnp.int32)
    origin = jnp.stack([source(head, s) for s in SHIFTS] + [head]).astype(jnp.int32)
    send_slot = destination // OWNERS * 2 + ranks(destination)

    small = gather_small(b_rows, c_rows, dt_rows)
    small = lax.all_to_all(small, "head", split_axis=0, concat_axis=0, tiled=True)
    small = small.reshape(OWNERS, SMALL_ROWS, STATE)
    small = to_owners(pack_small(send_slot, destination % OWNERS, small))
    src = find_source(small)

    x_slots = []
    for half in range(2):
        arrived = []
        for shift, piece in zip(SHIFTS, cut(half, dest_heads, x_rows)):
            pairs = [(h, partner(h, shift)) for h in range(PEERS)]
            arrived.append(lax.ppermute(piece, "head", pairs))
        x_slots.append(to_owners(pack_x(half, send_slot, origin, x_rows, arrived)))

    pieces = destination.shape[0]
    seg = jnp.cumsum(doc_start.reshape(pieces, PIECE), axis=1).astype(F32)[:, None, :]
    rows, scales, ends, total = decays(
        src, small, seg, dt_bias.reshape(HEADS, 1), a_log.reshape(HEADS, 1)
    )
    skip = jnp.repeat(d_skip, HEAD_DIM).reshape(1, WIDTH)
    spread_four, spread_two = spread(4), spread(2)

    g_local, g_state = backward_local(src, small, cotangent, rows, scales, spread_four, skip)
    y_a, state_a = forward_local(0, src, small, x_slots[0], rows, scales, spread_four, skip)
    state_b = forward_state(1, src, small, x_slots[1], ends, spread_two)
    y_b, unused = forward_local(1, src, small, x_slots[1], rows, scales, spread_four, skip)

    parts = to_owners(join_states(state_a, state_b, g_state, total))
    back = (me >= OWNERS // 2).astype(jnp.int32).reshape(1)
    enter = to_owners(scan_owners(back, parts)).reshape(2 * STATE, WIDTH)
    y, g = finish(src, small, y_a, y_b, g_local, enter, ends, spread_two)
    return (y, g)


def solution(mesh):
    in_specs = (
        P(("ctx", "head"), None),
        P(("ctx", "head"), None),
        P(("ctx", "head"), None),
        P(("ctx", "head"), None),
        P("ctx"),
        P("ctx"),
        P("head"),
        P("head"),
        P("head"),
        P("ctx", "head"),
    )
    out_specs = (P("ctx", "head"), P("ctx", "head"))
    return jax.shard_map(body, mesh=mesh, in_specs=in_specs, out_specs=out_specs, check_vma=False)
```

time: 724 us -> 284 us (0.39)
  local copies, waits for them, and re-layouts: 176 us -> 22 us
  waiting for transfers between devices: 207 us -> 84.3 us
  Pallas kernels: 0 us -> 107 us
  other arithmetic: 107 us -> 1.7 us
  matrix products: 81.7 us -> 0 us
  blocking collectives: 68.5 us -> 0 us
  between operations: 15 us -> 0.92 us
  starting transfers between devices: 53.2 us -> 65.3 us
    all_to_all x9 -> x6, waiting for transfers between devices: 167 us -> 45.5 us  [the longest x5 31.1 us: to_owners(): return lax.all_to_all(value, 'ctx', split_axis=0, concat_axis=0, tiled=True)]
    pallas_call x0 -> x15, Pallas kernels: none -> 107 us  [the longest x2 34.1 us: forward_local(): pl.pallas_call(partial(forward_kernel, half * HEADS // 2), grid_spec=pltp...]
    dot_general x42 -> x0, matrix products: 81.7 us -> none  [the longest x8 23.8 us: block_local(): jnp.einsum('gjtu,ugjp->tgjp', forward_weights, x_four, preferred_element_...]
    unnamed x1 -> x0, blocking collectives: 68.5 us -> none
    scatter x9 -> x0, local copies, waits for them, and re-layouts: 45.9 us -> none  [the longest x4 27 us: unpack(): placed = jnp.zeros((owners, piece_rows, col_count), received.dtype).at[ta...]
    all_gather x2 -> x0, waiting for transfers between devices: 39.7 us -> none  [entering(): everything = jax.tree.map(lambda part: lax.all_gather(part, axis), shard)]
    ppermute x0 -> x14, waiting for transfers between devices: none -> 38.8 us  [body(): arrived.append(lax.ppermute(piece, 'head', pairs))]
    unnamed x29 -> x52, local copies, waits for them, and re-layouts: 60.1 us -> 21.5 us
  transfers between devices with their start and end apart: 11 -> 20, of which waited for: 10 -> 14; matrix products, arithmetic and copies ran while one was open for 18% -> 1% of each run, Pallas kernels for 0% -> 28%
where the time goes in v1:
time: 284 us; the launch traced here: 281 us
  Pallas kernels  107 us (38%)
  waiting for transfers between devices  84.3 us (30%)
  starting transfers between devices  65.3 us (23%)
  local copies, waits for them, and re-layouts  22 us (8%)
    all_to_all x5, starting transfers between devices, to_owners(): return lax.all_to_all(value, 'ctx', split_axis=0, concat_axis=0, tiled=True)  48.8 us
    ppermute x14, waiting for transfers between devices, body(): arrived.append(lax.ppermute(piece, 'head', pairs))  38.8 us
    pallas_call x2, Pallas kernels, forward_local(): pl.pallas_call(partial(forward_kernel, half * HEADS // 2), grid_spec=pltp...  34.1 us
    pallas_call x1, Pallas kernels, backward_local(): pl.pallas_call(backward_kernel, grid_spec=pltpu.PrefetchScalarGridSpec(nu...  32.4 us
    all_to_all x5, waiting for transfers between devices, to_owners(): return lax.all_to_all(value, 'ctx', split_axis=0, concat_axis=0, tiled=True)  31.1 us
    unnamed x52, local copies, waits for them, and re-layouts  21.5 us
    pallas_call x1, Pallas kernels, finish(): pl.pallas_call(finish_kernel, grid_spec=pltpu.PrefetchScalarGridSpec(num_...  16.7 us
    all_to_all x1, waiting for transfers between devices, body(): lax.all_to_all(small, 'head', split_axis=0, concat_axis=0, tiled=True)  14.4 us
  transfers between devices with their start and end apart: 20, of which 14 were waited for; matrix products, arithmetic and copies ran while one was open for 1% of the time, Pallas kernels for 28%

profile of v1, /device:TPU:98, one launch (start us, length us, event | category | flops | bytes accessed | tf_op | source)
XLA Modules:
  0.0 281.3 jit_solution(15262781844683465893)
XLA Ops:
  4.8 4.5 %all-to-all-start = ((bf16[8,2,272,128]{3,2,1,0:T(8,128)(2,1)}), bf16[8,2,272,128]{3,2,1,0:T(8,128)(2,1)S(1)}, u32[]{:S(2)}, u32[]{:S(2)}) async-start(bf16[8,2,272,128]{3,2,1,0:T(8,128)(2,1)} %gather_small.1), calls=%async_computation | async-start | bytes 2228224 | tf_op jit(solution)/shard_map/all_to_all | solution.py:635
  9.6 14.4 %all-to-all-done = bf16[8,2,272,128]{3,2,1,0:T(8,128)(2,1)S(1)} async-done(((bf16[8,2,272,128]{3,2,1,0:T(8,128)(2,1)}), bf16[8,2,272,128]{3,2,1,0:T(8,128)(2,1)S(1)}, u32[]{:S(2)}, u32[]{:S(2)}) %all-to-all-start) | async-done | bytes 1114144 | tf_op jit(solution)/shard_map/all_to_all | solution.py:635
  27.6 7.5 %all-to-all-start.1 = ((bf16[32,288,128]{2,1,0:T(8,128)(2,1)}), bf16[32,288,128]{2,1,0:T(8,128)(2,1)S(1)}, u32[]{:S(2)}, u32[]{:S(2)}) async-start(bf16[32,288,128]{2,1,0:T(8,128)(2,1)} %copy-done.4), calls=%async_computation.1 | async-start | bytes 4718592 | tf_op jit(solution)/shard_map/all_to_all | solution.py:622
  45.0 3.4 %collective-permute-done.rest_0_ = bf16[256,512]{1,0:T(8,128)(2,1)S(1)} collective-permute-done((bf16[256,512]{1,0:T(8,128)(2,1)S(1)}, bf16[256,512]{1,0:T(8,128)(2,1)S(1)}, u32[]{:S(2)}, u32[]{:S(2)}) %collective-permute-start) | collective-permute-done | bytes 262176 | tf_op jit(solution)/shard_map/ppermute | solution.py:645
  48.4 3.3 %collective-permute-done.1.rest_1_ = bf16[256,512]{1,0:T(8,128)(2,1)S(1)} collective-permute-done((bf16[256,512]{1,0:T(8,128)(2,1)S(1)}, bf16[256,512]{1,0:T(8,128)(2,1)S(1)}, u32[]{:S(2)}, u32[]{:S(2)}) %collective-permute-start.1) | collective-permute-done | bytes 262176 | tf_op jit(solution)/shard_map/ppermute | solution.py:645
  51.7 11.3 %collective-permute-done.2.rest_2_ = bf16[256,512]{1,0:T(8,128)(2,1)S(1)} collective-permute-done((bf16[256,512]{1,0:T(8,128)(2,1)}, bf16[256,512]{1,0:T(8,128)(2,1)S(1)}, u32[]{:S(2)}, u32[]{:S(2)}) %collective-permute-start.2) | collective-permute-done | bytes 262176 | tf_op jit(solution)/shard_map/ppermute | solution.py:645
  64.2 3.3 %pack_x.2 = bf16[32,128,512]{2,1,0:T(8,128)(2,1)S(1)} custom-call(s32[16]{0:T(128)S(1)} %multiply_add_fusion.slot_ref, s32[8]{0:T(128)S(1)} %stack.47.from_ref, bf16[256,8192]{1,0:T(8,128)(2,1)} %x_ref.7, bf16[256,512]{1,0:T(8,128)(2,1)S(1)} %collective-permute-done.rest_0_, bf16[256,512]{1,0:T(8,128)(2,1)S(1)} %collective-permute-done.1.rest_1_, ...), custom_call_target="tpu_custom_call" | custom-call | tf_op jit(solution)/shard_map/pack_x/pallas_call | solution.py:199
  69.6 7.2 %all-to-all-start.2 = ((bf16[32,128,512]{2,1,0:T(8,128)(2,1)}), bf16[32,128,512]{2,1,0:T(8,128)(2,1)}, u32[]{:S(2)}, u32[]{:S(2)}) async-start(bf16[32,128,512]{2,1,0:T(8,128)(2,1)} %copy-done.2), calls=%async_computation.2 | async-start | bytes 8388608 | tf_op jit(solution)/shard_map/all_to_all | solution.py:622
  85.6 3.1 %collective-permute-done.7.rest_0_ = bf16[256,512]{1,0:T(8,128)(2,1)S(1)} collective-permute-done((bf16[256,512]{1,0:T(8,128)(2,1)S(1)}, bf16[256,512]{1,0:T(8,128)(2,1)S(1)}, u32[]{:S(2)}, u32[]{:S(2)}) %collective-permute-start.7) | collective-permute-done | bytes 262176 | tf_op jit(solution)/shard_map/ppermute | solution.py:645
  89.0 3.1 %collective-permute-done.8.rest_1_ = bf16[256,512]{1,0:T(8,128)(2,1)S(1)} collective-permute-done((bf16[256,512]{1,0:T(8,128)(2,1)S(1)}, bf16[256,512]{1,0:T(8,128)(2,1)S(1)}, u32[]{:S(2)}, u32[]{:S(2)}) %collective-permute-start.8) | collective-permute-done | bytes 262176 | tf_op jit(solution)/shard_map/ppermute | solution.py:645
  95.7 6.6 %collective-permute-done.11.rest_4_ = bf16[256,512]{1,0:T(8,128)(2,1)S(1)} collective-permute-done((bf16[256,512]{1,0:T(8,128)(2,1)S(1)}, bf16[256,512]{1,0:T(8,128)(2,1)S(1)}, u32[]{:S(2)}, u32[]{:S(2)}) %collective-permute-start.11) | collective-permute-done | bytes 262176 | tf_op jit(solution)/shard_map/ppermute | solution.py:645
  102.3 3.2 %collective-permute-done.12.rest_5_ = bf16[256,512]{1,0:T(8,128)(2,1)S(1)} collective-permute-done((bf16[256,512]{1,0:T(8,128)(2,1)S(1)}, bf16[256,512]{1,0:T(8,128)(2,1)S(1)}, u32[]{:S(2)}, u32[]{:S(2)}) %collective-permute-start.12) | collective-permute-done | bytes 262176 | tf_op jit(solution)/shard_map/ppermute | solution.py:645
  105.5 4.3 %pack_x.3 = bf16[32,128,512]{2,1,0:T(8,128)(2,1)S(1)} custom-call(s32[16]{0:T(128)S(1)} %multiply_add_fusion.slot_ref, s32[8]{0:T(128)S(1)} %stack.47.from_ref, bf16[256,8192]{1,0:T(8,128)(2,1)} %x_ref.7, bf16[256,512]{1,0:T(8,128)(2,1)S(1)} %collective-permute-done.7.rest_0_, bf16[256,512]{1,0:T(8,128)(2,1)S(1)} %collective-permute-done.8.rest_1_, ...), custom_call_target="tpu_custom_call" | custom-call | tf_op jit(solution)/shard_map/pack_x/pallas_call | solution.py:199
  111.8 20.5 %all-to-all-done.2.x_ref = bf16[32,128,512]{2,1,0:T(8,128)(2,1)} async-done(((bf16[32,128,512]{2,1,0:T(8,128)(2,1)}), bf16[32,128,512]{2,1,0:T(8,128)(2,1)}, u32[]{:S(2)}, u32[]{:S(2)}) %all-to-all-start.2) | async-done | bytes 4194336 | tf_op jit(solution)/shard_map/all_to_all | solution.py:622
  132.3 14.1 %all-to-all-start.3 = ((bf16[32,128,512]{2,1,0:T(8,128)(2,1)}), bf16[32,128,512]{2,1,0:T(8,128)(2,1)}, u32[]{:S(2)}, u32[]{:S(2)}) async-start(bf16[32,128,512]{2,1,0:T(8,128)(2,1)} %copy-done.3), calls=%async_computation.3 | async-start | bytes 8388608 | tf_op jit(solution)/shard_map/all_to_all | solution.py:622
  150.4 32.4 %backward_local.1 = (f32[16,128,1024]{2,1,0:T(8,128)}, bf16[128,1024]{1,0:T(8,128)(2,1)S(1)}) custom-call(s32[1,128]{1,0:T(1,128)S(1)} %find_source.1.src_ref, bf16[32,288,128]{2,1,0:T(8,128)(2,1)S(1)} %all-to-all-done.1.small_ref, bf16[2048,1024]{1,0:T(8,128)(2,1)} %cot_ref.1, f32[16,40,128]{2,1,0:T(8,128)S(1)} %get-tuple-element.32.rows_ref, ...), custom_call_target="tpu_custom_call" | custom-call | tf_op jit(solution)/shard_map/backward_local/pallas_call | solution.py:495
  183.5 17.0 %forward_local.2 = (f32[16,128,512]{2,1,0:T(8,128)}, bf16[128,512]{1,0:T(8,128)(2,1)S(1)}) custom-call(s32[1,128]{1,0:T(1,128)S(1)} %find_source.1.src_ref, bf16[32,288,128]{2,1,0:T(8,128)(2,1)S(1)} %all-to-all-done.1.small_ref, bf16[32,128,512]{2,1,0:T(8,128)(2,1)} %all-to-all-done.2.x_ref, f32[16,40,128]{2,1,0:T(8,128)S(1)} %get-tuple-element.32.rows_ref, ...), custom_call_target="tpu_custom_call" | custom-call | tf_op jit(solution)/shard_map/forward_local/pallas_call | solution.py:382
  203.4 6.0 %forward_state.1.b_ref = bf16[128,512]{1,0:T(8,128)(2,1)S(1)} custom-call(s32[1,128]{1,0:T(1,128)S(1)} %find_source.1.src_ref, bf16[32,288,128]{2,1,0:T(8,128)(2,1)S(1)} %all-to-all-done.1.small_ref, bf16[32,128,512]{2,1,0:T(8,128)(2,1)} %all-to-all-done.3.x_ref, bf16[16,64,128]{2,1,0:T(8,128)(2,1)S(1)} %copy-done.14, bf16[2,64,1024]{2,1,0:T(8,128)(2,1)S(1)} %copy-done.9), custom_call_target="tpu_custom_call" | custom-call | tf_op jit(solution)/shard_map/forward_state/pallas_call | solution.py:437
  210.4 13.8 %all-to-all-start.4 = ((bf16[16,16,1152]{2,1,0:T(8,128)(2,1)}), bf16[16,16,1152]{2,1,0:T(8,128)(2,1)}, u32[]{:S(2)}, u32[]{:S(2)}) async-start(bf16[16,16,1152]{2,1,0:T(8,128)(2,1)} %copy-done.11), calls=%async_computation.4 | async-start | bytes 1179648 | tf_op jit(solution)/shard_map/all_to_all | solution.py:622
  224.1 9.6 %all-to-all-done.4.part_ref = bf16[16,16,1152]{2,1,0:T(8,128)(2,1)} async-done(((bf16[16,16,1152]{2,1,0:T(8,128)(2,1)}), bf16[16,16,1152]{2,1,0:T(8,128)(2,1)}, u32[]{:S(2)}, u32[]{:S(2)}) %all-to-all-start.4) | async-done | bytes 589856 | tf_op jit(solution)/shard_map/all_to_all | solution.py:622
  233.8 2.9 %scan_owners.1 = bf16[16,16,1024]{2,1,0:T(8,128)(2,1)S(1)} custom-call(s32[1]{0:T(128)} %bitcast.14.back_ref, bf16[16,16,1152]{2,1,0:T(8,128)(2,1)} %all-to-all-done.4.part_ref), custom_call_target="tpu_custom_call" | custom-call | tf_op jit(solution)/shard_map/scan_owners/pallas_call | solution.py:563
  237.5 6.2 %all-to-all-start.5 = ((bf16[16,16,1024]{2,1,0:T(8,128)(2,1)}), bf16[16,16,1024]{2,1,0:T(8,128)(2,1)}, u32[]{:S(2)}, u32[]{:S(2)}) async-start(bf16[16,16,1024]{2,1,0:T(8,128)(2,1)} %copy-done.12), calls=%async_computation.5 | async-start | bytes 1048576 | tf_op jit(solution)/shard_map/all_to_all | solution.py:622
  245.7 17.1 %forward_local.3 = (f32[16,128,512]{2,1,0:T(8,128)}, bf16[128,512]{1,0:T(8,128)(2,1)}) custom-call(s32[1,128]{1,0:T(1,128)S(1)} %find_source.1.src_ref, bf16[32,288,128]{2,1,0:T(8,128)(2,1)S(1)} %all-to-all-done.1.small_ref, bf16[32,128,512]{2,1,0:T(8,128)(2,1)} %all-to-all-done.3.x_ref, f32[16,40,128]{2,1,0:T(8,128)S(1)} %copy-done.8, ...), custom_call_target="tpu_custom_call" | custom-call | tf_op jit(solution)/shard_map/forward_local/pallas_call | solution.py:382
  264.7 16.7 %finish.1 = (bf16[2048,1024]{1,0:T(8,128)(2,1)}, bf16[2048,1024]{1,0:T(8,128)(2,1)}) custom-call(s32[1,128]{1,0:T(1,128)S(1)} %find_source.1.src_ref, bf16[32,288,128]{2,1,0:T(8,128)(2,1)S(1)} %all-to-all-done.1.small_ref, f32[16,128,512]{2,1,0:T(8,128)} %get-tuple-element.34.ya_ref, f32[16,128,512]{2,1,0:T(8,128)} %get-tuple-element.42.yb_ref, ...), custom_call_target="tpu_custom_call" | custom-call | tf_op jit(solution)/shard_map/finish/pallas_call | solution.py:591
  (105 shorter events, 49.0 us)
Async XLA Ops:
  4.8 19.1 %all-to-all-start = ((bf16[8,2,272,128]{3,2,1,0:T(8,128)(2,1)}), bf16[8,2,272,128]{3,2,1,0:T(8,128)(2,1)S(1)}, u32[]{:S(2)}, u32[]{:S(2)}) async-start(bf16[8,2,272,128]{3,2,1,0:T(8,128)(2,1)} %gather_small.1), calls=%async_computation | async-start | bytes 2228224 | tf_op jit(solution)/shard_map/all_to_all | solution.py:635
  27.6 42.0 %all-to-all-start.1 = ((bf16[32,288,128]{2,1,0:T(8,128)(2,1)}), bf16[32,288,128]{2,1,0:T(8,128)(2,1)S(1)}, u32[]{:S(2)}, u32[]{:S(2)}) async-start(bf16[32,288,128]{2,1,0:T(8,128)(2,1)} %copy-done.4), calls=%async_computation.1 | async-start | bytes 4718592 | tf_op jit(solution)/shard_map/all_to_all | solution.py:622
  39.0 9.3 %collective-permute-start = (bf16[256,512]{1,0:T(8,128)(2,1)S(1)}, bf16[256,512]{1,0:T(8,128)(2,1)S(1)}, u32[]{:S(2)}, u32[]{:S(2)}) collective-permute-start(bf16[256,512]{1,0:T(8,128)(2,1)S(1)} %get-tuple-element.25), channel_id=1, source_target_pairs={{0,2},{1,3},{2,4},{3,5},{4,6},{5,7},{6,0},{7,1},{8,10},{9,11},{10,... | collective-permute-start | bytes 786440 | tf_op jit(solution)/shard_map/ppermute | solution.py:645
  41.2 10.5 %collective-permute-start.1 = (bf16[256,512]{1,0:T(8,128)(2,1)S(1)}, bf16[256,512]{1,0:T(8,128)(2,1)S(1)}, u32[]{:S(2)}, u32[]{:S(2)}) collective-permute-start(bf16[256,512]{1,0:T(8,128)(2,1)S(1)} %get-tuple-element.26), channel_id=1, source_target_pairs={{0,6},{1,7},{2,0},{3,1},{4,2},{5,3},{6,4},{7,5},{8,14},{9,15},{10,... | collective-permute-start | bytes 786440 | tf_op jit(solution)/shard_map/ppermute | solution.py:645
  41.2 21.8 %collective-permute-start.2 = (bf16[256,512]{1,0:T(8,128)(2,1)}, bf16[256,512]{1,0:T(8,128)(2,1)S(1)}, u32[]{:S(2)}, u32[]{:S(2)}) collective-permute-start(bf16[256,512]{1,0:T(8,128)(2,1)} %get-tuple-element.27), channel_id=1, source_target_pairs={{0,3},{1,2},{2,5},{3,4},{4,7},{5,6},{6,1},{7,0},{8,11},{9,10},{10,... | collective-permute-start | bytes 786440 | tf_op jit(solution)/shard_map/ppermute | solution.py:645
  42.5 20.4 %collective-permute-start.3 = (bf16[256,512]{1,0:T(8,128)(2,1)}, bf16[256,512]{1,0:T(8,128)(2,1)S(1)}, u32[]{:S(2)}, u32[]{:S(2)}) collective-permute-start(bf16[256,512]{1,0:T(8,128)(2,1)} %get-tuple-element.28), channel_id=1, source_target_pairs={{0,7},{1,6},{2,1},{3,0},{4,3},{5,2},{6,5},{7,4},{8,15},{9,14},{10,... | collective-permute-start | bytes 786440 | tf_op jit(solution)/shard_map/ppermute | solution.py:645
  42.9 20.1 %collective-permute-start.4 = (bf16[256,512]{1,0:T(8,128)(2,1)}, bf16[256,512]{1,0:T(8,128)(2,1)}, u32[]{:S(2)}, u32[]{:S(2)}) collective-permute-start(bf16[256,512]{1,0:T(8,128)(2,1)} %get-tuple-element.29), channel_id=1, source_target_pairs={{0,4},{1,5},{2,6},{3,7},{4,0},{5,1},{6,2},{7,3},{8,12},{9,13},{10,... | collective-permute-start | bytes 786440 | tf_op jit(solution)/shard_map/ppermute | solution.py:645
  48.4 15.8 %collective-permute-start.5 = (bf16[256,512]{1,0:T(8,128)(2,1)}, bf16[256,512]{1,0:T(8,128)(2,1)}, u32[]{:S(2)}, u32[]{:S(2)}) collective-permute-start(bf16[256,512]{1,0:T(8,128)(2,1)} %get-tuple-element.30), channel_id=1, source_target_pairs={{0,5},{1,4},{2,7},{3,6},{4,1},{5,0},{6,3},{7,2},{8,13},{9,12},{10,... | collective-permute-start | bytes 786440 | tf_op jit(solution)/shard_map/ppermute | solution.py:645
  51.6 12.6 %collective-permute-start.6 = (bf16[256,512]{1,0:T(8,128)(2,1)}, bf16[256,512]{1,0:T(8,128)(2,1)}, u32[]{:S(2)}, u32[]{:S(2)}) collective-permute-start(bf16[256,512]{1,0:T(8,128)(2,1)} %get-tuple-element.31), channel_id=1, source_target_pairs={{0,1},{1,0},{2,3},{3,2},{4,5},{5,4},{6,7},{7,6},{8,9},{9,8},{10,11... | collective-permute-start | bytes 786440 | tf_op jit(solution)/shard_map/ppermute | solution.py:645
  69.6 62.7 %all-to-all-start.2 = ((bf16[32,128,512]{2,1,0:T(8,128)(2,1)}), bf16[32,128,512]{2,1,0:T(8,128)(2,1)}, u32[]{:S(2)}, u32[]{:S(2)}) async-start(bf16[32,128,512]{2,1,0:T(8,128)(2,1)} %copy-done.2), calls=%async_computation.2 | async-start | bytes 8388608 | tf_op jit(solution)/shard_map/all_to_all | solution.py:622
  79.7 9.0 %collective-permute-start.7 = (bf16[256,512]{1,0:T(8,128)(2,1)S(1)}, bf16[256,512]{1,0:T(8,128)(2,1)S(1)}, u32[]{:S(2)}, u32[]{:S(2)}) collective-permute-start(bf16[256,512]{1,0:T(8,128)(2,1)S(1)} %get-tuple-element.35), channel_id=1, source_target_pairs={{0,2},{1,3},{2,4},{3,5},{4,6},{5,7},{6,0},{7,1},{8,10},{9,11},{10,... | collective-permute-start | bytes 786440 | tf_op jit(solution)/shard_map/ppermute | solution.py:645
  81.6 10.4 %collective-permute-start.8 = (bf16[256,512]{1,0:T(8,128)(2,1)S(1)}, bf16[256,512]{1,0:T(8,128)(2,1)S(1)}, u32[]{:S(2)}, u32[]{:S(2)}) collective-permute-start(bf16[256,512]{1,0:T(8,128)(2,1)S(1)} %get-tuple-element.36), channel_id=1, source_target_pairs={{0,6},{1,7},{2,0},{3,1},{4,2},{5,3},{6,4},{7,5},{8,14},{9,15},{10,... | collective-permute-start | bytes 786440 | tf_op jit(solution)/shard_map/ppermute | solution.py:645
  81.8 13.1 %collective-permute-start.9 = (bf16[256,512]{1,0:T(8,128)(2,1)S(1)}, bf16[256,512]{1,0:T(8,128)(2,1)S(1)}, u32[]{:S(2)}, u32[]{:S(2)}) collective-permute-start(bf16[256,512]{1,0:T(8,128)(2,1)S(1)} %get-tuple-element.37), channel_id=1, source_target_pairs={{0,3},{1,2},{2,5},{3,4},{4,7},{5,6},{6,1},{7,0},{8,11},{9,10},{10,... | collective-permute-start | bytes 786440 | tf_op jit(solution)/shard_map/ppermute | solution.py:645
  83.8 11.9 %collective-permute-start.10 = (bf16[256,512]{1,0:T(8,128)(2,1)S(1)}, bf16[256,512]{1,0:T(8,128)(2,1)S(1)}, u32[]{:S(2)}, u32[]{:S(2)}) collective-permute-start(bf16[256,512]{1,0:T(8,128)(2,1)S(1)} %get-tuple-element.38), channel_id=1, source_target_pairs={{0,7},{1,6},{2,1},{3,0},{4,3},{5,2},{6,5},{7,4},{8,15},{9,14},{10,... | collective-permute-start | bytes 786440 | tf_op jit(solution)/shard_map/ppermute | solution.py:645
  83.8 18.5 %collective-permute-start.11 = (bf16[256,512]{1,0:T(8,128)(2,1)S(1)}, bf16[256,512]{1,0:T(8,128)(2,1)S(1)}, u32[]{:S(2)}, u32[]{:S(2)}) collective-permute-start(bf16[256,512]{1,0:T(8,128)(2,1)S(1)} %get-tuple-element.39), channel_id=1, source_target_pairs={{0,4},{1,5},{2,6},{3,7},{4,0},{5,1},{6,2},{7,3},{8,12},{9,13},{10,... | collective-permute-start | bytes 786440 | tf_op jit(solution)/shard_map/ppermute | solution.py:645
  88.7 16.8 %collective-permute-start.12 = (bf16[256,512]{1,0:T(8,128)(2,1)S(1)}, bf16[256,512]{1,0:T(8,128)(2,1)S(1)}, u32[]{:S(2)}, u32[]{:S(2)}) collective-permute-start(bf16[256,512]{1,0:T(8,128)(2,1)S(1)} %get-tuple-element.40), channel_id=1, source_target_pairs={{0,5},{1,4},{2,7},{3,6},{4,1},{5,0},{6,3},{7,2},{8,13},{9,12},{10,... | collective-permute-start | bytes 786440 | tf_op jit(solution)/shard_map/ppermute | solution.py:645
  92.0 13.5 %collective-permute-start.13 = (bf16[256,512]{1,0:T(8,128)(2,1)S(1)}, bf16[256,512]{1,0:T(8,128)(2,1)S(1)}, u32[]{:S(2)}, u32[]{:S(2)}) collective-permute-start(bf16[256,512]{1,0:T(8,128)(2,1)S(1)} %get-tuple-element.41), channel_id=1, source_target_pairs={{0,1},{1,0},{2,3},{3,2},{4,5},{5,4},{6,7},{7,6},{8,9},{9,8},{10,11... | collective-permute-start | bytes 786440 | tf_op jit(solution)/shard_map/ppermute | solution.py:645
  111.8 34.6 %copy-start.21 = (s32[2048]{0:T(1024)S(1)}, s32[2048]{0:T(1024)}, u32[]{:S(2)}) copy-start(s32[2048]{0:T(1024)} %param.15) | copy-start | bytes 24580
  111.8 34.9 %copy-start.22 = (f32[16]{0:T(128)S(1)}, f32[16]{0:T(128)}, u32[]{:S(2)}) copy-start(f32[16]{0:T(128)} %param.16) | copy-start | bytes 196
  111.8 35.0 %copy-start.23 = (f32[16]{0:T(128)S(1)}, f32[16]{0:T(128)}, u32[]{:S(2)}) copy-start(f32[16]{0:T(128)} %param.17) | copy-start | bytes 196
  111.8 35.0 %copy-start.24 = (f32[16]{0:T(128)S(1)}, f32[16]{0:T(128)}, u32[]{:S(2)}) copy-start(f32[16]{0:T(128)} %param.18) | copy-start | bytes 196
  132.3 69.2 %all-to-all-start.3 = ((bf16[32,128,512]{2,1,0:T(8,128)(2,1)}), bf16[32,128,512]{2,1,0:T(8,128)(2,1)}, u32[]{:S(2)}, u32[]{:S(2)}) async-start(bf16[32,128,512]{2,1,0:T(8,128)(2,1)} %copy-done.3), calls=%async_computation.3 | async-start | bytes 8388608 | tf_op jit(solution)/shard_map/all_to_all | solution.py:622
  210.4 23.4 %all-to-all-start.4 = ((bf16[16,16,1152]{2,1,0:T(8,128)(2,1)}), bf16[16,16,1152]{2,1,0:T(8,128)(2,1)}, u32[]{:S(2)}, u32[]{:S(2)}) async-start(bf16[16,16,1152]{2,1,0:T(8,128)(2,1)} %copy-done.11), calls=%async_computation.4 | async-start | bytes 1179648 | tf_op jit(solution)/shard_map/all_to_all | solution.py:622
  237.5 25.3 %all-to-all-start.5 = ((bf16[16,16,1024]{2,1,0:T(8,128)(2,1)}), bf16[16,16,1024]{2,1,0:T(8,128)(2,1)}, u32[]{:S(2)}, u32[]{:S(2)}) async-start(bf16[16,16,1024]{2,1,0:T(8,128)(2,1)} %copy-done.12), calls=%async_computation.5 | async-start | bytes 1048576 | tf_op jit(solution)/shard_map/all_to_all | solution.py:622
  (22 other events, 98.2 us)

commit v2 on v1

v2 whole, which is shorter than its diff:
```python
from functools import partial

import jax
import jax.numpy as jnp
from jax import lax
from jax.experimental import pallas as pl
from jax.experimental.pallas import tpu as pltpu
from jax.sharding import PartitionSpec as P

OWNERS = 16
PEERS = 8
PIECE = 128
STATE = 128
HEADS = 16
HEAD_DIM = 64
WIDTH = HEADS * HEAD_DIM
HALF = WIDTH // 2
SMALL_ROWS = 2 * PIECE + HEADS
TAG_ROWS = 16
SENT_ROWS = SMALL_ROWS + TAG_ROWS
EXTRA = 128
LOG2E = 1.4426950408889634
F32 = jnp.float32
BF16 = jnp.bfloat16
ANY = pl.BlockSpec(memory_space=pl.ANY)
WHOLE = pl.BlockSpec(memory_space=pltpu.VMEM)
SMEM = pl.BlockSpec(memory_space=pltpu.SMEM)
SHIFTS = [(1, 0), (3, 0), (1, 1), (3, 1), (2, 0), (2, 1), (0, 1)]


def params(mib=56):
    return pltpu.CompilerParams(vmem_limit_bytes=mib * 1024 * 1024)


def partner(head, shift):
    return (head // 2 + shift[0]) % 4 * 2 + (head % 2 + shift[1]) % 2


def source(head, shift):
    return (head // 2 + 4 - shift[0]) % 4 * 2 + (head % 2 + shift[1]) % 2


def run_copies(copies):
    for copy in copies:
        copy.start()
    for copy in copies:
        copy.wait()


def gather_small_kernel(b_ref, c_ref, dt_ref, out_ref, turned, sems):
    copies = []
    for r in range(2):
        rows = pl.ds(r * PIECE, PIECE)
        for g in range(PEERS):
            cols = pl.ds(g * STATE, STATE)
            for kind, ref in enumerate((b_ref, c_ref)):
                copies.append(
                    pltpu.make_async_copy(
                        ref.at[rows, cols],
                        out_ref.at[g, r, pl.ds(kind * PIECE, PIECE), :],
                        sems.at[len(copies)],
                    )
                )
    for copy in copies:
        copy.start()
    last = []
    for r in range(2):
        dt_t = dt_ref[r * PIECE : (r + 1) * PIECE, :].astype(F32).T.astype(BF16)
        for g in range(PEERS):
            turned[g, r] = dt_t[g * HEADS : (g + 1) * HEADS, :]
    last = pltpu.make_async_copy(
        turned, out_ref.at[:, :, pl.ds(2 * PIECE, HEADS), :], sems.at[len(copies)]
    )
    last.start()
    for copy in copies + [last]:
        copy.wait()


def gather_small(b_rows, c_rows, dt_rows):
    return pl.pallas_call(
        gather_small_kernel,
        in_specs=[WHOLE, WHOLE, WHOLE],
        out_specs=ANY,
        out_shape=jax.ShapeDtypeStruct((PEERS, 2, SMALL_ROWS, STATE), BF16),
        scratch_shapes=[
            pltpu.VMEM((PEERS, 2, HEADS, PIECE), BF16),
            pltpu.SemaphoreType.DMA((4 * PEERS + 1,)),
        ],
        compiler_params=params(),
        name="gather_small",
    )(b_rows, c_rows, dt_rows)


def pack_small_kernel(slot_ref, place_ref, in_ref, out_ref, tags, sems):
    copies = [
        pltpu.make_async_copy(
            in_ref.at[j], out_ref.at[slot_ref[j], pl.ds(0, SMALL_ROWS), :], sems.at[j]
        )
        for j in range(OWNERS)
    ]
    for copy in copies:
        copy.start()
    tags[...] = jnp.full(tags.shape, -1.0, BF16)
    for j in range(OWNERS):
        place = place_ref[j].astype(F32)
        tags[slot_ref[j]] = jnp.full(tags.shape[1:], place, F32).astype(BF16)
    last = pltpu.make_async_copy(
        tags, out_ref.at[:, pl.ds(SMALL_ROWS, TAG_ROWS), :], sems.at[OWNERS]
    )
    last.start()
    for copy in copies + [last]:
        copy.wait()


def pack_small(slot, place, pieces):
    return pl.pallas_call(
        pack_small_kernel,
        in_specs=[SMEM, SMEM, WHOLE],
        out_specs=ANY,
        out_shape=jax.ShapeDtypeStruct((2 * OWNERS, SENT_ROWS, STATE), BF16),
        scratch_shapes=[
            pltpu.VMEM((2 * OWNERS, TAG_ROWS, STATE), BF16),
            pltpu.SemaphoreType.DMA((OWNERS + 1,)),
        ],
        compiler_params=params(),
        name="pack_small",
    )(slot, place, pieces)


def find_source_kernel(small_ref, out_ref, tags, sem):
    copy = pltpu.make_async_copy(
        small_ref.at[:, pl.ds(SMALL_ROWS, TAG_ROWS), :], tags, sem.at[0]
    )
    copy.start()
    copy.wait()
    slot = lax.broadcasted_iota(jnp.int32, tags.shape, 0).astype(F32)
    place = lax.broadcasted_iota(jnp.int32, tags.shape, 2).astype(F32)
    found = jnp.where(tags[...].astype(F32) == place, slot, 0.0)
    out_ref[...] = jnp.sum(found, axis=0)[0:1].astype(jnp.int32)


def find_source(small):
    return pl.pallas_call(
        find_source_kernel,
        in_specs=[ANY],
        out_specs=pl.BlockSpec(memory_space=pltpu.VMEM),
        out_shape=jax.ShapeDtypeStruct((1, STATE), jnp.int32),
        scratch_shapes=[
            pltpu.VMEM((2 * OWNERS, TAG_ROWS, STATE), BF16),
            pltpu.SemaphoreType.DMA((1,)),
        ],
        compiler_params=params(),
        name="find_source",
    )(small)


def cut_kernel(half, dest_ref, x_ref, *rest):
    count = len(SHIFTS)
    outs, (held, sems) = rest[:count], rest[count:]
    ins, copies = [], []
    for i in range(count):
        at = pl.multiple_of(dest_ref[i] * WIDTH + half * HALF, HALF)
        ins.append(pltpu.make_async_copy(x_ref.at[:, pl.ds(at, HALF)], held.at[i], sems.at[0, i]))
        copies.append(pltpu.make_async_copy(held.at[i], outs[i], sems.at[1, i]))
    for copy in ins:
        copy.start()
    for i in range(count):
        ins[i].wait()
        copies[i].start()
    for copy in copies:
        copy.wait()


def cut(half, dest, x_rows):
    count = len(SHIFTS)
    shape = (x_rows.shape[0], HALF)
    return pl.pallas_call(
        partial(cut_kernel, half),
        in_specs=[SMEM, ANY],
        out_specs=[ANY] * count,
        out_shape=[jax.ShapeDtypeStruct(shape, BF16)] * count,
        scratch_shapes=[
            pltpu.VMEM((count,) + shape, BF16),
            pltpu.SemaphoreType.DMA((2, count)),
        ],
        compiler_params=params(),
        name="cut",
    )(dest, x_rows)


def pack_x_kernel(half, slot_ref, from_ref, x_ref, *rest):
    arrived, (out_ref, held, sems) = rest[: len(SHIFTS)], rest[-3:]
    count = len(arrived)
    at = pl.multiple_of(from_ref[count] * WIDTH + half * HALF, HALF)
    ins, copies = [], []
    for i in range(count + 1):
        for r in range(2):
            n = 2 * i + r
            slot = slot_ref[from_ref[i] * 2 + r]
            rows = pl.ds(r * PIECE, PIECE)
            piece = arrived[i].at[rows, :] if i < count else x_ref.at[rows, pl.ds(at, HALF)]
            ins.append(pltpu.make_async_copy(piece, held.at[n], sems.at[0, n]))
            copies.append(pltpu.make_async_copy(held.at[n], out_ref.at[slot], sems.at[1, n]))
    for copy in ins:
        copy.start()
    for n, copy in enumerate(ins):
        copy.wait()
        copies[n].start()
    for copy in copies:
        copy.wait()


def pack_x(half, slot, origin, x_rows, arrived, after):
    return pl.pallas_call(
        partial(pack_x_kernel, half),
        in_specs=[SMEM, SMEM] + [ANY] * (1 + len(arrived) + len(after)),
        out_specs=ANY,
        out_shape=jax.ShapeDtypeStruct((2 * OWNERS, PIECE, HALF), BF16),
        scratch_shapes=[
            pltpu.VMEM((2 * PEERS, PIECE, HALF), BF16),
            pltpu.SemaphoreType.DMA((2, 2 * PEERS)),
        ],
        compiler_params=params(),
        name="pack_x",
    )(slot, origin, x_rows, *arrived, *after)


def split_two(value):
    high = value.astype(BF16)
    return high, (value - high.astype(F32)).astype(BF16)


def softplus(value):
    small = jnp.exp(-jnp.abs(value))
    series = small * (1.0 - small * (0.5 - small * (1.0 / 3.0 - small * 0.25)))
    return jnp.maximum(value, 0.0) + jnp.where(small < 1e-2, series, jnp.log(1.0 + small))


def decay_kernel(src_ref, small_ref, seg_ref, bias_ref, alog_ref, *rest):
    b_ref, c_ref, bt_ref, ct_ref, rows_ref, cols_ref, scale_ref, ends_ref, total_ref, dt_ref, sems = rest
    pieces = seg_ref.shape[0]
    copies = []
    for k in range(pieces):
        for at, to in enumerate((dt_ref, b_ref, c_ref)):
            start, size = ((2 * PIECE, HEADS), (0, PIECE), (PIECE, PIECE))[at]
            rows = small_ref.at[src_ref[0, k], pl.ds(start, size), :]
            copies.append(pltpu.make_async_copy(rows, to.at[k], sems.at[at, k]))
    for copy in copies:
        copy.start()
    for copy in copies:
        copy.wait()
    step_all = softplus(dt_ref[...].astype(F32) + bias_ref[...][None])
    rate_all = -step_all * (jnp.exp(alog_ref[...]) * LOG2E)[None]
    up_to = (
        lax.broadcasted_iota(jnp.int32, (PIECE, PIECE), 0)
        <= lax.broadcasted_iota(jnp.int32, (PIECE, PIECE), 1)
    ).astype(F32)
    log_all = jnp.dot(
        rate_all.reshape(pieces * HEADS, PIECE),
        up_to,
        precision=lax.Precision.HIGHEST,
        preferred_element_type=F32,
    ).reshape(pieces, HEADS, PIECE)
    ends = [log_all[k, :, PIECE - 1 :] for k in range(pieces)]
    starts = [seg_ref[k, :, PIECE - 1 :] for k in range(pieces)]
    none = jnp.zeros((1, 1), F32)
    log_before, starts_before = [jnp.zeros((HEADS, 1), F32)], [none]
    log_after, starts_after = [jnp.zeros((HEADS, 1), F32)], [none]
    for k in range(pieces):
        log_before.append(log_before[-1] + ends[k])
        starts_before.append(starts_before[-1] + starts[k])
        log_after.append(log_after[-1] + ends[pieces - 1 - k])
        starts_after.append(starts_after[-1] + starts[pieces - 1 - k])
    rest_rows = jnp.zeros((PIECE - 3 * HEADS - 1, PIECE), F32)
    head = lax.broadcasted_iota(jnp.int32, (HEADS, WIDTH), 0)
    lane = lax.broadcasted_iota(jnp.int32, (HEADS, WIDTH), 1)
    spread_one = (lane // HEAD_DIM == head).astype(BF16)
    for k in range(pieces):
        log, step, seg = log_all[k], step_all[k], seg_ref[k]
        shifted = log - jnp.log(step) * LOG2E
        rows = jnp.concatenate([log, shifted, step, seg, rest_rows], axis=0)
        rows_ref[k] = rows[0:ROW_COUNT]
        cols_ref[k] = rows.T
        bt_ref[k] = b_ref[k].astype(F32).T.astype(BF16)
        ct_ref[k] = c_ref[k].astype(F32).T.astype(BF16)
        none_yet = (seg == 0.0).astype(F32)
        none_left = (seg == starts[k]).astype(F32)
        left = pieces - 1 - k
        entry = jnp.exp2(log) * none_yet
        step_exit = step * (jnp.exp2(ends[k] - log) * none_left)
        no_before = none_yet * (starts_before[k] == 0.0).astype(F32)
        before = jnp.exp2(log_before[k] + log) * no_before
        no_after = none_left * (starts_after[left] == 0.0).astype(F32)
        after = step * (jnp.exp2(log_after[left] + (ends[k] - log)) * no_after)
        parts = []
        for value in (entry, step_exit, before, after):
            high = value.astype(BF16).astype(F32)
            parts += [high, value - high]
        scale_ref[k] = jnp.concatenate(parts, axis=0).T.astype(BF16)
        decay = jnp.exp2(ends[k]) * (starts[k] == 0.0).astype(F32)
        high, low = split_two(jnp.broadcast_to(decay, (HEADS, PIECE)))
        ends_ref[k] = (over_first(high, spread_one) + over_first(low, spread_one))[0:8]
    total_ref[...] = jnp.broadcast_to(
        jnp.exp2(log_before[-1]) * (starts_before[-1] == 0.0).astype(F32), total_ref.shape
    )


ROW_COUNT = 56
SEG = 3 * HEADS
ENTRY, STEP_EXIT, BEFORE, AFTER = range(4)
GROUP = 256
RUN = 4


def decays(src, small, seg, bias, alog):
    pieces = seg.shape[0]
    square = (pieces, PIECE, PIECE)
    return pl.pallas_call(
        decay_kernel,
        in_specs=[SMEM, ANY, WHOLE, WHOLE, WHOLE],
        out_specs=[WHOLE] * 9,
        out_shape=[
            jax.ShapeDtypeStruct(square, BF16),
            jax.ShapeDtypeStruct(square, BF16),
            jax.ShapeDtypeStruct(square, BF16),
            jax.ShapeDtypeStruct(square, BF16),
            jax.ShapeDtypeStruct((pieces, ROW_COUNT, PIECE), F32),
            jax.ShapeDtypeStruct(square, F32),
            jax.ShapeDtypeStruct(square, BF16),
            jax.ShapeDtypeStruct((pieces, 8, WIDTH), F32),
            jax.ShapeDtypeStruct((HEADS, PIECE), F32),
        ],
        scratch_shapes=[
            pltpu.VMEM((pieces, HEADS, PIECE), BF16),
            pltpu.SemaphoreType.DMA((3, pieces)),
        ],
        compiler_params=params(),
        name="decays",
    )(src, small, seg, bias, alog)


def spread(kinds):
    shape = (kinds, kinds * 2 * HEADS, WIDTH)
    rows = lax.broadcasted_iota(jnp.int32, shape, 1)
    kind = lax.broadcasted_iota(jnp.int32, shape, 0)
    head = lax.broadcasted_iota(jnp.int32, shape, 2) // HEAD_DIM
    return ((rows // (2 * HEADS) == kind) & (rows % HEADS == head)).astype(BF16)


def over_first(left, right):
    return lax.dot_general(left, right, (((0,), (0,)), ((), ())), preferred_element_type=F32)


def dot(left, right):
    return jnp.dot(left, right, preferred_element_type=F32)


def two_heads(weights, values):
    lane = lax.broadcasted_iota(jnp.int32, values.shape, 1)
    zero = jnp.zeros_like(values)
    stacked = jnp.concatenate(
        [jnp.where(lane < HEAD_DIM, values, zero), jnp.where(lane < HEAD_DIM, zero, values)], axis=0
    )
    return dot(jnp.concatenate(weights, axis=1), stacked)


def local_piece(forward, first, r, left, turned, values_of, rows_ref, cols_ref, scale_ref, ends_ref, spread_ref, skip_ref, out_ref, state):
    scales, by_token = scale_ref[r], cols_ref[r]
    row = lax.broadcasted_iota(jnp.int32, (PIECE, PIECE), 0)
    col = lax.broadcasted_iota(jnp.int32, (PIECE, PIECE), 1)
    same = by_token[:, SEG : SEG + 1] == rows_ref[r, SEG : SEG + 1, :]
    reach = (col <= row) if forward else (col >= row)
    scores = jnp.where(reach & same, dot(left, turned), 0.0)
    into, out_of = (ENTRY, STEP_EXIT) if forward else (STEP_EXIT, ENTRY)
    for group in range(out_ref.shape[2] // GROUP):
        cols = slice(group * GROUP, (group + 1) * GROUP)
        values = values_of(group)
        near = []
        for pair in range(2):
            weights = []
            for head in (first + 4 * group + 2 * pair, first + 4 * group + 2 * pair + 1):
                if forward:
                    gap = by_token[:, head : head + 1] - rows_ref[r, HEADS + head : HEADS + head + 1, :]
                else:
                    gap = rows_ref[r, head : head + 1, :] - by_token[:, head : head + 1]
                weights.append((scores * jnp.exp2(jnp.minimum(gap, 8.0))).astype(BF16))
            part = two_heads(weights, values[:, pair * 128 : (pair + 1) * 128])
            if not forward:
                at = 2 * HEADS + head
                lane = lax.broadcasted_iota(jnp.int32, part.shape, 1)
                part *= jnp.where(lane < HEAD_DIM, by_token[:, at - 1 : at], by_token[:, at : at + 1])
            near.append(part)
        wide = values.astype(F32)
        held = state[:, cols]
        out = jnp.concatenate(near, axis=1) + skip_ref[:, cols] * wide
        out += dot(scales, spread_ref[into, :, cols]) * dot(left, held.astype(BF16))
        out_ref[r, :, cols] = out
        scaled = (wide * dot(scales, spread_ref[out_of, :, cols])).astype(BF16)
        state[:, cols] = ends_ref[r, 0:1, cols] * held + dot(turned, scaled)


def forward_kernel(half, c_ref, bt_ref, *rest):
    x_refs, (after_ref, out_ref, state) = rest[:RUN], rest[-3:]

    @pl.when(pl.program_id(0) == 0)
    def _():
        state[...] = jnp.zeros_like(state)

    for r in range(RUN):

        def values_of(group):
            return x_refs[r][0, :, group * GROUP : (group + 1) * GROUP]

        local_piece(
            True, half * HEADS // 2, r, c_ref[r], bt_ref[r], values_of, *rest[RUN:-3], out_ref, state
        )


def backward_kernel(b_ref, ct_ref, cot_ref, *rest):
    after_ref, out_ref, state = rest[-3:]

    @pl.when(pl.program_id(0) == 0)
    def _():
        state[...] = jnp.zeros_like(state)

    for r in reversed(range(RUN)):

        def values_of(group):
            return cot_ref[r * PIECE : (r + 1) * PIECE, group * GROUP : (group + 1) * GROUP]

        local_piece(False, 0, r, b_ref[r], ct_ref[r], values_of, *rest[:-3], out_ref, state)


def local_call(kernel, place, width, half, firsts, specs, values, src, local, after, name):
    rows, cols, scales, ends, spread_four, skip = local
    pieces = rows.shape[0]
    at = lambda k, src: (place(k), 0, 0)
    square = pl.BlockSpec((RUN, PIECE, PIECE), at)
    return pl.pallas_call(
        skip_src(kernel),
        grid_spec=pltpu.PrefetchScalarGridSpec(
            num_scalar_prefetch=1,
            grid=(pieces // RUN,),
            in_specs=[
                square,
                square,
                *specs,
                pl.BlockSpec((RUN, ROW_COUNT, PIECE), at),
                square,
                square,
                pl.BlockSpec((RUN, 8, width), lambda k, src: (place(k), 0, half)),
                pl.BlockSpec(spread_four.shape[:2] + (width,), lambda k, src: (0, 0, half)),
                pl.BlockSpec((1, width), lambda k, src: (0, half)),
                ANY,
            ],
            out_specs=pl.BlockSpec((RUN, PIECE, width), at),
            scratch_shapes=[pltpu.VMEM((STATE, width), F32)],
        ),
        out_shape=jax.ShapeDtypeStruct((pieces, PIECE, width), F32),
        compiler_params=params(),
        name=name,
    )(src, *firsts, *values, rows, cols, scales, ends, spread_four, skip, after)


def skip_src(kernel):
    return lambda src_ref, *refs: kernel(*refs)


def forward_local(half, src, c, bt, x_slots, local, after):
    specs = [
        pl.BlockSpec((1, PIECE, HALF), lambda k, src, r=r: (src[0, RUN * k + r], 0, 0))
        for r in range(RUN)
    ]
    kernel = partial(forward_kernel, half)
    values = [x_slots[half]] * RUN
    return local_call(
        kernel, lambda k: k, HALF, half, [c, bt], specs, values, src, local, after, "forward_local"
    )


def backward_local(src, b, ct, cotangent, local, after):
    last = b.shape[0] // RUN - 1
    specs = [pl.BlockSpec((RUN * PIECE, WIDTH), lambda k, src: (last - k, 0))]
    place = lambda k: last - k
    return local_call(
        backward_kernel, place, WIDTH, 0, [b, ct], specs, [cotangent], src, local, after, "backward_local"
    )


def leaving_state(kind, keys_ref, v_all, scale_ref, spread_ref, store):
    pieces = scale_ref.shape[0]
    for group in range(WIDTH // GROUP):
        cols = slice(group * GROUP, (group + 1) * GROUP)
        state = None
        for k in range(0, pieces, 4):
            scales = scale_ref[k : k + 4].reshape(4 * PIECE, PIECE)
            scale = dot(scales, spread_ref[kind, :, cols])
            values = v_all[k : k + 4, :, cols].reshape(4 * PIECE, GROUP)
            scaled = (values.astype(F32) * scale).astype(BF16)
            for r in range(4):
                update = dot(keys_ref[k + r], scaled[r * PIECE : (r + 1) * PIECE])
                state = update if state is None else state + update
        store(cols, state.astype(BF16))


def leaving_gradient_kernel(cot_ref, keys_ref, scale_ref, spread_ref, out_ref):
    def store(cols, value):
        out_ref[:, cols] = value

    leaving_state(BEFORE, keys_ref, cot_ref, scale_ref, spread_ref, store)


def leaving_gradient(keys, cotangent, scales, spread_four):
    pieces = scales.shape[0]
    return pl.pallas_call(
        leaving_gradient_kernel,
        out_shape=jax.ShapeDtypeStruct((STATE, WIDTH), BF16),
        compiler_params=params(),
        name="leaving_gradient",
    )(cotangent.reshape(pieces, PIECE, WIDTH), keys, scales, spread_four)


def leaving_kernel(src_ref, xa_ref, xb_ref, keys_ref, scale_ref, spread_ref, g_ref, total_ref, out_ref, v_all, sems):
    ins = []
    for k in range(scale_ref.shape[0]):
        for half, ref in enumerate((xa_ref, xb_ref)):
            to = v_all.at[k, :, pl.ds(half * HALF, HALF)]
            ins.append(pltpu.make_async_copy(ref.at[src_ref[0, k]], to, sems.at[half, k]))
    for copy in ins:
        copy.start()
    high, low = split_two(total_ref[...])
    lane = lax.broadcasted_iota(jnp.int32, high.shape, 1)
    decay = jnp.where(lane == 0, high, jnp.where(lane == 1, low, jnp.zeros_like(low)))
    for part in range(OWNERS):
        out_ref[part, :, WIDTH:] = decay
        if part >= 8:
            out_ref[part, :, 0:WIDTH] = g_ref[part % 8 * 16 : part % 8 * 16 + 16, :]
    for copy in ins:
        copy.wait()

    def store(cols, value):
        for part in range(8):
            out_ref[part, :, cols] = value[part * 16 : part * 16 + 16]

    leaving_state(AFTER, keys_ref, v_all, scale_ref, spread_ref, store)


def leaving(src, x_slots, keys, scales, spread_four, g_state, total):
    pieces = scales.shape[0]
    return pl.pallas_call(
        leaving_kernel,
        in_specs=[SMEM, ANY, ANY] + [WHOLE] * 5,
        out_specs=WHOLE,
        out_shape=jax.ShapeDtypeStruct((OWNERS, 16, WIDTH + EXTRA), BF16),
        scratch_shapes=[
            pltpu.VMEM((pieces, PIECE, WIDTH), BF16),
            pltpu.SemaphoreType.DMA((2, pieces)),
        ],
        compiler_params=params(),
        name="leaving",
    )(src, *x_slots, keys, scales, spread_four, g_state, total)


def scan_kernel(back_ref, part_ref, after_ref, out_ref):
    back = back_ref[0]
    head = lax.broadcasted_iota(jnp.int32, (HEADS, WIDTH), 0)
    lane = lax.broadcasted_iota(jnp.int32, (HEADS, WIDTH), 1)
    spread_one = (lane // HEAD_DIM == head).astype(BF16)
    held = jnp.zeros((HEADS, WIDTH), F32)
    for k in range(OWNERS):
        at = jnp.where(back == 1, OWNERS - 1 - k, k)
        out_ref[at] = held.astype(BF16)
        decay = over_first(part_ref[at, :, WIDTH:], spread_one)
        held = (decay[0:1] + decay[1:2]) * held + part_ref[at, :, 0:WIDTH].astype(F32)


def scan_owners(back, parts, after):
    return pl.pallas_call(
        scan_kernel,
        in_specs=[SMEM, WHOLE, ANY],
        out_specs=WHOLE,
        out_shape=jax.ShapeDtypeStruct((OWNERS, 16, WIDTH), BF16),
        compiler_params=params(),
        name="scan_owners",
    )(back, parts, after)


def finish_kernel(b_ref, c_ref, ya_ref, yb_ref, g_ref, enter_ref, scale_ref, spread_ref, y_out, g_out):
    rows = 2 * PIECE
    b, c, scales = b_ref[...].reshape(rows, STATE), c_ref[...].reshape(rows, STATE), scale_ref[...].reshape(rows, PIECE)
    for group in range(WIDTH // GROUP):
        cols = slice(group * GROUP, (group + 1) * GROUP)
        y_off = dot(scales, spread_ref[BEFORE, :, cols]) * dot(c, enter_ref[0:STATE, cols])
        start = group % 2 * GROUP
        y = (ya_ref if group < 2 else yb_ref)[:, :, start : start + GROUP].reshape(rows, GROUP)
        y_out[:, cols] = (y + y_off).astype(BF16)
        g_off = dot(scales, spread_ref[AFTER, :, cols]) * dot(b, enter_ref[STATE:, cols])
        g_out[:, cols] = (g_ref[:, :, cols].reshape(rows, GROUP) + g_off).astype(BF16)


def finish(b, c, y_a, y_b, g_local, enter, scales, spread_four):
    pieces = scales.shape[0]
    out = jax.ShapeDtypeStruct((pieces * PIECE, WIDTH), BF16)
    square = pl.BlockSpec((2, PIECE, PIECE), lambda k: (k, 0, 0))
    half = pl.BlockSpec((2, PIECE, HALF), lambda k: (k, 0, 0))
    wide = pl.BlockSpec((2, PIECE, WIDTH), lambda k: (k, 0, 0))
    return pl.pallas_call(
        finish_kernel,
        grid=(pieces // 2,),
        in_specs=[
            square,
            square,
            half,
            half,
            wide,
            pl.BlockSpec((2 * STATE, WIDTH), lambda k: (0, 0)),
            square,
            pl.BlockSpec(spread_four.shape, lambda k: (0, 0, 0)),
        ],
        out_specs=[pl.BlockSpec((2 * PIECE, WIDTH), lambda k: (k, 0))] * 2,
        out_shape=[out, out],
        compiler_params=params(),
        name="finish",
    )(b, c, y_a, y_b, g_local, enter, scales, spread_four)


def ranks(dest):
    owner = dest // OWNERS
    here = lax.broadcasted_iota(jnp.int32, (OWNERS, OWNERS), 0)
    other = lax.broadcasted_iota(jnp.int32, (OWNERS, OWNERS), 1)
    same = (owner[..., None, :] == owner[..., :, None]) & (other < here)
    return jnp.sum(same.astype(jnp.int32), axis=-1)


def to_owners(value):
    return lax.all_to_all(value, "ctx", split_axis=0, concat_axis=0, tiled=True)


def body(
    x_rows, b_rows, c_rows, dt_rows, destination, doc_start, a_log, dt_bias, d_skip, cotangent
):
    head = lax.axis_index("head")
    me = lax.axis_index("ctx")
    dest_heads = jnp.stack([partner(head, s) for s in SHIFTS]).astype(jnp.int32)
    origin = jnp.stack([source(head, s) for s in SHIFTS] + [head]).astype(jnp.int32)
    send_slot = destination // OWNERS * 2 + ranks(destination)

    small = gather_small(b_rows, c_rows, dt_rows)
    small = lax.all_to_all(small, "head", split_axis=0, concat_axis=0, tiled=True)
    small = small.reshape(OWNERS, SMALL_ROWS, STATE)
    small = to_owners(pack_small(send_slot, destination % OWNERS, small))
    src = find_source(small)
    pieces = destination.shape[0]
    seg = jnp.cumsum(doc_start.reshape(pieces, PIECE), axis=1).astype(F32)[:, None, :]
    b, c, bt, ct, rows, cols, scales, ends, total = decays(
        src, small, seg, dt_bias.reshape(HEADS, 1), a_log.reshape(HEADS, 1)
    )
    skip = jnp.repeat(d_skip, HEAD_DIM).reshape(1, WIDTH)
    spread_four = spread(4)
    local = (rows, cols, scales, ends, spread_four, skip)

    x_slots = []
    after = []
    for half in range(2):
        arrived = []
        for shift, piece in zip(SHIFTS, cut(half, dest_heads, x_rows)):
            pairs = [(h, partner(h, shift)) for h in range(PEERS)]
            arrived.append(lax.ppermute(piece, "head", pairs))
        x_slots.append(to_owners(pack_x(half, send_slot, origin, x_rows, arrived, after)))
        if half == 0:
            g_state = leaving_gradient(ct, cotangent, scales, spread_four)
            g_local = backward_local(src, b, ct, cotangent, local, g_state)
            after = [g_local]

    parts = leaving(src, x_slots, bt, scales, spread_four, g_state, total)
    y_a = forward_local(0, src, c, bt, x_slots, local, parts)
    back = (me >= OWNERS // 2).astype(jnp.int32).reshape(1)
    enter = scan_owners(back, to_owners(parts), y_a)
    y_b = forward_local(1, src, c, bt, x_slots, local, enter)
    enter = to_owners(enter).reshape(2 * STATE, WIDTH)
    return tuple(finish(b, c, y_a, y_b, g_local, enter, scales, spread_four))


def solution(mesh):
    in_specs = (
        P(("ctx", "head"), None),
        P(("ctx", "head"), None),
        P(("ctx", "head"), None),
        P(("ctx", "head"), None),
        P("ctx"),
        P("ctx"),
        P("head"),
        P("head"),
        P("head"),
        P("ctx", "head"),
    )
    out_specs = (P("ctx", "head"), P("ctx", "head"))
    return jax.shard_map(body, mesh=mesh, in_specs=in_specs, out_specs=out_specs, check_vma=False)
```

time: 284 us -> 256 us (0.901)
  blocking collectives: 0 us -> 63.4 us
  waiting for transfers between devices: 84.3 us -> 38.3 us
  starting transfers between devices: 65.3 us -> 45.6 us
  local copies, waits for them, and re-layouts: 22 us -> 8.94 us
  Pallas kernels: 107 us -> 94 us
    all_to_all x0 -> x1, blocking collectives: none -> 63.4 us  [to_owners(): return lax.all_to_all(value, 'ctx', split_axis=0, concat_axis=0, tiled=True)]
    all_to_all x5 -> x4, waiting for transfers between devices: 31.1 us -> 0.01 us  [to_owners(): return lax.all_to_all(value, 'ctx', split_axis=0, concat_axis=0, tiled=True)]
    all_to_all x5 -> x4, starting transfers between devices: 48.8 us -> 28.1 us  [to_owners(): return lax.all_to_all(value, 'ctx', split_axis=0, concat_axis=0, tiled=True)]
    pallas_call x10, Pallas kernels: 97 us -> 80 us  [the longest x3 37.3 us: local_call(): pl.pallas_call(skip_src(kernel), grid_spec=pltpu.PrefetchScalarGridSpec(n...]
    unnamed x52 -> x40, local copies, waits for them, and re-layouts: 21.5 us -> 5.64 us
    ppermute x14, waiting for transfers between devices: 38.8 us -> 24.9 us  [body(): arrived.append(lax.ppermute(piece, 'head', pairs))]
    pallas_call x2, Pallas kernels: 2.46 us -> 6.05 us  [cut(): pl.pallas_call(partial(cut_kernel, half), in_specs=[SMEM, ANY], out_specs...]
  transfers between devices with their start and end apart: 20 -> 19, of which waited for: 14 -> 7; matrix products, arithmetic and copies ran while one was open for 1% -> 3% of each run, Pallas kernels for 28% -> 25%
where the time goes in v2:
time: 256 us; the launch traced here: 255 us
  Pallas kernels  94 us (37%)
  blocking collectives  63.4 us (25%)
  starting transfers between devices  45.6 us (18%)
  waiting for transfers between devices  38.3 us (15%)
  local copies, waits for them, and re-layouts  8.94 us (3%)
  other arithmetic  3.42 us (1%)
    all_to_all x1, blocking collectives, to_owners(): return lax.all_to_all(value, 'ctx', split_axis=0, concat_axis=0, tiled=True)  63.4 us
    pallas_call x3, Pallas kernels, local_call(): pl.pallas_call(skip_src(kernel), grid_spec=pltpu.PrefetchScalarGridSpec(n...  37.3 us
    all_to_all x4, starting transfers between devices, to_owners(): return lax.all_to_all(value, 'ctx', split_axis=0, concat_axis=0, tiled=True)  28.1 us
    ppermute x14, waiting for transfers between devices, body(): arrived.append(lax.ppermute(piece, 'head', pairs))  24.9 us
    pallas_call x1, Pallas kernels, finish(): pl.pallas_call(finish_kernel, grid=(pieces // 2,), in_specs=[square, squa...  13.8 us
    all_to_all x1, waiting for transfers between devices, body(): lax.all_to_all(small, 'head', split_axis=0, concat_axis=0, tiled=True)  13.4 us
    ppermute x14, starting transfers between devices, body(): arrived.append(lax.ppermute(piece, 'head', pairs))  13 us
    pallas_call x1, Pallas kernels, leaving(): pl.pallas_call(leaving_kernel, in_specs=[SMEM, ANY, ANY] + [WHOLE] * 5, o...  7.47 us
  transfers between devices with their start and end apart: 19, of which 7 were waited for; matrix products, arithmetic and copies ran while one was open for 3% of the time, Pallas kernels for 25%

profile of v2, /device:TPU:98, one launch (start us, length us, event | category | flops | bytes accessed | tf_op | source)
XLA Modules:
  0.0 254.6 jit_solution(14015678523522810260)
XLA Ops:
  3.2 4.5 %all-to-all-start = ((bf16[8,2,272,128]{3,2,1,0:T(8,128)(2,1)}), bf16[8,2,272,128]{3,2,1,0:T(8,128)(2,1)S(1)}, u32[]{:S(2)}, u32[]{:S(2)}) async-start(bf16[8,2,272,128]{3,2,1,0:T(8,128)(2,1)} %gather_small.1), calls=%async_computation | async-start | bytes 2228224 | tf_op jit(solution)/shard_map/all_to_all | solution.py:649
  8.9 13.4 %all-to-all-done = bf16[8,2,272,128]{3,2,1,0:T(8,128)(2,1)S(1)} async-done(((bf16[8,2,272,128]{3,2,1,0:T(8,128)(2,1)}), bf16[8,2,272,128]{3,2,1,0:T(8,128)(2,1)S(1)}, u32[]{:S(2)}, u32[]{:S(2)}) %all-to-all-start) | async-done | bytes 1114144 | tf_op jit(solution)/shard_map/all_to_all | solution.py:649
  25.7 7.5 %all-to-all-start.1 = ((bf16[32,288,128]{2,1,0:T(8,128)(2,1)}), bf16[32,288,128]{2,1,0:T(8,128)(2,1)S(1)}, u32[]{:S(2)}, u32[]{:S(2)}) async-start(bf16[32,288,128]{2,1,0:T(8,128)(2,1)} %pack_small.1), calls=%async_computation.1 | async-start | bytes 4718592 | tf_op jit(solution)/shard_map/all_to_all | solution.py:636
  33.8 3.0 %cut.2 = (bf16[256,512]{1,0:T(8,128)(2,1)}, bf16[256,512]{1,0:T(8,128)(2,1)}, bf16[256,512]{1,0:T(8,128)(2,1)}, bf16[256,512]{1,0:T(8,128)(2,1)}, bf16[256,512]{...) custom-call(s32[7]{0:T(128)} %stack.49.dest_ref, bf16[256,8192]{1,0:T(8,128)(2,1)} %x_ref.7), custom_call_target="tpu_custom_call" | custom-call | tf_op jit(solution)/shard_map/cut/pallas_call | solution.py:177
  42.7 3.6 %collective-permute-done.rest_0_ = bf16[256,512]{1,0:T(8,128)(2,1)S(1)} collective-permute-done((bf16[256,512]{1,0:T(8,128)(2,1)}, bf16[256,512]{1,0:T(8,128)(2,1)S(1)}, u32[]{:S(2)}, u32[]{:S(2)}) %collective-permute-start) | collective-permute-done | bytes 262176 | tf_op jit(solution)/shard_map/ppermute | solution.py:668
  46.3 3.3 %collective-permute-done.1.rest_1_ = bf16[256,512]{1,0:T(8,128)(2,1)S(1)} collective-permute-done((bf16[256,512]{1,0:T(8,128)(2,1)}, bf16[256,512]{1,0:T(8,128)(2,1)S(1)}, u32[]{:S(2)}, u32[]{:S(2)}) %collective-permute-start.1) | collective-permute-done | bytes 262176 | tf_op jit(solution)/shard_map/ppermute | solution.py:668
  50.2 10.8 %collective-permute-done.2.rest_2_ = bf16[256,512]{1,0:T(8,128)(2,1)S(1)} collective-permute-done((bf16[256,512]{1,0:T(8,128)(2,1)}, bf16[256,512]{1,0:T(8,128)(2,1)S(1)}, u32[]{:S(2)}, u32[]{:S(2)}) %collective-permute-start.2) | collective-permute-done | bytes 262176 | tf_op jit(solution)/shard_map/ppermute | solution.py:668
  62.0 3.2 %pack_x.2 = bf16[32,128,512]{2,1,0:T(8,128)(2,1)} custom-call(s32[16]{0:T(128)} %multiply_add_fusion.slot_ref, s32[8]{0:T(128)} %stack.47.from_ref, bf16[256,8192]{1,0:T(8,128)(2,1)} %x_ref.7, bf16[256,512]{1,0:T(8,128)(2,1)} %copy-done.11, bf16[256,512]{1,0:T(8,128)(2,1)} %copy-done.12, bf16[256,512]{1,0:T(8,128)(2,1)} %copy-done.13, ...), custom_call_target="tpu_custom_call" | custom-call | tf_op jit(solution)/shard_map/pack_x/pallas_call | solution.py:214
  66.7 7.2 %all-to-all-start.2 = ((bf16[32,128,512]{2,1,0:T(8,128)(2,1)}), bf16[32,128,512]{2,1,0:T(8,128)(2,1)}, u32[]{:S(2)}, u32[]{:S(2)}) async-start(bf16[32,128,512]{2,1,0:T(8,128)(2,1)} %pack_x.2), calls=%async_computation.2 | async-start | bytes 8388608 | tf_op jit(solution)/shard_map/all_to_all | solution.py:636
  73.9 3.1 %cut.3 = (bf16[256,512]{1,0:T(8,128)(2,1)}, bf16[256,512]{1,0:T(8,128)(2,1)}, bf16[256,512]{1,0:T(8,128)(2,1)}, bf16[256,512]{1,0:T(8,128)(2,1)}, bf16[256,512]{...) custom-call(s32[7]{0:T(128)} %stack.49.dest_ref, bf16[256,8192]{1,0:T(8,128)(2,1)} %x_ref.7), custom_call_target="tpu_custom_call" | custom-call | tf_op jit(solution)/shard_map/cut/pallas_call | solution.py:177
  83.6 3.1 %collective-permute-done.7.rest_0_ = bf16[256,512]{1,0:T(8,128)(2,1)S(1)} collective-permute-done((bf16[256,512]{1,0:T(8,128)(2,1)}, bf16[256,512]{1,0:T(8,128)(2,1)S(1)}, u32[]{:S(2)}, u32[]{:S(2)}) %collective-permute-start.7) | collective-permute-done | bytes 262176 | tf_op jit(solution)/shard_map/ppermute | solution.py:668
  87.2 3.1 %collective-permute-done.8.rest_1_ = bf16[256,512]{1,0:T(8,128)(2,1)S(1)} collective-permute-done((bf16[256,512]{1,0:T(8,128)(2,1)}, bf16[256,512]{1,0:T(8,128)(2,1)S(1)}, u32[]{:S(2)}, u32[]{:S(2)}) %collective-permute-start.8) | collective-permute-done | bytes 262176 | tf_op jit(solution)/shard_map/ppermute | solution.py:668
  96.2 7.4 %decays.1 = (bf16[16,128,128]{2,1,0:T(8,128)(2,1)}, bf16[16,128,128]{2,1,0:T(8,128)(2,1)}, bf16[16,128,128]{2,1,0:T(8,128)(2,1)}, bf16[16,128,128]{2,1,0:T(8,128...) custom-call(s32[1,128]{1,0:T(1,128)} %find_source.1.src_ref, ...), custom_call_target="tpu_custom_call" | custom-call | tf_op jit(solution)/shard_map/decays/pallas_call | solution.py:318
  103.6 6.0 %leaving_gradient.1.refs_9_.g_ref = bf16[128,1024]{1,0:T(8,128)(2,1)} custom-call(bf16[16,128,1024]{2,1,0:T(8,128)(2,1)} %bitcast.17, bf16[16,128,128]{2,1,0:T(8,128)(2,1)} %get-tuple-element.46.keys_ref.refs_1_, bf16[16,128,128]{2,1,0:T(8,128)(2,1)} %get-tuple-element.37.scale_ref.refs_5_.refs_8_, bf16[4,128,1024]{2,1,0:T(8,128)(2,1)} %fusion.1.spread_ref.refs_7_.refs_10_), custom_call_target="tpu_custom_call" | custom-call | tf_op jit(solution)/shard_map/leaving_gradient/pallas_call | solution.py:515
  109.7 16.2 %backward_local.1.rest_7_.g_ref = f32[16,128,1024]{2,1,0:T(8,128)} custom-call(s32[1,128]{1,0:T(1,128)} %find_source.1.src_ref, bf16[16,128,128]{2,1,0:T(8,128)(2,1)} %get-tuple-element.25.refs_0_.b_ref, bf16[16,128,128]{2,1,0:T(8,128)(2,1)} %get-tuple-element.46.keys_ref.refs_1_, bf16[2048,1024]{1,0:T(8,128)(2,1)} %refs_2_.1, ...), custom_call_target="tpu_custom_call" | custom-call | tf_op jit(solution)/shard_map/backward_local/pallas_call | solution.py:439
  127.5 3.2 %pack_x.3 = bf16[32,128,512]{2,1,0:T(8,128)(2,1)} custom-call(s32[16]{0:T(128)} %multiply_add_fusion.slot_ref, s32[8]{0:T(128)} %stack.47.from_ref, bf16[256,8192]{1,0:T(8,128)(2,1)} %x_ref.7, bf16[256,512]{1,0:T(8,128)(2,1)} %copy-done.4, bf16[256,512]{1,0:T(8,128)(2,1)} %copy-done.5, bf16[256,512]{1,0:T(8,128)(2,1)} %copy-done.6, ...), custom_call_target="tpu_custom_call" | custom-call | tf_op jit(solution)/shard_map/pack_x/pallas_call | solution.py:214
  130.8 63.4 %all_to_all.30.xb_ref.refs_2_.refs_3_.refs_4_.refs_5_ = bf16[32,128,512]{2,1,0:T(8,128)(2,1)} all-to-all(bf16[32,128,512]{2,1,0:T(8,128)(2,1)} %pack_x.3), channel_id=1, replica_groups=mesh['ctx'=16,'head'=8] {'ctx'}, dimensions={0} | all-to-all | bytes 8388608 | tf_op jit(solution)/shard_map/all_to_all | solution.py:636
  194.2 7.5 %leaving.1.refs_12_ = bf16[16,16,1152]{2,1,0:T(8,128)(2,1)} custom-call(s32[1,128]{1,0:T(1,128)} %find_source.1.src_ref, bf16[32,128,512]{2,1,0:T(8,128)(2,1)} %all-to-all-done.2.xa_ref.refs_2_.refs_3_.refs_4_.refs_5_, bf16[32,128,512]{2,1,0:T(8,128)(2,1)} %all_to_all.30.xb_ref.refs_2_.refs_3_.refs_4_.refs_5_, ...), custom_call_target="tpu_custom_call" | custom-call | tf_op jit(solution)/shard_map/leaving/pallas_call | solution.py:550
  201.7 6.2 %all-to-all-start.4 = ((bf16[16,16,1152]{2,1,0:T(8,128)(2,1)}), bf16[16,16,1152]{2,1,0:T(8,128)(2,1)S(1)}, u32[]{:S(2)}, u32[]{:S(2)}) async-start(bf16[16,16,1152]{2,1,0:T(8,128)(2,1)} %leaving.1.refs_12_), calls=%async_computation.4 | async-start | bytes 1179648 | tf_op jit(solution)/shard_map/all_to_all | solution.py:636
  207.8 10.5 %forward_local.2.after_ref.ya_ref = f32[16,128,512]{2,1,0:T(8,128)} custom-call(s32[1,128]{1,0:T(1,128)} %find_source.1.src_ref, bf16[16,128,128]{2,1,0:T(8,128)(2,1)} %get-tuple-element.26.refs_0_.c_ref, bf16[16,128,128]{2,1,0:T(8,128)(2,1)} %get-tuple-element.27.keys_ref.refs_1_, ...), custom_call_target="tpu_custom_call" | custom-call | tf_op jit(solution)/shard_map/forward_local/pallas_call | solution.py:439
  219.2 3.0 %scan_owners.1.refs_12_ = bf16[16,16,1024]{2,1,0:T(8,128)(2,1)} custom-call(s32[1]{0:T(128)} %bitcast.15.back_ref, bf16[16,16,1152]{2,1,0:T(8,128)(2,1)} %copy-done.2, f32[16,128,512]{2,1,0:T(8,128)} %forward_local.2.after_ref.ya_ref), custom_call_target="tpu_custom_call" | custom-call | tf_op jit(solution)/shard_map/scan_owners/pallas_call | solution.py:578
  222.2 7.2 %all-to-all-start.5 = ((bf16[16,16,1024]{2,1,0:T(8,128)(2,1)}), bf16[16,16,1024]{2,1,0:T(8,128)(2,1)S(1)}, u32[]{:S(2)}, u32[]{:S(2)}) async-start(bf16[16,16,1024]{2,1,0:T(8,128)(2,1)} %scan_owners.1.refs_12_), calls=%async_computation.5 | async-start | bytes 1048576 | tf_op jit(solution)/shard_map/all_to_all | solution.py:636
  229.4 10.6 %forward_local.3.yb_ref = f32[16,128,512]{2,1,0:T(8,128)} custom-call(s32[1,128]{1,0:T(1,128)} %find_source.1.src_ref, bf16[16,128,128]{2,1,0:T(8,128)(2,1)} %get-tuple-element.26.refs_0_.c_ref, bf16[16,128,128]{2,1,0:T(8,128)(2,1)} %get-tuple-element.27.keys_ref.refs_1_, bf16[32,128,512]{2,1,0:T(8,128)(2,1)} %all_to_all.30.xb_ref.refs_2_.refs_3_.refs_4_.refs_5_, ...), custom_call_target="tpu_custom_call" | custom-call | tf_op jit(solution)/shard_map/forward_local/pallas_call | solution.py:439
  240.8 13.8 %finish.1 = (bf16[2048,1024]{1,0:T(8,128)(2,1)}, bf16[2048,1024]{1,0:T(8,128)(2,1)}) custom-call(bf16[16,128,128]{2,1,0:T(8,128)(2,1)} %get-tuple-element.25.refs_0_.b_ref, bf16[16,128,128]{2,1,0:T(8,128)(2,1)} %get-tuple-element.26.refs_0_.c_ref, f32[16,128,512]{2,1,0:T(8,128)} %forward_local.2.after_ref.ya_ref, f32[16,128,512]{2,1,0:T(8,128)} %forward_local.3.yb_ref, ...), custom_call_target="tpu_custom_call" | custom-call | tf_op jit(solution)/shard_map/finish/pallas_call | solution.py:607
  (87 shorter events, 32.8 us)
Async XLA Ops:
  3.2 19.1 %all-to-all-start = ((bf16[8,2,272,128]{3,2,1,0:T(8,128)(2,1)}), bf16[8,2,272,128]{3,2,1,0:T(8,128)(2,1)S(1)}, u32[]{:S(2)}, u32[]{:S(2)}) async-start(bf16[8,2,272,128]{3,2,1,0:T(8,128)(2,1)} %gather_small.1), calls=%async_computation | async-start | bytes 2228224 | tf_op jit(solution)/shard_map/all_to_all | solution.py:649
  25.7 39.5 %all-to-all-start.1 = ((bf16[32,288,128]{2,1,0:T(8,128)(2,1)}), bf16[32,288,128]{2,1,0:T(8,128)(2,1)S(1)}, u32[]{:S(2)}, u32[]{:S(2)}) async-start(bf16[32,288,128]{2,1,0:T(8,128)(2,1)} %pack_small.1), calls=%async_computation.1 | async-start | bytes 4718592 | tf_op jit(solution)/shard_map/all_to_all | solution.py:636
  36.8 9.5 %collective-permute-start = (bf16[256,512]{1,0:T(8,128)(2,1)}, bf16[256,512]{1,0:T(8,128)(2,1)S(1)}, u32[]{:S(2)}, u32[]{:S(2)}) collective-permute-start(bf16[256,512]{1,0:T(8,128)(2,1)} %get-tuple-element.28), channel_id=1, source_target_pairs={{0,2},{1,3},{2,4},{3,5},{4,6},{5,7},{6,0},{7,1},{8,10},{9,11},{10,... | collective-permute-start | bytes 786440 | tf_op jit(solution)/shard_map/ppermute | solution.py:668
  39.0 10.7 %collective-permute-start.1 = (bf16[256,512]{1,0:T(8,128)(2,1)}, bf16[256,512]{1,0:T(8,128)(2,1)S(1)}, u32[]{:S(2)}, u32[]{:S(2)}) collective-permute-start(bf16[256,512]{1,0:T(8,128)(2,1)} %get-tuple-element.29), channel_id=1, source_target_pairs={{0,6},{1,7},{2,0},{3,1},{4,2},{5,3},{6,4},{7,5},{8,14},{9,15},{10,... | collective-permute-start | bytes 786440 | tf_op jit(solution)/shard_map/ppermute | solution.py:668
  39.0 22.0 %collective-permute-start.2 = (bf16[256,512]{1,0:T(8,128)(2,1)}, bf16[256,512]{1,0:T(8,128)(2,1)S(1)}, u32[]{:S(2)}, u32[]{:S(2)}) collective-permute-start(bf16[256,512]{1,0:T(8,128)(2,1)} %get-tuple-element.30), channel_id=1, source_target_pairs={{0,3},{1,2},{2,5},{3,4},{4,7},{5,6},{6,1},{7,0},{8,11},{9,10},{10,... | collective-permute-start | bytes 786440 | tf_op jit(solution)/shard_map/ppermute | solution.py:668
  40.3 20.7 %collective-permute-start.3 = (bf16[256,512]{1,0:T(8,128)(2,1)}, bf16[256,512]{1,0:T(8,128)(2,1)S(1)}, u32[]{:S(2)}, u32[]{:S(2)}) collective-permute-start(bf16[256,512]{1,0:T(8,128)(2,1)} %get-tuple-element.31), channel_id=1, source_target_pairs={{0,7},{1,6},{2,1},{3,0},{4,3},{5,2},{6,5},{7,4},{8,15},{9,14},{10,... | collective-permute-start | bytes 786440 | tf_op jit(solution)/shard_map/ppermute | solution.py:668
  40.7 20.3 %collective-permute-start.4 = (bf16[256,512]{1,0:T(8,128)(2,1)}, bf16[256,512]{1,0:T(8,128)(2,1)}, u32[]{:S(2)}, u32[]{:S(2)}) collective-permute-start(bf16[256,512]{1,0:T(8,128)(2,1)} %get-tuple-element.32), channel_id=1, source_target_pairs={{0,4},{1,5},{2,6},{3,7},{4,0},{5,1},{6,2},{7,3},{8,12},{9,13},{10,... | collective-permute-start | bytes 786440 | tf_op jit(solution)/shard_map/ppermute | solution.py:668
  46.3 15.6 %collective-permute-start.5 = (bf16[256,512]{1,0:T(8,128)(2,1)}, bf16[256,512]{1,0:T(8,128)(2,1)}, u32[]{:S(2)}, u32[]{:S(2)}) collective-permute-start(bf16[256,512]{1,0:T(8,128)(2,1)} %get-tuple-element.33), channel_id=1, source_target_pairs={{0,5},{1,4},{2,7},{3,6},{4,1},{5,0},{6,3},{7,2},{8,13},{9,12},{10,... | collective-permute-start | bytes 786440 | tf_op jit(solution)/shard_map/ppermute | solution.py:668
  49.6 12.3 %collective-permute-start.6 = (bf16[256,512]{1,0:T(8,128)(2,1)}, bf16[256,512]{1,0:T(8,128)(2,1)}, u32[]{:S(2)}, u32[]{:S(2)}) collective-permute-start(bf16[256,512]{1,0:T(8,128)(2,1)} %get-tuple-element.34), channel_id=1, source_target_pairs={{0,1},{1,0},{2,3},{3,2},{4,5},{5,4},{6,7},{7,6},{8,9},{9,8},{10,11... | collective-permute-start | bytes 786440 | tf_op jit(solution)/shard_map/ppermute | solution.py:668
  66.7 64.1 %all-to-all-start.2 = ((bf16[32,128,512]{2,1,0:T(8,128)(2,1)}), bf16[32,128,512]{2,1,0:T(8,128)(2,1)}, u32[]{:S(2)}, u32[]{:S(2)}) async-start(bf16[32,128,512]{2,1,0:T(8,128)(2,1)} %pack_x.2), calls=%async_computation.2 | async-start | bytes 8388608 | tf_op jit(solution)/shard_map/all_to_all | solution.py:636
  73.9 16.5 %copy-start.15 = (s32[2048]{0:T(1024)S(1)}, s32[2048]{0:T(1024)}, u32[]{:S(2)}) copy-start(s32[2048]{0:T(1024)} %param.15) | copy-start | bytes 24580
  73.9 17.4 %copy-start.16 = (f32[16]{0:T(128)S(1)}, f32[16]{0:T(128)}, u32[]{:S(2)}) copy-start(f32[16]{0:T(128)} %param.16) | copy-start | bytes 196
  73.9 18.1 %copy-start.17 = (f32[16]{0:T(128)S(1)}, f32[16]{0:T(128)}, u32[]{:S(2)}) copy-start(f32[16]{0:T(128)} %param.17) | copy-start | bytes 196
  73.9 18.7 %copy-start.18 = (f32[16]{0:T(128)S(1)}, f32[16]{0:T(128)}, u32[]{:S(2)}) copy-start(f32[16]{0:T(128)} %param.18) | copy-start | bytes 196
  77.0 9.7 %collective-permute-start.7 = (bf16[256,512]{1,0:T(8,128)(2,1)}, bf16[256,512]{1,0:T(8,128)(2,1)S(1)}, u32[]{:S(2)}, u32[]{:S(2)}) collective-permute-start(bf16[256,512]{1,0:T(8,128)(2,1)} %get-tuple-element.39), channel_id=1, source_target_pairs={{0,2},{1,3},{2,4},{3,5},{4,6},{5,7},{6,0},{7,1},{8,10},{9,11},{10,... | collective-permute-start | bytes 786440 | tf_op jit(solution)/shard_map/ppermute | solution.py:668
  79.7 10.6 %collective-permute-start.8 = (bf16[256,512]{1,0:T(8,128)(2,1)}, bf16[256,512]{1,0:T(8,128)(2,1)S(1)}, u32[]{:S(2)}, u32[]{:S(2)}) collective-permute-start(bf16[256,512]{1,0:T(8,128)(2,1)} %get-tuple-element.40), channel_id=1, source_target_pairs={{0,6},{1,7},{2,0},{3,1},{4,2},{5,3},{6,4},{7,5},{8,14},{9,15},{10,... | collective-permute-start | bytes 786440 | tf_op jit(solution)/shard_map/ppermute | solution.py:668
  79.7 46.1 %collective-permute-start.9 = (bf16[256,512]{1,0:T(8,128)(2,1)}, bf16[256,512]{1,0:T(8,128)(2,1)S(1)}, u32[]{:S(2)}, u32[]{:S(2)}) collective-permute-start(bf16[256,512]{1,0:T(8,128)(2,1)} %get-tuple-element.41), channel_id=1, source_target_pairs={{0,3},{1,2},{2,5},{3,4},{4,7},{5,6},{6,1},{7,0},{8,11},{9,10},{10,... | collective-permute-start | bytes 786440 | tf_op jit(solution)/shard_map/ppermute | solution.py:668
  82.1 43.8 %collective-permute-start.10 = (bf16[256,512]{1,0:T(8,128)(2,1)}, bf16[256,512]{1,0:T(8,128)(2,1)S(1)}, u32[]{:S(2)}, u32[]{:S(2)}) collective-permute-start(bf16[256,512]{1,0:T(8,128)(2,1)} %get-tuple-element.42), channel_id=1, source_target_pairs={{0,7},{1,6},{2,1},{3,0},{4,3},{5,2},{6,5},{7,4},{8,15},{9,14},{10,... | collective-permute-start | bytes 786440 | tf_op jit(solution)/shard_map/ppermute | solution.py:668
  82.1 43.8 %collective-permute-start.11 = (bf16[256,512]{1,0:T(8,128)(2,1)}, bf16[256,512]{1,0:T(8,128)(2,1)S(1)}, u32[]{:S(2)}, u32[]{:S(2)}) collective-permute-start(bf16[256,512]{1,0:T(8,128)(2,1)} %get-tuple-element.43), channel_id=1, source_target_pairs={{0,4},{1,5},{2,6},{3,7},{4,0},{5,1},{6,2},{7,3},{8,12},{9,13},{10,... | collective-permute-start | bytes 786440 | tf_op jit(solution)/shard_map/ppermute | solution.py:668
  86.7 16.9 %copy-start.4 = (bf16[256,512]{1,0:T(8,128)(2,1)}, bf16[256,512]{1,0:T(8,128)(2,1)S(1)}, u32[]{:S(2)}) copy-start(bf16[256,512]{1,0:T(8,128)(2,1)S(1)} %collective-permute-done.7.rest_0_) | copy-start | bytes 786436
  86.7 39.2 %collective-permute-start.12 = (bf16[256,512]{1,0:T(8,128)(2,1)}, bf16[256,512]{1,0:T(8,128)(2,1)S(1)}, u32[]{:S(2)}, u32[]{:S(2)}) collective-permute-start(bf16[256,512]{1,0:T(8,128)(2,1)} %get-tuple-element.44), channel_id=1, source_target_pairs={{0,5},{1,4},{2,7},{3,6},{4,1},{5,0},{6,3},{7,2},{8,13},{9,12},{10,... | collective-permute-start | bytes 786440 | tf_op jit(solution)/shard_map/ppermute | solution.py:668
  90.4 35.6 %collective-permute-start.13 = (bf16[256,512]{1,0:T(8,128)(2,1)}, bf16[256,512]{1,0:T(8,128)(2,1)S(1)}, u32[]{:S(2)}, u32[]{:S(2)}) collective-permute-start(bf16[256,512]{1,0:T(8,128)(2,1)} %get-tuple-element.45), channel_id=1, source_target_pairs={{0,1},{1,0},{2,3},{3,2},{4,5},{5,4},{6,7},{7,6},{8,9},{9,8},{10,11... | collective-permute-start | bytes 786440 | tf_op jit(solution)/shard_map/ppermute | solution.py:668
  201.7 16.7 %all-to-all-start.4 = ((bf16[16,16,1152]{2,1,0:T(8,128)(2,1)}), bf16[16,16,1152]{2,1,0:T(8,128)(2,1)S(1)}, u32[]{:S(2)}, u32[]{:S(2)}) async-start(bf16[16,16,1152]{2,1,0:T(8,128)(2,1)} %leaving.1.refs_12_), calls=%async_computation.4 | async-start | bytes 1179648 | tf_op jit(solution)/shard_map/all_to_all | solution.py:636
  222.2 17.8 %all-to-all-start.5 = ((bf16[16,16,1024]{2,1,0:T(8,128)(2,1)}), bf16[16,16,1024]{2,1,0:T(8,128)(2,1)S(1)}, u32[]{:S(2)}, u32[]{:S(2)}) async-start(bf16[16,16,1024]{2,1,0:T(8,128)(2,1)} %scan_owners.1.refs_12_), calls=%async_computation.5 | async-start | bytes 1048576 | tf_op jit(solution)/shard_map/all_to_all | solution.py:636
  (15 other events, 58.3 us)

commit v3 on v2

--- a/solution.py
+++ b/solution.py
@@ -25,6 +25,7 @@
 ANY = pl.BlockSpec(memory_space=pl.ANY)
 WHOLE = pl.BlockSpec(memory_space=pltpu.VMEM)
 SMEM = pl.BlockSpec(memory_space=pltpu.SMEM)
+EARLY = 2
 SHIFTS = [(1, 0), (3, 0), (1, 1), (3, 1), (2, 0), (2, 1), (0, 1)]
 
 
@@ -91,7 +92,8 @@
     )(b_rows, c_rows, dt_rows)
 
 
-def pack_small_kernel(slot_ref, place_ref, in_ref, out_ref, tags, sems):
+def pack_small_kernel(slot_ref, place_ref, in_ref, *rest):
+    out_ref, tags, sems = rest[-3:]
     copies = [
         pltpu.make_async_copy(
             in_ref.at[j], out_ref.at[slot_ref[j], pl.ds(0, SMALL_ROWS), :], sems.at[j]
@@ -112,10 +114,10 @@
         copy.wait()
 
 
-def pack_small(slot, place, pieces):
+def pack_small(slot, place, pieces, after):
     return pl.pallas_call(
         pack_small_kernel,
-        in_specs=[SMEM, SMEM, WHOLE],
+        in_specs=[SMEM, SMEM, WHOLE] + [ANY] * len(after),
         out_specs=ANY,
         out_shape=jax.ShapeDtypeStruct((2 * OWNERS, SENT_ROWS, STATE), BF16),
         scratch_shapes=[
@@ -124,7 +126,7 @@
         ],
         compiler_params=params(),
         name="pack_small",
-    )(slot, place, pieces)
+    )(slot, place, pieces, *after)
 
 
 def find_source_kernel(small_ref, out_ref, tags, sem):
@@ -223,6 +225,22 @@
         compiler_params=params(),
         name="pack_x",
     )(slot, origin, x_rows, *arrived, *after)
+
+
+def hold_kernel(value_ref, *rest):
+    del value_ref, rest
+
+
+def hold(value, after):
+    return pl.pallas_call(
+        hold_kernel,
+        in_specs=[ANY] * (1 + len(after)),
+        out_specs=ANY,
+        out_shape=jax.ShapeDtypeStruct(value.shape, value.dtype),
+        input_output_aliases={0: 0},
+        compiler_params=params(),
+        name="hold",
+    )(value, *after)
 
 
 def split_two(value):
@@ -300,9 +318,11 @@
         decay = jnp.exp2(ends[k]) * (starts[k] == 0.0).astype(F32)
         high, low = split_two(jnp.broadcast_to(decay, (HEADS, PIECE)))
         ends_ref[k] = (over_first(high, spread_one) + over_first(low, spread_one))[0:8]
-    total_ref[...] = jnp.broadcast_to(
-        jnp.exp2(log_before[-1]) * (starts_before[-1] == 0.0).astype(F32), total_ref.shape
-    )
+    total = jnp.exp2(log_before[-1]) * (starts_before[-1] == 0.0).astype(F32)
+    total = jnp.broadcast_to(total, (HEADS, PIECE))
+    high = total.astype(BF16).astype(F32)
+    blank = jnp.zeros((PIECE - 2 * HEADS, PIECE), F32)
+    total_ref[...] = jnp.concatenate([high, total - high, blank], axis=0).T[0:16].astype(BF16)
 
 
 ROW_COUNT = 56
@@ -328,7 +348,7 @@
             jax.ShapeDtypeStruct(square, F32),
             jax.ShapeDtypeStruct(square, BF16),
             jax.ShapeDtypeStruct((pieces, 8, WIDTH), F32),
-            jax.ShapeDtypeStruct((HEADS, PIECE), F32),
+            jax.ShapeDtypeStruct((16, EXTRA), BF16),
         ],
         scratch_shapes=[
             pltpu.VMEM((pieces, HEADS, PIECE), BF16),
@@ -394,7 +414,7 @@
         held = state[:, cols]
         out = jnp.concatenate(near, axis=1) + skip_ref[:, cols] * wide
         out += dot(scales, spread_ref[into, :, cols]) * dot(left, held.astype(BF16))
-        out_ref[r, :, cols] = out
+        out_ref[r, :, cols] = out.astype(BF16)
         scaled = (wide * dot(scales, spread_ref[out_of, :, cols])).astype(BF16)
         state[:, cols] = ends_ref[r, 0:1, cols] * held + dot(turned, scaled)
 
@@ -456,7 +476,7 @@
             out_specs=pl.BlockSpec((RUN, PIECE, width), at),
             scratch_shapes=[pltpu.VMEM((STATE, width), F32)],
         ),
-        out_shape=jax.ShapeDtypeStruct((pieces, PIECE, width), F32),
+        out_shape=jax.ShapeDtypeStruct((pieces, PIECE, width), BF16),
         compiler_params=params(),
         name=name,
     )(src, *firsts, *values, rows, cols, scales, ends, spread_four, skip, after)
@@ -487,40 +507,62 @@
     )
 
 
-def leaving_state(kind, keys_ref, v_all, scale_ref, spread_ref, store):
+def leaving_state(kind, keys_ref, v_all, scale_ref, spread_ref, state, wait):
     pieces = scale_ref.shape[0]
-    for group in range(WIDTH // GROUP):
-        cols = slice(group * GROUP, (group + 1) * GROUP)
-        state = None
-        for k in range(0, pieces, 4):
-            scales = scale_ref[k : k + 4].reshape(4 * PIECE, PIECE)
-            scale = dot(scales, spread_ref[kind, :, cols])
-            values = v_all[k : k + 4, :, cols].reshape(4 * PIECE, GROUP)
+    for k in range(0, pieces, RUN):
+        wait(k)
+        scales = scale_ref[k : k + RUN].reshape(RUN * PIECE, PIECE)
+        for group in range(WIDTH // GROUP):
+            cols = slice(group * GROUP, (group + 1) * GROUP)
+            scale = dot(scales, spread_ref[0, :, cols])
+            values = v_all[k : k + RUN, :, cols].reshape(RUN * PIECE, GROUP)
             scaled = (values.astype(F32) * scale).astype(BF16)
-            for r in range(4):
+            total = None if k == 0 else state[:, cols]
+            for r in range(RUN):
                 update = dot(keys_ref[k + r], scaled[r * PIECE : (r + 1) * PIECE])
-                state = update if state is None else state + update
-        store(cols, state.astype(BF16))
-
-
-def leaving_gradient_kernel(cot_ref, keys_ref, scale_ref, spread_ref, out_ref):
-    def store(cols, value):
-        out_ref[:, cols] = value
-
-    leaving_state(BEFORE, keys_ref, cot_ref, scale_ref, spread_ref, store)
+                total = update if total is None else total + update
+            state[:, cols] = total
+
+
+def leaving_gradient_kernel(cot_ref, keys_ref, scale_ref, spread_ref, out_ref, v_all, state, sems):
+    copies = [
+        pltpu.make_async_copy(cot_ref.at[pl.ds(k * PIECE, PIECE), :], v_all.at[k], sems.at[k])
+        for k in range(scale_ref.shape[0])
+    ]
+    for copy in copies:
+        copy.start()
+
+    def wait(k):
+        for copy in copies[k : k + RUN]:
+            copy.wait()
+
+    leaving_state(BEFORE, keys_ref, v_all, scale_ref, spread_ref, state, wait)
+    out_ref[...] = state[...].astype(BF16)
+
+
+def kind_spec(kind):
+    return pl.BlockSpec((1, PIECE, WIDTH), lambda i: (kind, 0, 0))
 
 
 def leaving_gradient(keys, cotangent, scales, spread_four):
     pieces = scales.shape[0]
     return pl.pallas_call(
         leaving_gradient_kernel,
+        grid=(1,),
+        in_specs=[ANY, WHOLE, WHOLE, kind_spec(BEFORE)],
+        out_specs=WHOLE,
         out_shape=jax.ShapeDtypeStruct((STATE, WIDTH), BF16),
+        scratch_shapes=[
+            pltpu.VMEM((pieces, PIECE, WIDTH), BF16),
+            pltpu.VMEM((STATE, WIDTH), F32),
+            pltpu.SemaphoreType.DMA((pieces,)),
+        ],
         compiler_params=params(),
         name="leaving_gradient",
-    )(cotangent.reshape(pieces, PIECE, WIDTH), keys, scales, spread_four)
-
-
-def leaving_kernel(src_ref, xa_ref, xb_ref, keys_ref, scale_ref, spread_ref, g_ref, total_ref, out_ref, v_all, sems):
+    )(cotangent, keys, scales, spread_four)
+
+
+def leaving_kernel(src_ref, xa_ref, xb_ref, keys_ref, scale_ref, spread_ref, g_ref, total_ref, out_ref, v_all, state, sems):
     ins = []
     for k in range(scale_ref.shape[0]):
         for half, ref in enumerate((xa_ref, xb_ref)):
@@ -528,32 +570,31 @@
             ins.append(pltpu.make_async_copy(ref.at[src_ref[0, k]], to, sems.at[half, k]))
     for copy in ins:
         copy.start()
-    high, low = split_two(total_ref[...])
-    lane = lax.broadcasted_iota(jnp.int32, high.shape, 1)
-    decay = jnp.where(lane == 0, high, jnp.where(lane == 1, low, jnp.zeros_like(low)))
     for part in range(OWNERS):
-        out_ref[part, :, WIDTH:] = decay
+        out_ref[part, :, WIDTH:] = total_ref[...]
         if part >= 8:
             out_ref[part, :, 0:WIDTH] = g_ref[part % 8 * 16 : part % 8 * 16 + 16, :]
-    for copy in ins:
-        copy.wait()
-
-    def store(cols, value):
-        for part in range(8):
-            out_ref[part, :, cols] = value[part * 16 : part * 16 + 16]
-
-    leaving_state(AFTER, keys_ref, v_all, scale_ref, spread_ref, store)
+
+    def wait(k):
+        for copy in ins[2 * k : 2 * (k + RUN)]:
+            copy.wait()
+
+    leaving_state(AFTER, keys_ref, v_all, scale_ref, spread_ref, state, wait)
+    for part in range(8):
+        out_ref[part, :, 0:WIDTH] = state[part * 16 : part * 16 + 16, :].astype(BF16)
 
 
 def leaving(src, x_slots, keys, scales, spread_four, g_state, total):
     pieces = scales.shape[0]
     return pl.pallas_call(
         leaving_kernel,
-        in_specs=[SMEM, ANY, ANY] + [WHOLE] * 5,
+        grid=(1,),
+        in_specs=[SMEM, ANY, ANY, WHOLE, WHOLE, kind_spec(AFTER), WHOLE, WHOLE],
         out_specs=WHOLE,
         out_shape=jax.ShapeDtypeStruct((OWNERS, 16, WIDTH + EXTRA), BF16),
         scratch_shapes=[
             pltpu.VMEM((pieces, PIECE, WIDTH), BF16),
+            pltpu.VMEM((STATE, WIDTH), F32),
             pltpu.SemaphoreType.DMA((2, pieces)),
         ],
         compiler_params=params(),
@@ -563,15 +604,17 @@
 
 def scan_kernel(back_ref, part_ref, after_ref, out_ref):
     back = back_ref[0]
-    head = lax.broadcasted_iota(jnp.int32, (HEADS, WIDTH), 0)
-    lane = lax.broadcasted_iota(jnp.int32, (HEADS, WIDTH), 1)
-    spread_one = (lane // HEAD_DIM == head).astype(BF16)
-    held = jnp.zeros((HEADS, WIDTH), F32)
-    for k in range(OWNERS):
-        at = jnp.where(back == 1, OWNERS - 1 - k, k)
+    head = lax.broadcasted_iota(jnp.int32, (EXTRA, WIDTH), 0)
+    lane = lax.broadcasted_iota(jnp.int32, (EXTRA, WIDTH), 1)
+    spread_one = ((head < 2 * HEADS) & (lane // HEAD_DIM == head % HEADS)).astype(BF16)
+    decays_in = part_ref[:, :, WIDTH:].reshape(OWNERS * 16, EXTRA)
+    decay_ref = dot(decays_in, spread_one).reshape(OWNERS, 16, WIDTH)
+    order = [jnp.where(back == 1, OWNERS - 1 - k, k) for k in range(OWNERS)]
+    held = jnp.zeros((16, WIDTH), F32)
+    for k, at in enumerate(order):
         out_ref[at] = held.astype(BF16)
-        decay = over_first(part_ref[at, :, WIDTH:], spread_one)
-        held = (decay[0:1] + decay[1:2]) * held + part_ref[at, :, 0:WIDTH].astype(F32)
+        decay = jnp.where(back == 1, decay_ref[OWNERS - 1 - k], decay_ref[k])
+        held = decay * held + part_ref[at, :, 0:WIDTH].astype(F32)
 
 
 def scan_owners(back, parts, after):
@@ -586,8 +629,9 @@
 
 
 def finish_kernel(b_ref, c_ref, ya_ref, yb_ref, g_ref, enter_ref, scale_ref, spread_ref, y_out, g_out):
-    rows = 2 * PIECE
-    b, c, scales = b_ref[...].reshape(rows, STATE), c_ref[...].reshape(rows, STATE), scale_ref[...].reshape(rows, PIECE)
+    rows = RUN * PIECE
+    b, c = b_ref[...].reshape(rows, STATE), c_ref[...].reshape(rows, STATE)
+    scales = scale_ref[...].reshape(rows, PIECE)
     for group in range(WIDTH // GROUP):
         cols = slice(group * GROUP, (group + 1) * GROUP)
         y_off = dot(scales, spread_ref[BEFORE, :, cols]) * dot(c, enter_ref[0:STATE, cols])
@@ -601,12 +645,12 @@
 def finish(b, c, y_a, y_b, g_local, enter, scales, spread_four):
     pieces = scales.shape[0]
     out = jax.ShapeDtypeStruct((pieces * PIECE, WIDTH), BF16)
-    square = pl.BlockSpec((2, PIECE, PIECE), lambda k: (k, 0, 0))
-    half = pl.BlockSpec((2, PIECE, HALF), lambda k: (k, 0, 0))
-    wide = pl.BlockSpec((2, PIECE, WIDTH), lambda k: (k, 0, 0))
+    square = pl.BlockSpec((RUN, PIECE, PIECE), lambda k: (k, 0, 0))
+    half = pl.BlockSpec((RUN, PIECE, HALF), lambda k: (k, 0, 0))
+    wide = pl.BlockSpec((RUN, PIECE, WIDTH), lambda k: (k, 0, 0))
     return pl.pallas_call(
         finish_kernel,
-        grid=(pieces // 2,),
+        grid=(pieces // RUN,),
         in_specs=[
             square,
             square,
@@ -617,7 +661,7 @@
             square,
             pl.BlockSpec(spread_four.shape, lambda k: (0, 0, 0)),
         ],
-        out_specs=[pl.BlockSpec((2 * PIECE, WIDTH), lambda k: (k, 0))] * 2,
+        out_specs=[pl.BlockSpec((RUN * PIECE, WIDTH), lambda k: (k, 0))] * 2,
         out_shape=[out, out],
         compiler_params=params(),
         name="finish",
@@ -647,31 +691,34 @@
 
     small = gather_small(b_rows, c_rows, dt_rows)
     small = lax.all_to_all(small, "head", split_axis=0, concat_axis=0, tiled=True)
+    cuts = [cut(half, dest_heads, x_rows) for half in range(2)]
+    arrived = []
+    for half in range(2):
+        arrived.append([])
+        for shift, piece in zip(SHIFTS, cuts[half]):
+            pairs = [(h, partner(h, shift)) for h in range(PEERS)]
+            arrived[half].append(lax.ppermute(piece, "head", pairs))
     small = small.reshape(OWNERS, SMALL_ROWS, STATE)
-    small = to_owners(pack_small(send_slot, destination % OWNERS, small))
-    src = find_source(small)
+    small = pack_small(send_slot, destination % OWNERS, small, arrived[0][:EARLY])
+    small = to_owners(small)
+
     pieces = destination.shape[0]
     seg = jnp.cumsum(doc_start.reshape(pieces, PIECE), axis=1).astype(F32)[:, None, :]
-    b, c, bt, ct, rows, cols, scales, ends, total = decays(
-        src, small, seg, dt_bias.reshape(HEADS, 1), a_log.reshape(HEADS, 1)
-    )
+    bias, alog = dt_bias.reshape(HEADS, 1), a_log.reshape(HEADS, 1)
     skip = jnp.repeat(d_skip, HEAD_DIM).reshape(1, WIDTH)
     spread_four = spread(4)
+    first = [seg, bias, alog, skip, spread_four, cuts[1][0]]
+    x_a = pack_x(0, send_slot, origin, x_rows, arrived[0], first)
+    x_a = to_owners(x_a)
+
+    src = find_source(small)
+    b, c, bt, ct, rows, cols, scales, ends, total = decays(src, small, seg, bias, alog)
     local = (rows, cols, scales, ends, spread_four, skip)
-
-    x_slots = []
-    after = []
-    for half in range(2):
-        arrived = []
-        for shift, piece in zip(SHIFTS, cut(half, dest_heads, x_rows)):
-            pairs = [(h, partner(h, shift)) for h in range(PEERS)]
-            arrived.append(lax.ppermute(piece, "head", pairs))
-        x_slots.append(to_owners(pack_x(half, send_slot, origin, x_rows, arrived, after)))
-        if half == 0:
-            g_state = leaving_gradient(ct, cotangent, scales, spread_four)
-            g_local = backward_local(src, b, ct, cotangent, local, g_state)
-            after = [g_local]
-
+    g_state = leaving_gradient(ct, cotangent, scales, spread_four)
+    g_local = backward_local(src, b, ct, cotangent, local, g_state)
+
+    x_b = pack_x(1, send_slot, origin, x_rows, arrived[1], [g_state])
+    x_slots = [x_a, to_owners(hold(x_b, [g_local]))]
     parts = leaving(src, x_slots, bt, scales, spread_four, g_state, total)
     y_a = forward_local(0, src, c, bt, x_slots, local, parts)
     back = (me >= OWNERS // 2).astype(jnp.int32).reshape(1)

time: 256 us -> 239 us (0.934)
  waiting for transfers between devices: 38.3 us -> 29 us
  blocking collectives: 63.4 us -> 55.8 us
  Pallas kernels: 94 us -> 88.6 us
  starting transfers between devices: 45.6 us -> 48.9 us
    all_to_all x1, waiting for transfers between devices: 13.4 us -> 0.01 us  [body(): lax.all_to_all(small, 'head', split_axis=0, concat_axis=0, tiled=True)]
    all_to_all x1, blocking collectives: 63.4 us -> 55.8 us  [to_owners(): return lax.all_to_all(value, 'ctx', split_axis=0, concat_axis=0, tiled=True)]
    all_to_all x4, waiting for transfers between devices: 0.01 us -> 4.86 us  [to_owners(): return lax.all_to_all(value, 'ctx', split_axis=0, concat_axis=0, tiled=True)]
    pallas_call x4 -> x5, Pallas kernels: 29.7 us -> 25.7 us  [the longest x1 10.1 us: finish(): pl.pallas_call(finish_kernel, grid=(pieces // RUN,), in_specs=[square, sq...]
    ppermute x14, starting transfers between devices: 13 us -> 16 us  [body(): arrived[half].append(lax.ppermute(piece, 'head', pairs))]
    unnamed x40 -> x52, local copies, waits for them, and re-layouts: 5.64 us -> 6.48 us
  transfers between devices with their start and end apart: 19 -> 19, of which waited for: 7 -> 6; matrix products, arithmetic and copies ran while one was open for 3% -> 3% of each run, Pallas kernels for 25% -> 27%
where the time goes in v3:
time: 239 us; the launch traced here: 237 us
  Pallas kernels  88.6 us (37%)
  blocking collectives  55.8 us (23%)
  starting transfers between devices  48.9 us (20%)
  waiting for transfers between devices  29 us (12%)
  local copies, waits for them, and re-layouts  9.9 us (4%)
  other arithmetic  3.52 us (1%)
    all_to_all x1, blocking collectives, to_owners(): return lax.all_to_all(value, 'ctx', split_axis=0, concat_axis=0, tiled=True)  55.8 us
    pallas_call x3, Pallas kernels, local_call(): pl.pallas_call(skip_src(kernel), grid_spec=pltpu.PrefetchScalarGridSpec(n...  36.6 us
    all_to_all x4, starting transfers between devices, to_owners(): return lax.all_to_all(value, 'ctx', split_axis=0, concat_axis=0, tiled=True)  28.4 us
    ppermute x14, waiting for transfers between devices, body(): arrived[half].append(lax.ppermute(piece, 'head', pairs))  24.1 us
    ppermute x14, starting transfers between devices, body(): arrived[half].append(lax.ppermute(piece, 'head', pairs))  16 us
    pallas_call x1, Pallas kernels, finish(): pl.pallas_call(finish_kernel, grid=(pieces // RUN,), in_specs=[square, sq...  10.1 us
    pallas_call x1, Pallas kernels, decays(): pl.pallas_call(decay_kernel, in_specs=[SMEM, ANY, WHOLE, WHOLE, WHOLE], o...  7.24 us
    pallas_call x1, Pallas kernels, leaving(): pl.pallas_call(leaving_kernel, grid=(1,), in_specs=[SMEM, ANY, ANY, WHOLE...  6.79 us
  transfers between devices with their start and end apart: 19, of which 6 were waited for; matrix products, arithmetic and copies ran while one was open for 3% of the time, Pallas kernels for 27%

profile of v3, /device:TPU:98, one launch (start us, length us, event | category | flops | bytes accessed | tf_op | source)
XLA Modules:
  0.0 236.7 jit_solution(1638910064608432106)
XLA Ops:
  0.6 2.5 %gather_small.1 = bf16[8,2,272,128]{3,2,1,0:T(8,128)(2,1)} custom-call(bf16[256,1024]{1,0:T(8,128)(2,1)} %b_ref.1, bf16[256,1024]{1,0:T(8,128)(2,1)} %c_ref.1, bf16[256,128]{1,0:T(8,128)(2,1)} %dt_ref.1), custom_call_target="tpu_custom_call" | custom-call | tf_op jit(solution)/shard_map/gather_small/pallas_call | solution.py:81
  3.1 4.5 %all-to-all-start = ((bf16[8,2,272,128]{3,2,1,0:T(8,128)(2,1)}), bf16[8,2,272,128]{3,2,1,0:T(8,128)(2,1)S(1)}, u32[]{:S(2)}, u32[]{:S(2)}) async-start(bf16[8,2,272,128]{3,2,1,0:T(8,128)(2,1)} %gather_small.1), calls=%async_computation | async-start | bytes 2228224 | tf_op jit(solution)/shard_map/all_to_all | solution.py:693
  8.3 3.1 %cut.2 = (bf16[256,512]{1,0:T(8,128)(2,1)}, bf16[256,512]{1,0:T(8,128)(2,1)}, bf16[256,512]{1,0:T(8,128)(2,1)}, bf16[256,512]{1,0:T(8,128)(2,1)}, bf16[256,512]{...) custom-call(s32[7]{0:T(128)} %stack.46.dest_ref, bf16[256,8192]{1,0:T(8,128)(2,1)} %x_ref.7), custom_call_target="tpu_custom_call" | custom-call | tf_op jit(solution)/shard_map/cut/pallas_call | solution.py:179
  14.8 12.4 %collective-permute-done.rest_0_ = bf16[256,512]{1,0:T(8,128)(2,1)S(1)} collective-permute-done((bf16[256,512]{1,0:T(8,128)(2,1)}, bf16[256,512]{1,0:T(8,128)(2,1)S(1)}, u32[]{:S(2)}, u32[]{:S(2)}) %collective-permute-start) | collective-permute-done | bytes 262176 | tf_op jit(solution)/shard_map/ppermute | solution.py:700
  30.9 7.5 %all-to-all-start.1 = ((bf16[32,288,128]{2,1,0:T(8,128)(2,1)}), bf16[32,288,128]{2,1,0:T(8,128)(2,1)S(1)}, u32[]{:S(2)}, u32[]{:S(2)}) async-start(bf16[32,288,128]{2,1,0:T(8,128)(2,1)} %pack_small.1), calls=%async_computation.1 | async-start | bytes 4718592 | tf_op jit(solution)/shard_map/all_to_all | solution.py:680
  43.9 3.2 %cut.3 = (bf16[256,512]{1,0:T(8,128)(2,1)}, bf16[256,512]{1,0:T(8,128)(2,1)}, bf16[256,512]{1,0:T(8,128)(2,1)}, bf16[256,512]{1,0:T(8,128)(2,1)}, bf16[256,512]{...) custom-call(s32[7]{0:T(128)} %stack.46.dest_ref, bf16[256,8192]{1,0:T(8,128)(2,1)} %x_ref.7), custom_call_target="tpu_custom_call" | custom-call | tf_op jit(solution)/shard_map/cut/pallas_call | solution.py:179
  52.0 3.0 %collective-permute-done.4.rest_4_ = bf16[256,512]{1,0:T(8,128)(2,1)S(1)} collective-permute-done((bf16[256,512]{1,0:T(8,128)(2,1)}, bf16[256,512]{1,0:T(8,128)(2,1)S(1)}, u32[]{:S(2)}, u32[]{:S(2)}) %collective-permute-start.4) | collective-permute-done | bytes 262176 | tf_op jit(solution)/shard_map/ppermute | solution.py:700
  55.1 5.0 %collective-permute-done.5.rest_5_ = bf16[256,512]{1,0:T(8,128)(2,1)S(1)} collective-permute-done((bf16[256,512]{1,0:T(8,128)(2,1)}, bf16[256,512]{1,0:T(8,128)(2,1)S(1)}, u32[]{:S(2)}, u32[]{:S(2)}) %collective-permute-start.5) | collective-permute-done | bytes 262176 | tf_op jit(solution)/shard_map/ppermute | solution.py:700
  60.8 3.2 %pack_x.2 = bf16[32,128,512]{2,1,0:T(8,128)(2,1)} custom-call(s32[16]{0:T(128)} %multiply_add_fusion.slot_ref, s32[8]{0:T(128)} %stack.49.from_ref, bf16[256,8192]{1,0:T(8,128)(2,1)} %x_ref.7, bf16[256,512]{1,0:T(8,128)(2,1)} %copy-done.4, bf16[256,512]{1,0:T(8,128)(2,1)} %copy-done.5, bf16[256,512]{1,0:T(8,128)(2,1)} %copy-done.7, ...), custom_call_target="tpu_custom_call" | custom-call | tf_op jit(solution)/shard_map/pack_x/pallas_call | solution.py:216
  64.1 4.3 %all-to-all-done.1.small_ref = bf16[32,288,128]{2,1,0:T(8,128)(2,1)S(1)} async-done(((bf16[32,288,128]{2,1,0:T(8,128)(2,1)}), bf16[32,288,128]{2,1,0:T(8,128)(2,1)S(1)}, u32[]{:S(2)}, u32[]{:S(2)}) %all-to-all-start.1) | async-done | bytes 2359328 | tf_op jit(solution)/shard_map/all_to_all | solution.py:680
  69.8 7.7 %all-to-all-start.2 = ((bf16[32,128,512]{2,1,0:T(8,128)(2,1)}), bf16[32,128,512]{2,1,0:T(8,128)(2,1)}, u32[]{:S(2)}, u32[]{:S(2)}) async-start(bf16[32,128,512]{2,1,0:T(8,128)(2,1)} %pack_x.2), calls=%async_computation.2 | async-start | bytes 8388608 | tf_op jit(solution)/shard_map/all_to_all | solution.py:680
  80.3 3.0 %collective-permute-start.11 = (bf16[256,512]{1,0:T(8,128)(2,1)S(1)}, bf16[256,512]{1,0:T(8,128)(2,1)S(1)}, u32[]{:S(2)}, u32[]{:S(2)}) collective-permute-start(bf16[256,512]{1,0:T(8,128)(2,1)S(1)} %copy-done.24), channel_id=1, source_target_pairs={{0,4},{1,5},{2,6},{3,7},{4,0},{5,1},{6,2},{7,3},{8,12},{9,13},{10,... | collective-permute-start | bytes 786440 | tf_op jit(solution)/shard_map/ppermute | solution.py:700
  83.7 3.6 %collective-permute-done.8.rest_1_ = bf16[256,512]{1,0:T(8,128)(2,1)S(1)} collective-permute-done((bf16[256,512]{1,0:T(8,128)(2,1)}, bf16[256,512]{1,0:T(8,128)(2,1)S(1)}, u32[]{:S(2)}, u32[]{:S(2)}) %collective-permute-start.8) | collective-permute-done | bytes 262176 | tf_op jit(solution)/shard_map/ppermute | solution.py:700
  91.2 7.2 %decays.1 = (bf16[16,128,128]{2,1,0:T(8,128)(2,1)}, bf16[16,128,128]{2,1,0:T(8,128)(2,1)}, bf16[16,128,128]{2,1,0:T(8,128)(2,1)}, bf16[16,128,128]{2,1,0:T(8,128...) custom-call(s32[1,128]{1,0:T(1,128)} %find_source.1.src_ref, ...), custom_call_target="tpu_custom_call" | custom-call | tf_op jit(solution)/shard_map/decays/pallas_call | solution.py:338
  98.4 6.3 %leaving_gradient.1.rest_7_.refs_9_.g_ref = bf16[128,1024]{1,0:T(8,128)(2,1)} custom-call(bf16[2048,1024]{1,0:T(8,128)(2,1)} %refs_2_.1, bf16[16,128,128]{2,1,0:T(8,128)(2,1)} %get-tuple-element.46.keys_ref.refs_1_, bf16[16,128,128]{2,1,0:T(8,128)(2,1)} %get-tuple-element.38.scale_ref.refs_5_.refs_8_, ...), custom_call_target="tpu_custom_call" | custom-call | tf_op jit(solution)/shard_map/leaving_gradient/pallas_call | solution.py:549
  104.8 15.9 %backward_local.1.rest_0_.g_ref = bf16[16,128,1024]{2,1,0:T(8,128)(2,1)} custom-call(s32[1,128]{1,0:T(1,128)} %find_source.1.src_ref, bf16[16,128,128]{2,1,0:T(8,128)(2,1)} %get-tuple-element.27.refs_0_.b_ref, bf16[16,128,128]{2,1,0:T(8,128)(2,1)} %get-tuple-element.46.keys_ref.refs_1_, bf16[2048,1024]{1,0:T(8,128)(2,1)} %refs_2_.1, ...), custom_call_target="tpu_custom_call" | custom-call | tf_op jit(solution)/shard_map/backward_local/pallas_call | solution.py:459
  122.4 3.2 %pack_x.3.value_ref = bf16[32,128,512]{2,1,0:T(8,128)(2,1)} custom-call(s32[16]{0:T(128)} %multiply_add_fusion.slot_ref, s32[8]{0:T(128)} %stack.49.from_ref, bf16[256,8192]{1,0:T(8,128)(2,1)} %x_ref.7, bf16[256,512]{1,0:T(8,128)(2,1)} %copy-done.17, bf16[256,512]{1,0:T(8,128)(2,1)} %copy-done.11, bf16[256,512]{1,0:T(8,128)(2,1)} %copy-done.12, ...), custom_call_target="tpu_custom_call" | custom-call | tf_op jit(solution)/shard_map/pack_x/pallas_call | solution.py:216
  126.2 55.8 %all_to_all.30.xb_ref.refs_2_.refs_3_.refs_4_.refs_5_ = bf16[32,128,512]{2,1,0:T(8,128)(2,1)} all-to-all(bf16[32,128,512]{2,1,0:T(8,128)(2,1)} %hold.1), channel_id=1, replica_groups=mesh['ctx'=16,'head'=8] {'ctx'}, dimensions={0} | all-to-all | bytes 8388608 | tf_op jit(solution)/shard_map/all_to_all | solution.py:680
  182.0 6.8 %leaving.1.refs_12_ = bf16[16,16,1152]{2,1,0:T(8,128)(2,1)} custom-call(s32[1,128]{1,0:T(1,128)} %find_source.1.src_ref, bf16[32,128,512]{2,1,0:T(8,128)(2,1)} %all-to-all-done.2.xa_ref.refs_2_.refs_3_.refs_4_.refs_5_, bf16[32,128,512]{2,1,0:T(8,128)(2,1)} %all_to_all.30.xb_ref.refs_2_.refs_3_.refs_4_.refs_5_, ...), custom_call_target="tpu_custom_call" | custom-call | tf_op jit(solution)/shard_map/leaving/pallas_call | solution.py:589
  188.8 5.9 %all-to-all-start.4 = ((bf16[16,16,1152]{2,1,0:T(8,128)(2,1)}), bf16[16,16,1152]{2,1,0:T(8,128)(2,1)S(1)}, u32[]{:S(2)}, u32[]{:S(2)}) async-start(bf16[16,16,1152]{2,1,0:T(8,128)(2,1)} %leaving.1.refs_12_), calls=%async_computation.4 | async-start | bytes 1179648 | tf_op jit(solution)/shard_map/all_to_all | solution.py:680
  194.7 10.4 %forward_local.2.after_ref.ya_ref = bf16[16,128,512]{2,1,0:T(8,128)(2,1)} custom-call(s32[1,128]{1,0:T(1,128)} %find_source.1.src_ref, bf16[16,128,128]{2,1,0:T(8,128)(2,1)} %get-tuple-element.28.refs_0_.c_ref, bf16[16,128,128]{2,1,0:T(8,128)(2,1)} %get-tuple-element.29.keys_ref.refs_1_, ...), custom_call_target="tpu_custom_call" | custom-call | tf_op jit(solution)/shard_map/forward_local/pallas_call | solution.py:459
  208.1 7.3 %all-to-all-start.5 = ((bf16[16,16,1024]{2,1,0:T(8,128)(2,1)}), bf16[16,16,1024]{2,1,0:T(8,128)(2,1)S(1)}, u32[]{:S(2)}, u32[]{:S(2)}) async-start(bf16[16,16,1024]{2,1,0:T(8,128)(2,1)} %scan_owners.1.refs_12_), calls=%async_computation.5 | async-start | bytes 1048576 | tf_op jit(solution)/shard_map/all_to_all | solution.py:680
  215.4 10.4 %forward_local.3.yb_ref = bf16[16,128,512]{2,1,0:T(8,128)(2,1)} custom-call(s32[1,128]{1,0:T(1,128)} %find_source.1.src_ref, bf16[16,128,128]{2,1,0:T(8,128)(2,1)} %get-tuple-element.28.refs_0_.c_ref, bf16[16,128,128]{2,1,0:T(8,128)(2,1)} %get-tuple-element.29.keys_ref.refs_1_, bf16[32,128,512]{2,1,0:T(8,128)(2,1)} %all_to_all.30.xb_ref.refs_2_.refs_3_.refs_4_.refs_5_, ...), custom_call_target="tpu_custom_call" | custom-call | tf_op jit(solution)/shard_map/forward_local/pallas_call | solution.py:459
  226.6 10.1 %finish.1 = (bf16[2048,1024]{1,0:T(8,128)(2,1)}, bf16[2048,1024]{1,0:T(8,128)(2,1)}) custom-call(bf16[16,128,128]{2,1,0:T(8,128)(2,1)} %get-tuple-element.27.refs_0_.b_ref, bf16[16,128,128]{2,1,0:T(8,128)(2,1)} %get-tuple-element.28.refs_0_.c_ref, bf16[16,128,512]{2,1,0:T(8,128)(2,1)} %forward_local.2.after_ref.ya_ref, ...), custom_call_target="tpu_custom_call" | custom-call | tf_op jit(solution)/shard_map/finish/pallas_call | solution.py:651
  (100 shorter events, 33.3 us)
Async XLA Ops:
  3.1 24.2 %all-to-all-start = ((bf16[8,2,272,128]{3,2,1,0:T(8,128)(2,1)}), bf16[8,2,272,128]{3,2,1,0:T(8,128)(2,1)S(1)}, u32[]{:S(2)}, u32[]{:S(2)}) async-start(bf16[8,2,272,128]{3,2,1,0:T(8,128)(2,1)} %gather_small.1), calls=%async_computation | async-start | bytes 2228224 | tf_op jit(solution)/shard_map/all_to_all | solution.py:693
  11.4 15.9 %collective-permute-start = (bf16[256,512]{1,0:T(8,128)(2,1)}, bf16[256,512]{1,0:T(8,128)(2,1)S(1)}, u32[]{:S(2)}, u32[]{:S(2)}) collective-permute-start(bf16[256,512]{1,0:T(8,128)(2,1)} %get-tuple-element.25), channel_id=1, source_target_pairs={{0,2},{1,3},{2,4},{3,5},{4,6},{5,7},{6,0},{7,1},{8,10},{9,11},{10,... | collective-permute-start | bytes 786440 | tf_op jit(solution)/shard_map/ppermute | solution.py:700
  11.5 15.8 %collective-permute-start.1 = (bf16[256,512]{1,0:T(8,128)(2,1)}, bf16[256,512]{1,0:T(8,128)(2,1)S(1)}, u32[]{:S(2)}, u32[]{:S(2)}) collective-permute-start(bf16[256,512]{1,0:T(8,128)(2,1)} %get-tuple-element.26), channel_id=1, source_target_pairs={{0,6},{1,7},{2,0},{3,1},{4,2},{5,3},{6,4},{7,5},{8,14},{9,15},{10,... | collective-permute-start | bytes 786440 | tf_op jit(solution)/shard_map/ppermute | solution.py:700
  30.9 37.5 %all-to-all-start.1 = ((bf16[32,288,128]{2,1,0:T(8,128)(2,1)}), bf16[32,288,128]{2,1,0:T(8,128)(2,1)S(1)}, u32[]{:S(2)}, u32[]{:S(2)}) async-start(bf16[32,288,128]{2,1,0:T(8,128)(2,1)} %pack_small.1), calls=%async_computation.1 | async-start | bytes 4718592 | tf_op jit(solution)/shard_map/all_to_all | solution.py:680
  38.4 13.6 %collective-permute-start.2 = (bf16[256,512]{1,0:T(8,128)(2,1)}, bf16[256,512]{1,0:T(8,128)(2,1)S(1)}, u32[]{:S(2)}, u32[]{:S(2)}) collective-permute-start(bf16[256,512]{1,0:T(8,128)(2,1)} %get-tuple-element.30), channel_id=1, source_target_pairs={{0,3},{1,2},{2,5},{3,4},{4,7},{5,6},{6,1},{7,0},{8,11},{9,10},{10,... | collective-permute-start | bytes 786440 | tf_op jit(solution)/shard_map/ppermute | solution.py:700
  39.5 12.5 %collective-permute-start.3 = (bf16[256,512]{1,0:T(8,128)(2,1)}, bf16[256,512]{1,0:T(8,128)(2,1)S(1)}, u32[]{:S(2)}, u32[]{:S(2)}) collective-permute-start(bf16[256,512]{1,0:T(8,128)(2,1)} %get-tuple-element.31), channel_id=1, source_target_pairs={{0,7},{1,6},{2,1},{3,0},{4,3},{5,2},{6,5},{7,4},{8,15},{9,14},{10,... | collective-permute-start | bytes 786440 | tf_op jit(solution)/shard_map/ppermute | solution.py:700
  40.1 14.9 %collective-permute-start.4 = (bf16[256,512]{1,0:T(8,128)(2,1)}, bf16[256,512]{1,0:T(8,128)(2,1)S(1)}, u32[]{:S(2)}, u32[]{:S(2)}) collective-permute-start(bf16[256,512]{1,0:T(8,128)(2,1)} %get-tuple-element.32), channel_id=1, source_target_pairs={{0,4},{1,5},{2,6},{3,7},{4,0},{5,1},{6,2},{7,3},{8,12},{9,13},{10,... | collective-permute-start | bytes 786440 | tf_op jit(solution)/shard_map/ppermute | solution.py:700
  42.1 18.0 %collective-permute-start.5 = (bf16[256,512]{1,0:T(8,128)(2,1)}, bf16[256,512]{1,0:T(8,128)(2,1)S(1)}, u32[]{:S(2)}, u32[]{:S(2)}) collective-permute-start(bf16[256,512]{1,0:T(8,128)(2,1)} %get-tuple-element.33), channel_id=1, source_target_pairs={{0,5},{1,4},{2,7},{3,6},{4,1},{5,0},{6,3},{7,2},{8,13},{9,12},{10,... | collective-permute-start | bytes 786440 | tf_op jit(solution)/shard_map/ppermute | solution.py:700
  43.7 16.4 %collective-permute-start.6 = (bf16[256,512]{1,0:T(8,128)(2,1)}, bf16[256,512]{1,0:T(8,128)(2,1)}, u32[]{:S(2)}, u32[]{:S(2)}) collective-permute-start(bf16[256,512]{1,0:T(8,128)(2,1)} %get-tuple-element.34), channel_id=1, source_target_pairs={{0,1},{1,0},{2,3},{3,2},{4,5},{5,4},{6,7},{7,6},{8,9},{9,8},{10,11... | collective-permute-start | bytes 786440 | tf_op jit(solution)/shard_map/ppermute | solution.py:700
  64.0 16.3 %copy-start.24 = (bf16[256,512]{1,0:T(8,128)(2,1)S(1)}, bf16[256,512]{1,0:T(8,128)(2,1)}, u32[]{:S(2)}) copy-start(bf16[256,512]{1,0:T(8,128)(2,1)} %get-tuple-element.43) | copy-start | bytes 786436
  64.1 19.2 %copy-start.23 = (bf16[256,512]{1,0:T(8,128)(2,1)S(1)}, bf16[256,512]{1,0:T(8,128)(2,1)}, u32[]{:S(2)}) copy-start(bf16[256,512]{1,0:T(8,128)(2,1)} %get-tuple-element.44) | copy-start | bytes 786436
  64.1 23.3 %copy-start.22 = (bf16[256,512]{1,0:T(8,128)(2,1)S(1)}, bf16[256,512]{1,0:T(8,128)(2,1)}, u32[]{:S(2)}) copy-start(bf16[256,512]{1,0:T(8,128)(2,1)} %get-tuple-element.45) | copy-start | bytes 786436
  64.1 23.3 %copy-start.6 = (bf16[256,512]{1,0:T(8,128)(2,1)S(1)}, bf16[256,512]{1,0:T(8,128)(2,1)}, u32[]{:S(2)}) copy-start(bf16[256,512]{1,0:T(8,128)(2,1)} %get-tuple-element.35.rest_12_) | copy-start | bytes 786436
  69.8 56.5 %all-to-all-start.2 = ((bf16[32,128,512]{2,1,0:T(8,128)(2,1)}), bf16[32,128,512]{2,1,0:T(8,128)(2,1)}, u32[]{:S(2)}, u32[]{:S(2)}) async-start(bf16[32,128,512]{2,1,0:T(8,128)(2,1)} %pack_x.2), calls=%async_computation.2 | async-start | bytes 8388608 | tf_op jit(solution)/shard_map/all_to_all | solution.py:680
  77.5 9.8 %collective-permute-start.8 = (bf16[256,512]{1,0:T(8,128)(2,1)}, bf16[256,512]{1,0:T(8,128)(2,1)S(1)}, u32[]{:S(2)}, u32[]{:S(2)}) collective-permute-start(bf16[256,512]{1,0:T(8,128)(2,1)} %get-tuple-element.40), channel_id=1, source_target_pairs={{0,6},{1,7},{2,0},{3,1},{4,2},{5,3},{6,4},{7,5},{8,14},{9,15},{10,... | collective-permute-start | bytes 786440 | tf_op jit(solution)/shard_map/ppermute | solution.py:700
  78.6 8.8 %collective-permute-start.9 = (bf16[256,512]{1,0:T(8,128)(2,1)}, bf16[256,512]{1,0:T(8,128)(2,1)S(1)}, u32[]{:S(2)}, u32[]{:S(2)}) collective-permute-start(bf16[256,512]{1,0:T(8,128)(2,1)} %get-tuple-element.41), channel_id=1, source_target_pairs={{0,3},{1,2},{2,5},{3,4},{4,7},{5,6},{6,1},{7,0},{8,11},{9,10},{10,... | collective-permute-start | bytes 786440 | tf_op jit(solution)/shard_map/ppermute | solution.py:700
  78.6 42.1 %collective-permute-start.10 = (bf16[256,512]{1,0:T(8,128)(2,1)}, bf16[256,512]{1,0:T(8,128)(2,1)S(1)}, u32[]{:S(2)}, u32[]{:S(2)}) collective-permute-start(bf16[256,512]{1,0:T(8,128)(2,1)} %get-tuple-element.42), channel_id=1, source_target_pairs={{0,7},{1,6},{2,1},{3,0},{4,3},{5,2},{6,5},{7,4},{8,15},{9,14},{10,... | collective-permute-start | bytes 786440 | tf_op jit(solution)/shard_map/ppermute | solution.py:700
  80.3 40.4 %collective-permute-start.11 = (bf16[256,512]{1,0:T(8,128)(2,1)S(1)}, bf16[256,512]{1,0:T(8,128)(2,1)S(1)}, u32[]{:S(2)}, u32[]{:S(2)}) collective-permute-start(bf16[256,512]{1,0:T(8,128)(2,1)S(1)} %copy-done.24), channel_id=1, source_target_pairs={{0,4},{1,5},{2,6},{3,7},{4,0},{5,1},{6,2},{7,3},{8,12},{9,13},{10,... | collective-permute-start | bytes 786440 | tf_op jit(solution)/shard_map/ppermute | solution.py:700
  83.3 37.5 %collective-permute-start.12 = (bf16[256,512]{1,0:T(8,128)(2,1)S(1)}, bf16[256,512]{1,0:T(8,128)(2,1)S(1)}, u32[]{:S(2)}, u32[]{:S(2)}) collective-permute-start(bf16[256,512]{1,0:T(8,128)(2,1)S(1)} %copy-done.23), channel_id=1, source_target_pairs={{0,5},{1,4},{2,7},{3,6},{4,1},{5,0},{6,3},{7,2},{8,13},{9,12},{10,... | collective-permute-start | bytes 786440 | tf_op jit(solution)/shard_map/ppermute | solution.py:700
  87.3 11.1 %copy-start.11 = (bf16[256,512]{1,0:T(8,128)(2,1)}, bf16[256,512]{1,0:T(8,128)(2,1)S(1)}, u32[]{:S(2)}) copy-start(bf16[256,512]{1,0:T(8,128)(2,1)S(1)} %collective-permute-done.8.rest_1_) | copy-start | bytes 786436
  87.3 33.4 %collective-permute-start.13 = (bf16[256,512]{1,0:T(8,128)(2,1)S(1)}, bf16[256,512]{1,0:T(8,128)(2,1)S(1)}, u32[]{:S(2)}, u32[]{:S(2)}) collective-permute-start(bf16[256,512]{1,0:T(8,128)(2,1)S(1)} %copy-done.22), channel_id=1, source_target_pairs={{0,1},{1,0},{2,3},{3,2},{4,5},{5,4},{6,7},{7,6},{8,9},{9,8},{10,11... | collective-permute-start | bytes 786440 | tf_op jit(solution)/shard_map/ppermute | solution.py:700
  87.4 33.4 %collective-permute-start.7 = (bf16[256,512]{1,0:T(8,128)(2,1)S(1)}, bf16[256,512]{1,0:T(8,128)(2,1)S(1)}, u32[]{:S(2)}, u32[]{:S(2)}) collective-permute-start(bf16[256,512]{1,0:T(8,128)(2,1)S(1)} %copy-done.6), channel_id=1, source_target_pairs={{0,2},{1,3},{2,4},{3,5},{4,6},{5,7},{6,0},{7,1},{8,10},{9,11},{10,... | collective-permute-start | bytes 786440 | tf_op jit(solution)/shard_map/ppermute | solution.py:700
  188.8 16.3 %all-to-all-start.4 = ((bf16[16,16,1152]{2,1,0:T(8,128)(2,1)}), bf16[16,16,1152]{2,1,0:T(8,128)(2,1)S(1)}, u32[]{:S(2)}, u32[]{:S(2)}) async-start(bf16[16,16,1152]{2,1,0:T(8,128)(2,1)} %leaving.1.refs_12_), calls=%async_computation.4 | async-start | bytes 1179648 | tf_op jit(solution)/shard_map/all_to_all | solution.py:680
  208.1 17.6 %all-to-all-start.5 = ((bf16[16,16,1024]{2,1,0:T(8,128)(2,1)}), bf16[16,16,1024]{2,1,0:T(8,128)(2,1)S(1)}, u32[]{:S(2)}, u32[]{:S(2)}) async-start(bf16[16,16,1024]{2,1,0:T(8,128)(2,1)} %scan_owners.1.refs_12_), calls=%async_computation.5 | async-start | bytes 1048576 | tf_op jit(solution)/shard_map/all_to_all | solution.py:680
  (21 other events, 65.0 us)

commit v4 on v3

--- a/solution.py
+++ b/solution.py
@@ -151,7 +151,7 @@
             pltpu.VMEM((2 * OWNERS, TAG_ROWS, STATE), BF16),
             pltpu.SemaphoreType.DMA((1,)),
         ],
-        compiler_params=params(),
+        compiler_params=params(20),
         name="find_source",
     )(small)
 
@@ -469,7 +469,7 @@
                 square,
                 square,
                 pl.BlockSpec((RUN, 8, width), lambda k, src: (place(k), 0, half)),
-                pl.BlockSpec(spread_four.shape[:2] + (width,), lambda k, src: (0, 0, half)),
+                pl.BlockSpec((2, PIECE, width), lambda k, src: (0, 0, half)),
                 pl.BlockSpec((1, width), lambda k, src: (0, half)),
                 ANY,
             ],
@@ -634,11 +634,11 @@
     scales = scale_ref[...].reshape(rows, PIECE)
     for group in range(WIDTH // GROUP):
         cols = slice(group * GROUP, (group + 1) * GROUP)
-        y_off = dot(scales, spread_ref[BEFORE, :, cols]) * dot(c, enter_ref[0:STATE, cols])
+        y_off = dot(scales, spread_ref[BEFORE - 2, :, cols]) * dot(c, enter_ref[0:STATE, cols])
         start = group % 2 * GROUP
         y = (ya_ref if group < 2 else yb_ref)[:, :, start : start + GROUP].reshape(rows, GROUP)
         y_out[:, cols] = (y + y_off).astype(BF16)
-        g_off = dot(scales, spread_ref[AFTER, :, cols]) * dot(b, enter_ref[STATE:, cols])
+        g_off = dot(scales, spread_ref[AFTER - 2, :, cols]) * dot(b, enter_ref[STATE:, cols])
         g_out[:, cols] = (g_ref[:, :, cols].reshape(rows, GROUP) + g_off).astype(BF16)
 
 
@@ -659,7 +659,7 @@
             wide,
             pl.BlockSpec((2 * STATE, WIDTH), lambda k: (0, 0)),
             square,
-            pl.BlockSpec(spread_four.shape, lambda k: (0, 0, 0)),
+            pl.BlockSpec((2, PIECE, WIDTH), lambda k: (1, 0, 0)),
         ],
         out_specs=[pl.BlockSpec((RUN * PIECE, WIDTH), lambda k: (k, 0))] * 2,
         out_shape=[out, out],

time: 239 us -> 238 us (level)
    unnamed x52 -> x54, local copies, waits for them, and re-layouts: 6.48 us -> 5.61 us
where the time goes in v4:
time: 238 us; the launch traced here: 234 us
  Pallas kernels  86.6 us (36%)
  blocking collectives  54.7 us (23%)
  starting transfers between devices  48.9 us (21%)
  waiting for transfers between devices  30.2 us (13%)
  local copies, waits for them, and re-layouts  9.01 us (4%)
  other arithmetic  3.46 us (1%)
    all_to_all x1, blocking collectives, to_owners(): return lax.all_to_all(value, 'ctx', split_axis=0, concat_axis=0, tiled=True)  54.7 us
    pallas_call x3, Pallas kernels, local_call(): pl.pallas_call(skip_src(kernel), grid_spec=pltpu.PrefetchScalarGridSpec(n...  36.2 us
    all_to_all x4, starting transfers between devices, to_owners(): return lax.all_to_all(value, 'ctx', split_axis=0, concat_axis=0, tiled=True)  28.4 us
    ppermute x14, waiting for transfers between devices, body(): arrived[half].append(lax.ppermute(piece, 'head', pairs))  24.2 us
    ppermute x14, starting transfers between devices, body(): arrived[half].append(lax.ppermute(piece, 'head', pairs))  16 us
    pallas_call x1, Pallas kernels, finish(): pl.pallas_call(finish_kernel, grid=(pieces // RUN,), in_specs=[square, sq...  9.99 us
    pallas_call x1, Pallas kernels, decays(): pl.pallas_call(decay_kernel, in_specs=[SMEM, ANY, WHOLE, WHOLE, WHOLE], o...  7.22 us
    pallas_call x1, Pallas kernels, leaving(): pl.pallas_call(leaving_kernel, grid=(1,), in_specs=[SMEM, ANY, ANY, WHOLE...  6.79 us
  transfers between devices with their start and end apart: 19, of which 6 were waited for; matrix products, arithmetic and copies ran while one was open for 3% of the time, Pallas kernels for 27%

profile of v4, /device:TPU:98, one launch (start us, length us, event | category | flops | bytes accessed | tf_op | source)
XLA Modules:
  0.0 233.9 jit_solution(10922964182375594105)
XLA Ops:
  0.6 2.5 %gather_small.1 = bf16[8,2,272,128]{3,2,1,0:T(8,128)(2,1)} custom-call(bf16[256,1024]{1,0:T(8,128)(2,1)} %b_ref.1, bf16[256,1024]{1,0:T(8,128)(2,1)} %c_ref.1, bf16[256,128]{1,0:T(8,128)(2,1)} %dt_ref.1), custom_call_target="tpu_custom_call" | custom-call | tf_op jit(solution)/shard_map/gather_small/pallas_call | solution.py:81
  3.1 4.5 %all-to-all-start = ((bf16[8,2,272,128]{3,2,1,0:T(8,128)(2,1)}), bf16[8,2,272,128]{3,2,1,0:T(8,128)(2,1)S(1)}, u32[]{:S(2)}, u32[]{:S(2)}) async-start(bf16[8,2,272,128]{3,2,1,0:T(8,128)(2,1)} %gather_small.1), calls=%async_computation | async-start | bytes 2228224 | tf_op jit(solution)/shard_map/all_to_all | solution.py:693
  8.3 3.1 %cut.2 = (bf16[256,512]{1,0:T(8,128)(2,1)}, bf16[256,512]{1,0:T(8,128)(2,1)}, bf16[256,512]{1,0:T(8,128)(2,1)}, bf16[256,512]{1,0:T(8,128)(2,1)}, bf16[256,512]{...) custom-call(s32[7]{0:T(128)} %stack.46.dest_ref, bf16[256,8192]{1,0:T(8,128)(2,1)} %x_ref.7), custom_call_target="tpu_custom_call" | custom-call | tf_op jit(solution)/shard_map/cut/pallas_call | solution.py:179
  14.8 12.5 %collective-permute-done.rest_0_ = bf16[256,512]{1,0:T(8,128)(2,1)S(1)} collective-permute-done((bf16[256,512]{1,0:T(8,128)(2,1)}, bf16[256,512]{1,0:T(8,128)(2,1)S(1)}, u32[]{:S(2)}, u32[]{:S(2)}) %collective-permute-start) | collective-permute-done | bytes 262176 | tf_op jit(solution)/shard_map/ppermute | solution.py:700
  30.9 7.5 %all-to-all-start.1 = ((bf16[32,288,128]{2,1,0:T(8,128)(2,1)}), bf16[32,288,128]{2,1,0:T(8,128)(2,1)S(1)}, u32[]{:S(2)}, u32[]{:S(2)}) async-start(bf16[32,288,128]{2,1,0:T(8,128)(2,1)} %pack_small.1), calls=%async_computation.1 | async-start | bytes 4718592 | tf_op jit(solution)/shard_map/all_to_all | solution.py:680
  43.9 3.2 %cut.3 = (bf16[256,512]{1,0:T(8,128)(2,1)}, bf16[256,512]{1,0:T(8,128)(2,1)}, bf16[256,512]{1,0:T(8,128)(2,1)}, bf16[256,512]{1,0:T(8,128)(2,1)}, bf16[256,512]{...) custom-call(s32[7]{0:T(128)} %stack.46.dest_ref, bf16[256,8192]{1,0:T(8,128)(2,1)} %x_ref.7), custom_call_target="tpu_custom_call" | custom-call | tf_op jit(solution)/shard_map/cut/pallas_call | solution.py:179
  52.0 3.0 %collective-permute-done.4.rest_4_ = bf16[256,512]{1,0:T(8,128)(2,1)S(1)} collective-permute-done((bf16[256,512]{1,0:T(8,128)(2,1)}, bf16[256,512]{1,0:T(8,128)(2,1)S(1)}, u32[]{:S(2)}, u32[]{:S(2)}) %collective-permute-start.4) | collective-permute-done | bytes 262176 | tf_op jit(solution)/shard_map/ppermute | solution.py:700
  55.1 5.0 %collective-permute-done.5.rest_5_ = bf16[256,512]{1,0:T(8,128)(2,1)S(1)} collective-permute-done((bf16[256,512]{1,0:T(8,128)(2,1)}, bf16[256,512]{1,0:T(8,128)(2,1)S(1)}, u32[]{:S(2)}, u32[]{:S(2)}) %collective-permute-start.5) | collective-permute-done | bytes 262176 | tf_op jit(solution)/shard_map/ppermute | solution.py:700
  60.8 3.2 %pack_x.2 = bf16[32,128,512]{2,1,0:T(8,128)(2,1)} custom-call(s32[16]{0:T(128)} %multiply_add_fusion.slot_ref, s32[8]{0:T(128)} %stack.49.from_ref, bf16[256,8192]{1,0:T(8,128)(2,1)} %x_ref.7, bf16[256,512]{1,0:T(8,128)(2,1)} %copy-done.5, bf16[256,512]{1,0:T(8,128)(2,1)} %copy-done.6, bf16[256,512]{1,0:T(8,128)(2,1)} %copy-done.8, ...), custom_call_target="tpu_custom_call" | custom-call | tf_op jit(solution)/shard_map/pack_x/pallas_call | solution.py:216
  64.1 4.3 %all-to-all-done.1.small_ref = bf16[32,288,128]{2,1,0:T(8,128)(2,1)S(1)} async-done(((bf16[32,288,128]{2,1,0:T(8,128)(2,1)}), bf16[32,288,128]{2,1,0:T(8,128)(2,1)S(1)}, u32[]{:S(2)}, u32[]{:S(2)}) %all-to-all-start.1) | async-done | bytes 2359328 | tf_op jit(solution)/shard_map/all_to_all | solution.py:680
  68.4 7.7 %all-to-all-start.2 = ((bf16[32,128,512]{2,1,0:T(8,128)(2,1)}), bf16[32,128,512]{2,1,0:T(8,128)(2,1)}, u32[]{:S(2)}, u32[]{:S(2)}) async-start(bf16[32,128,512]{2,1,0:T(8,128)(2,1)} %pack_x.2), calls=%async_computation.2 | async-start | bytes 8388608 | tf_op jit(solution)/shard_map/all_to_all | solution.py:680
  78.9 3.0 %collective-permute-start.11 = (bf16[256,512]{1,0:T(8,128)(2,1)S(1)}, bf16[256,512]{1,0:T(8,128)(2,1)S(1)}, u32[]{:S(2)}, u32[]{:S(2)}) collective-permute-start(bf16[256,512]{1,0:T(8,128)(2,1)S(1)} %copy-done.25), channel_id=1, source_target_pairs={{0,4},{1,5},{2,6},{3,7},{4,0},{5,1},{6,2},{7,3},{8,12},{9,13},{10,... | collective-permute-start | bytes 786440 | tf_op jit(solution)/shard_map/ppermute | solution.py:700
  82.3 3.6 %collective-permute-done.8.rest_1_ = bf16[256,512]{1,0:T(8,128)(2,1)S(1)} collective-permute-done((bf16[256,512]{1,0:T(8,128)(2,1)}, bf16[256,512]{1,0:T(8,128)(2,1)S(1)}, u32[]{:S(2)}, u32[]{:S(2)}) %collective-permute-start.8) | collective-permute-done | bytes 262176 | tf_op jit(solution)/shard_map/ppermute | solution.py:700
  88.9 7.2 %decays.1 = (bf16[16,128,128]{2,1,0:T(8,128)(2,1)}, bf16[16,128,128]{2,1,0:T(8,128)(2,1)}, bf16[16,128,128]{2,1,0:T(8,128)(2,1)}, bf16[16,128,128]{2,1,0:T(8,128...) custom-call(s32[1,128]{1,0:T(1,128)} %copy-done.1, ...), custom_call_target="tpu_custom_call" | custom-call | tf_op jit(solution)/shard_map/decays/pallas_call | solution.py:338
  96.1 6.3 %leaving_gradient.1.rest_7_.refs_9_.g_ref = bf16[128,1024]{1,0:T(8,128)(2,1)} custom-call(bf16[2048,1024]{1,0:T(8,128)(2,1)} %refs_2_.1, bf16[16,128,128]{2,1,0:T(8,128)(2,1)} %get-tuple-element.46.keys_ref.refs_1_, bf16[16,128,128]{2,1,0:T(8,128)(2,1)} %get-tuple-element.38.scale_ref.refs_5_.refs_8_, ...), custom_call_target="tpu_custom_call" | custom-call | tf_op jit(solution)/shard_map/leaving_gradient/pallas_call | solution.py:549
  102.5 15.7 %backward_local.1.rest_0_.g_ref = bf16[16,128,1024]{2,1,0:T(8,128)(2,1)} custom-call(s32[1,128]{1,0:T(1,128)} %copy-done.1, bf16[16,128,128]{2,1,0:T(8,128)(2,1)} %get-tuple-element.27.refs_0_.b_ref, bf16[16,128,128]{2,1,0:T(8,128)(2,1)} %get-tuple-element.46.keys_ref.refs_1_, bf16[2048,1024]{1,0:T(8,128)(2,1)} %refs_2_.1, ...), custom_call_target="tpu_custom_call" | custom-call | tf_op jit(solution)/shard_map/backward_local/pallas_call | solution.py:459
  119.9 3.2 %pack_x.3.value_ref = bf16[32,128,512]{2,1,0:T(8,128)(2,1)} custom-call(s32[16]{0:T(128)} %multiply_add_fusion.slot_ref, s32[8]{0:T(128)} %stack.49.from_ref, bf16[256,8192]{1,0:T(8,128)(2,1)} %x_ref.7, bf16[256,512]{1,0:T(8,128)(2,1)} %copy-done.18, bf16[256,512]{1,0:T(8,128)(2,1)} %copy-done.12, bf16[256,512]{1,0:T(8,128)(2,1)} %copy-done.13, ...), custom_call_target="tpu_custom_call" | custom-call | tf_op jit(solution)/shard_map/pack_x/pallas_call | solution.py:216
  124.8 54.7 %all_to_all.30.xb_ref.refs_2_.refs_3_.refs_4_.refs_5_ = bf16[32,128,512]{2,1,0:T(8,128)(2,1)} all-to-all(bf16[32,128,512]{2,1,0:T(8,128)(2,1)} %hold.1), channel_id=1, replica_groups=mesh['ctx'=16,'head'=8] {'ctx'}, dimensions={0} | all-to-all | bytes 8388608 | tf_op jit(solution)/shard_map/all_to_all | solution.py:680
  179.5 6.8 %leaving.1.refs_12_ = bf16[16,16,1152]{2,1,0:T(8,128)(2,1)} custom-call(s32[1,128]{1,0:T(1,128)} %copy-done.1, bf16[32,128,512]{2,1,0:T(8,128)(2,1)} %all-to-all-done.2.xa_ref.refs_2_.refs_3_.refs_4_.refs_5_, bf16[32,128,512]{2,1,0:T(8,128)(2,1)} %all_to_all.30.xb_ref.refs_2_.refs_3_.refs_4_.refs_5_, ...), custom_call_target="tpu_custom_call" | custom-call | tf_op jit(solution)/shard_map/leaving/pallas_call | solution.py:589
  186.3 5.9 %all-to-all-start.4 = ((bf16[16,16,1152]{2,1,0:T(8,128)(2,1)}), bf16[16,16,1152]{2,1,0:T(8,128)(2,1)S(1)}, u32[]{:S(2)}, u32[]{:S(2)}) async-start(bf16[16,16,1152]{2,1,0:T(8,128)(2,1)} %leaving.1.refs_12_), calls=%async_computation.4 | async-start | bytes 1179648 | tf_op jit(solution)/shard_map/all_to_all | solution.py:680
  192.2 10.3 %forward_local.2.after_ref.ya_ref = bf16[16,128,512]{2,1,0:T(8,128)(2,1)} custom-call(s32[1,128]{1,0:T(1,128)} %copy-done.1, bf16[16,128,128]{2,1,0:T(8,128)(2,1)} %get-tuple-element.28.refs_0_.c_ref, bf16[16,128,128]{2,1,0:T(8,128)(2,1)} %get-tuple-element.29.keys_ref.refs_1_, bf16[32,128,512]{2,1,0:T(8,128)(2,1)} %all-to-all-done.2.xa_ref.refs_2_.refs_3_.refs_4_.refs_5_, ...), custom_call_target="tpu_custom_call" | custom-call | tf_op jit(solution)/shard_map/forward_local/pallas_call | solution.py:459
  205.5 7.3 %all-to-all-start.5 = ((bf16[16,16,1024]{2,1,0:T(8,128)(2,1)}), bf16[16,16,1024]{2,1,0:T(8,128)(2,1)S(1)}, u32[]{:S(2)}, u32[]{:S(2)}) async-start(bf16[16,16,1024]{2,1,0:T(8,128)(2,1)} %scan_owners.1.refs_12_), calls=%async_computation.5 | async-start | bytes 1048576 | tf_op jit(solution)/shard_map/all_to_all | solution.py:680
  212.8 10.3 %forward_local.3.yb_ref = bf16[16,128,512]{2,1,0:T(8,128)(2,1)} custom-call(s32[1,128]{1,0:T(1,128)} %copy-done.1, bf16[16,128,128]{2,1,0:T(8,128)(2,1)} %get-tuple-element.28.refs_0_.c_ref, bf16[16,128,128]{2,1,0:T(8,128)(2,1)} %get-tuple-element.29.keys_ref.refs_1_, bf16[32,128,512]{2,1,0:T(8,128)(2,1)} %all_to_all.30.xb_ref.refs_2_.refs_3_.refs_4_.refs_5_, ...), custom_call_target="tpu_custom_call" | custom-call | tf_op jit(solution)/shard_map/forward_local/pallas_call | solution.py:459
  223.9 10.0 %finish.1 = (bf16[2048,1024]{1,0:T(8,128)(2,1)}, bf16[2048,1024]{1,0:T(8,128)(2,1)}) custom-call(bf16[16,128,128]{2,1,0:T(8,128)(2,1)} %get-tuple-element.27.refs_0_.b_ref, bf16[16,128,128]{2,1,0:T(8,128)(2,1)} %get-tuple-element.28.refs_0_.c_ref, bf16[16,128,512]{2,1,0:T(8,128)(2,1)} %forward_local.2.after_ref.ya_ref, ...), custom_call_target="tpu_custom_call" | custom-call | tf_op jit(solution)/shard_map/finish/pallas_call | solution.py:651
  (102 shorter events, 32.0 us)
Async XLA Ops:
  3.1 24.2 %all-to-all-start = ((bf16[8,2,272,128]{3,2,1,0:T(8,128)(2,1)}), bf16[8,2,272,128]{3,2,1,0:T(8,128)(2,1)S(1)}, u32[]{:S(2)}, u32[]{:S(2)}) async-start(bf16[8,2,272,128]{3,2,1,0:T(8,128)(2,1)} %gather_small.1), calls=%async_computation | async-start | bytes 2228224 | tf_op jit(solution)/shard_map/all_to_all | solution.py:693
  11.4 15.9 %collective-permute-start = (bf16[256,512]{1,0:T(8,128)(2,1)}, bf16[256,512]{1,0:T(8,128)(2,1)S(1)}, u32[]{:S(2)}, u32[]{:S(2)}) collective-permute-start(bf16[256,512]{1,0:T(8,128)(2,1)} %get-tuple-element.25), channel_id=1, source_target_pairs={{0,2},{1,3},{2,4},{3,5},{4,6},{5,7},{6,0},{7,1},{8,10},{9,11},{10,... | collective-permute-start | bytes 786440 | tf_op jit(solution)/shard_map/ppermute | solution.py:700
  11.5 15.8 %collective-permute-start.1 = (bf16[256,512]{1,0:T(8,128)(2,1)}, bf16[256,512]{1,0:T(8,128)(2,1)S(1)}, u32[]{:S(2)}, u32[]{:S(2)}) collective-permute-start(bf16[256,512]{1,0:T(8,128)(2,1)} %get-tuple-element.26), channel_id=1, source_target_pairs={{0,6},{1,7},{2,0},{3,1},{4,2},{5,3},{6,4},{7,5},{8,14},{9,15},{10,... | collective-permute-start | bytes 786440 | tf_op jit(solution)/shard_map/ppermute | solution.py:700
  30.9 37.5 %all-to-all-start.1 = ((bf16[32,288,128]{2,1,0:T(8,128)(2,1)}), bf16[32,288,128]{2,1,0:T(8,128)(2,1)S(1)}, u32[]{:S(2)}, u32[]{:S(2)}) async-start(bf16[32,288,128]{2,1,0:T(8,128)(2,1)} %pack_small.1), calls=%async_computation.1 | async-start | bytes 4718592 | tf_op jit(solution)/shard_map/all_to_all | solution.py:680
  38.4 13.6 %collective-permute-start.2 = (bf16[256,512]{1,0:T(8,128)(2,1)}, bf16[256,512]{1,0:T(8,128)(2,1)S(1)}, u32[]{:S(2)}, u32[]{:S(2)}) collective-permute-start(bf16[256,512]{1,0:T(8,128)(2,1)} %get-tuple-element.30), channel_id=1, source_target_pairs={{0,3},{1,2},{2,5},{3,4},{4,7},{5,6},{6,1},{7,0},{8,11},{9,10},{10,... | collective-permute-start | bytes 786440 | tf_op jit(solution)/shard_map/ppermute | solution.py:700
  39.5 12.4 %collective-permute-start.3 = (bf16[256,512]{1,0:T(8,128)(2,1)}, bf16[256,512]{1,0:T(8,128)(2,1)S(1)}, u32[]{:S(2)}, u32[]{:S(2)}) collective-permute-start(bf16[256,512]{1,0:T(8,128)(2,1)} %get-tuple-element.31), channel_id=1, source_target_pairs={{0,7},{1,6},{2,1},{3,0},{4,3},{5,2},{6,5},{7,4},{8,15},{9,14},{10,... | collective-permute-start | bytes 786440 | tf_op jit(solution)/shard_map/ppermute | solution.py:700
  40.1 14.9 %collective-permute-start.4 = (bf16[256,512]{1,0:T(8,128)(2,1)}, bf16[256,512]{1,0:T(8,128)(2,1)S(1)}, u32[]{:S(2)}, u32[]{:S(2)}) collective-permute-start(bf16[256,512]{1,0:T(8,128)(2,1)} %get-tuple-element.32), channel_id=1, source_target_pairs={{0,4},{1,5},{2,6},{3,7},{4,0},{5,1},{6,2},{7,3},{8,12},{9,13},{10,... | collective-permute-start | bytes 786440 | tf_op jit(solution)/shard_map/ppermute | solution.py:700
  42.1 18.0 %collective-permute-start.5 = (bf16[256,512]{1,0:T(8,128)(2,1)}, bf16[256,512]{1,0:T(8,128)(2,1)S(1)}, u32[]{:S(2)}, u32[]{:S(2)}) collective-permute-start(bf16[256,512]{1,0:T(8,128)(2,1)} %get-tuple-element.33), channel_id=1, source_target_pairs={{0,5},{1,4},{2,7},{3,6},{4,1},{5,0},{6,3},{7,2},{8,13},{9,12},{10,... | collective-permute-start | bytes 786440 | tf_op jit(solution)/shard_map/ppermute | solution.py:700
  43.7 16.4 %collective-permute-start.6 = (bf16[256,512]{1,0:T(8,128)(2,1)}, bf16[256,512]{1,0:T(8,128)(2,1)}, u32[]{:S(2)}, u32[]{:S(2)}) collective-permute-start(bf16[256,512]{1,0:T(8,128)(2,1)} %get-tuple-element.34), channel_id=1, source_target_pairs={{0,1},{1,0},{2,3},{3,2},{4,5},{5,4},{6,7},{7,6},{8,9},{9,8},{10,11... | collective-permute-start | bytes 786440 | tf_op jit(solution)/shard_map/ppermute | solution.py:700
  64.0 14.9 %copy-start.25 = (bf16[256,512]{1,0:T(8,128)(2,1)S(1)}, bf16[256,512]{1,0:T(8,128)(2,1)}, u32[]{:S(2)}) copy-start(bf16[256,512]{1,0:T(8,128)(2,1)} %get-tuple-element.43) | copy-start | bytes 786436
  64.1 17.8 %copy-start.24 = (bf16[256,512]{1,0:T(8,128)(2,1)S(1)}, bf16[256,512]{1,0:T(8,128)(2,1)}, u32[]{:S(2)}) copy-start(bf16[256,512]{1,0:T(8,128)(2,1)} %get-tuple-element.44) | copy-start | bytes 786436
  64.1 21.9 %copy-start.23 = (bf16[256,512]{1,0:T(8,128)(2,1)S(1)}, bf16[256,512]{1,0:T(8,128)(2,1)}, u32[]{:S(2)}) copy-start(bf16[256,512]{1,0:T(8,128)(2,1)} %get-tuple-element.45) | copy-start | bytes 786436
  64.1 21.9 %copy-start.7 = (bf16[256,512]{1,0:T(8,128)(2,1)S(1)}, bf16[256,512]{1,0:T(8,128)(2,1)}, u32[]{:S(2)}) copy-start(bf16[256,512]{1,0:T(8,128)(2,1)} %get-tuple-element.35.rest_12_) | copy-start | bytes 786436
  68.3 19.9 %copy-start = (bf16[32,288,128]{2,1,0:T(8,128)(2,1)}, bf16[32,288,128]{2,1,0:T(8,128)(2,1)S(1)}, u32[]{:S(2)}) copy-start(bf16[32,288,128]{2,1,0:T(8,128)(2,1)S(1)} %all-to-all-done.1.small_ref) | copy-start | bytes 7077892
  68.4 56.5 %all-to-all-start.2 = ((bf16[32,128,512]{2,1,0:T(8,128)(2,1)}), bf16[32,128,512]{2,1,0:T(8,128)(2,1)}, u32[]{:S(2)}, u32[]{:S(2)}) async-start(bf16[32,128,512]{2,1,0:T(8,128)(2,1)} %pack_x.2), calls=%async_computation.2 | async-start | bytes 8388608 | tf_op jit(solution)/shard_map/all_to_all | solution.py:680
  76.1 9.8 %collective-permute-start.8 = (bf16[256,512]{1,0:T(8,128)(2,1)}, bf16[256,512]{1,0:T(8,128)(2,1)S(1)}, u32[]{:S(2)}, u32[]{:S(2)}) collective-permute-start(bf16[256,512]{1,0:T(8,128)(2,1)} %get-tuple-element.40), channel_id=1, source_target_pairs={{0,6},{1,7},{2,0},{3,1},{4,2},{5,3},{6,4},{7,5},{8,14},{9,15},{10,... | collective-permute-start | bytes 786440 | tf_op jit(solution)/shard_map/ppermute | solution.py:700
  77.2 8.8 %collective-permute-start.9 = (bf16[256,512]{1,0:T(8,128)(2,1)}, bf16[256,512]{1,0:T(8,128)(2,1)S(1)}, u32[]{:S(2)}, u32[]{:S(2)}) collective-permute-start(bf16[256,512]{1,0:T(8,128)(2,1)} %get-tuple-element.41), channel_id=1, source_target_pairs={{0,3},{1,2},{2,5},{3,4},{4,7},{5,6},{6,1},{7,0},{8,11},{9,10},{10,... | collective-permute-start | bytes 786440 | tf_op jit(solution)/shard_map/ppermute | solution.py:700
  77.2 41.0 %collective-permute-start.10 = (bf16[256,512]{1,0:T(8,128)(2,1)}, bf16[256,512]{1,0:T(8,128)(2,1)S(1)}, u32[]{:S(2)}, u32[]{:S(2)}) collective-permute-start(bf16[256,512]{1,0:T(8,128)(2,1)} %get-tuple-element.42), channel_id=1, source_target_pairs={{0,7},{1,6},{2,1},{3,0},{4,3},{5,2},{6,5},{7,4},{8,15},{9,14},{10,... | collective-permute-start | bytes 786440 | tf_op jit(solution)/shard_map/ppermute | solution.py:700
  78.9 39.3 %collective-permute-start.11 = (bf16[256,512]{1,0:T(8,128)(2,1)S(1)}, bf16[256,512]{1,0:T(8,128)(2,1)S(1)}, u32[]{:S(2)}, u32[]{:S(2)}) collective-permute-start(bf16[256,512]{1,0:T(8,128)(2,1)S(1)} %copy-done.25), channel_id=1, source_target_pairs={{0,4},{1,5},{2,6},{3,7},{4,0},{5,1},{6,2},{7,3},{8,12},{9,13},{10,... | collective-permute-start | bytes 786440 | tf_op jit(solution)/shard_map/ppermute | solution.py:700
  81.9 36.3 %collective-permute-start.12 = (bf16[256,512]{1,0:T(8,128)(2,1)S(1)}, bf16[256,512]{1,0:T(8,128)(2,1)S(1)}, u32[]{:S(2)}, u32[]{:S(2)}) collective-permute-start(bf16[256,512]{1,0:T(8,128)(2,1)S(1)} %copy-done.24), channel_id=1, source_target_pairs={{0,5},{1,4},{2,7},{3,6},{4,1},{5,0},{6,3},{7,2},{8,13},{9,12},{10,... | collective-permute-start | bytes 786440 | tf_op jit(solution)/shard_map/ppermute | solution.py:700
  85.9 32.3 %collective-permute-start.13 = (bf16[256,512]{1,0:T(8,128)(2,1)S(1)}, bf16[256,512]{1,0:T(8,128)(2,1)S(1)}, u32[]{:S(2)}, u32[]{:S(2)}) collective-permute-start(bf16[256,512]{1,0:T(8,128)(2,1)S(1)} %copy-done.23), channel_id=1, source_target_pairs={{0,1},{1,0},{2,3},{3,2},{4,5},{5,4},{6,7},{7,6},{8,9},{9,8},{10,11... | collective-permute-start | bytes 786440 | tf_op jit(solution)/shard_map/ppermute | solution.py:700
  86.0 32.3 %collective-permute-start.7 = (bf16[256,512]{1,0:T(8,128)(2,1)S(1)}, bf16[256,512]{1,0:T(8,128)(2,1)S(1)}, u32[]{:S(2)}, u32[]{:S(2)}) collective-permute-start(bf16[256,512]{1,0:T(8,128)(2,1)S(1)} %copy-done.7), channel_id=1, source_target_pairs={{0,2},{1,3},{2,4},{3,5},{4,6},{5,7},{6,0},{7,1},{8,10},{9,11},{10,... | collective-permute-start | bytes 786440 | tf_op jit(solution)/shard_map/ppermute | solution.py:700
  186.3 16.2 %all-to-all-start.4 = ((bf16[16,16,1152]{2,1,0:T(8,128)(2,1)}), bf16[16,16,1152]{2,1,0:T(8,128)(2,1)S(1)}, u32[]{:S(2)}, u32[]{:S(2)}) async-start(bf16[16,16,1152]{2,1,0:T(8,128)(2,1)} %leaving.1.refs_12_), calls=%async_computation.4 | async-start | bytes 1179648 | tf_op jit(solution)/shard_map/all_to_all | solution.py:680
  205.5 17.5 %all-to-all-start.5 = ((bf16[16,16,1024]{2,1,0:T(8,128)(2,1)}), bf16[16,16,1024]{2,1,0:T(8,128)(2,1)S(1)}, u32[]{:S(2)}, u32[]{:S(2)}) async-start(bf16[16,16,1024]{2,1,0:T(8,128)(2,1)} %scan_owners.1.refs_12_), calls=%async_computation.5 | async-start | bytes 1048576 | tf_op jit(solution)/shard_map/all_to_all | solution.py:680
  (22 other events, 73.4 us)

commit v5 on v4

--- a/solution.py
+++ b/solution.py
@@ -119,12 +119,12 @@
         pack_small_kernel,
         in_specs=[SMEM, SMEM, WHOLE] + [ANY] * len(after),
         out_specs=ANY,
-        out_shape=jax.ShapeDtypeStruct((2 * OWNERS, SENT_ROWS, STATE), BF16),
+        out_shape=pltpu.HBM((2 * OWNERS, SENT_ROWS, STATE), BF16),
         scratch_shapes=[
             pltpu.VMEM((2 * OWNERS, TAG_ROWS, STATE), BF16),
             pltpu.SemaphoreType.DMA((OWNERS + 1,)),
         ],
-        compiler_params=params(),
+        compiler_params=params(20),
         name="pack_small",
     )(slot, place, pieces, *after)
 
@@ -157,7 +157,7 @@
 
 
 def cut_kernel(half, dest_ref, x_ref, *rest):
-    count = len(SHIFTS)
+    count = PEERS
     outs, (held, sems) = rest[:count], rest[count:]
     ins, copies = [], []
     for i in range(count):
@@ -174,7 +174,7 @@
 
 
 def cut(half, dest, x_rows):
-    count = len(SHIFTS)
+    count = PEERS
     shape = (x_rows.shape[0], HALF)
     return pl.pallas_call(
         partial(cut_kernel, half),
@@ -190,17 +190,15 @@
     )(dest, x_rows)
 
 
-def pack_x_kernel(half, slot_ref, from_ref, x_ref, *rest):
-    arrived, (out_ref, held, sems) = rest[: len(SHIFTS)], rest[-3:]
-    count = len(arrived)
-    at = pl.multiple_of(from_ref[count] * WIDTH + half * HALF, HALF)
+def pack_x_kernel(slot_ref, from_ref, *rest):
+    arrived, (out_ref, held, sems) = rest[:PEERS], rest[-3:]
     ins, copies = [], []
-    for i in range(count + 1):
+    for i in range(PEERS):
         for r in range(2):
             n = 2 * i + r
             slot = slot_ref[from_ref[i] * 2 + r]
             rows = pl.ds(r * PIECE, PIECE)
-            piece = arrived[i].at[rows, :] if i < count else x_ref.at[rows, pl.ds(at, HALF)]
+            piece = arrived[i].at[rows, :]
             ins.append(pltpu.make_async_copy(piece, held.at[n], sems.at[0, n]))
             copies.append(pltpu.make_async_copy(held.at[n], out_ref.at[slot], sems.at[1, n]))
     for copy in ins:
@@ -212,19 +210,19 @@
         copy.wait()
 
 
-def pack_x(half, slot, origin, x_rows, arrived, after):
-    return pl.pallas_call(
-        partial(pack_x_kernel, half),
-        in_specs=[SMEM, SMEM] + [ANY] * (1 + len(arrived) + len(after)),
+def pack_x(slot, origin, arrived, after):
+    return pl.pallas_call(
+        pack_x_kernel,
+        in_specs=[SMEM, SMEM] + [ANY] * (len(arrived) + len(after)),
         out_specs=ANY,
-        out_shape=jax.ShapeDtypeStruct((2 * OWNERS, PIECE, HALF), BF16),
+        out_shape=pltpu.HBM((2 * OWNERS, PIECE, HALF), BF16),
         scratch_shapes=[
             pltpu.VMEM((2 * PEERS, PIECE, HALF), BF16),
             pltpu.SemaphoreType.DMA((2, 2 * PEERS)),
         ],
-        compiler_params=params(),
+        compiler_params=params(20),
         name="pack_x",
-    )(slot, origin, x_rows, *arrived, *after)
+    )(slot, origin, *arrived, *after)
 
 
 def hold_kernel(value_ref, *rest):
@@ -685,7 +683,7 @@
 ):
     head = lax.axis_index("head")
     me = lax.axis_index("ctx")
-    dest_heads = jnp.stack([partner(head, s) for s in SHIFTS]).astype(jnp.int32)
+    dest_heads = jnp.stack([partner(head, s) for s in SHIFTS] + [head]).astype(jnp.int32)
     origin = jnp.stack([source(head, s) for s in SHIFTS] + [head]).astype(jnp.int32)
     send_slot = destination // OWNERS * 2 + ranks(destination)
 
@@ -698,6 +696,7 @@
         for shift, piece in zip(SHIFTS, cuts[half]):
             pairs = [(h, partner(h, shift)) for h in range(PEERS)]
             arrived[half].append(lax.ppermute(piece, "head", pairs))
+        arrived[half].append(cuts[half][-1])
     small = small.reshape(OWNERS, SMALL_ROWS, STATE)
     small = pack_small(send_slot, destination % OWNERS, small, arrived[0][:EARLY])
     small = to_owners(small)
@@ -708,7 +707,7 @@
     skip = jnp.repeat(d_skip, HEAD_DIM).reshape(1, WIDTH)
     spread_four = spread(4)
     first = [seg, bias, alog, skip, spread_four, cuts[1][0]]
-    x_a = pack_x(0, send_slot, origin, x_rows, arrived[0], first)
+    x_a = pack_x(send_slot, origin, arrived[0], first)
     x_a = to_owners(x_a)
 
     src = find_source(small)
@@ -717,7 +716,7 @@
     g_state = leaving_gradient(ct, cotangent, scales, spread_four)
     g_local = backward_local(src, b, ct, cotangent, local, g_state)
 
-    x_b = pack_x(1, send_slot, origin, x_rows, arrived[1], [g_state])
+    x_b = pack_x(send_slot, origin, arrived[1], [g_state])
     x_slots = [x_a, to_owners(hold(x_b, [g_local]))]
     parts = leaving(src, x_slots, bt, scales, spread_four, g_state, total)
     y_a = forward_local(0, src, c, bt, x_slots, local, parts)

time: 238 us -> 249 us (1.046); the launches traced: 234 us -> 248 us
  starting transfers between devices: 48.9 us -> 59.1 us
  blocking collectives: 54.7 us -> 60.9 us
  other arithmetic: 3.46 us -> 0.84 us
    ppermute x14, starting transfers between devices: 16 us -> 26.5 us  [body(): arrived[half].append(lax.ppermute(piece, 'head', pairs))]
    all_to_all x1, blocking collectives: 54.7 us -> 60.9 us  [to_owners(): return lax.all_to_all(value, 'ctx', split_axis=0, concat_axis=0, tiled=True)]
    ppermute x14, waiting for transfers between devices: 24.2 us -> 29.8 us  [body(): arrived[half].append(lax.ppermute(piece, 'head', pairs))]
    all_to_all x4, waiting for transfers between devices: 5.96 us -> 0.58 us  [to_owners(): return lax.all_to_all(value, 'ctx', split_axis=0, concat_axis=0, tiled=True)]
    unnamed x54 -> x46, local copies, waits for them, and re-layouts: 5.61 us -> 6.05 us
  transfers between devices with their start and end apart: 19 -> 19, of which waited for: 6 -> 5; matrix products, arithmetic and copies ran while one was open for 3% -> 1% of each run, Pallas kernels for 27% -> 26%
where the time goes in v5:
time: 249 us; the launch traced here: 248 us
  Pallas kernels  88.4 us (36%)
  blocking collectives  60.9 us (24%)
  starting transfers between devices  59.1 us (24%)
  waiting for transfers between devices  30.4 us (12%)
  local copies, waits for them, and re-layouts  7.12 us (3%)
    all_to_all x1, blocking collectives, to_owners(): return lax.all_to_all(value, 'ctx', split_axis=0, concat_axis=0, tiled=True)  60.9 us
    pallas_call x3, Pallas kernels, local_call(): pl.pallas_call(skip_src(kernel), grid_spec=pltpu.PrefetchScalarGridSpec(n...  36.4 us
    ppermute x14, waiting for transfers between devices, body(): arrived[half].append(lax.ppermute(piece, 'head', pairs))  29.8 us
    all_to_all x4, starting transfers between devices, to_owners(): return lax.all_to_all(value, 'ctx', split_axis=0, concat_axis=0, tiled=True)  28.1 us
    ppermute x14, starting transfers between devices, body(): arrived[half].append(lax.ppermute(piece, 'head', pairs))  26.5 us
    pallas_call x1, Pallas kernels, finish(): pl.pallas_call(finish_kernel, grid=(pieces // RUN,), in_specs=[square, sq...  9.99 us
    pallas_call x2, Pallas kernels, pack_x(): pl.pallas_call(pack_x_kernel, in_specs=[SMEM, SMEM] + [ANY] * (len(arrive...  8.65 us
    pallas_call x1, Pallas kernels, decays(): pl.pallas_call(decay_kernel, in_specs=[SMEM, ANY, WHOLE, WHOLE, WHOLE], o...  7.23 us
  transfers between devices with their start and end apart: 19, of which 5 were waited for; matrix products, arithmetic and copies ran while one was open for 1% of the time, Pallas kernels for 26%

profile of v5, /device:TPU:98, one launch (start us, length us, event | category | flops | bytes accessed | tf_op | source)
XLA Modules:
  0.0 247.8 jit_solution(11445940950393902587)
XLA Ops:
  0.6 2.5 gather_small.1
  3.1 4.5 %all-to-all-start = ((bf16[8,2,272,128]{3,2,1,0:T(8,128)(2,1)}), bf16[8,2,272,128]{3,2,1,0:T(8,128)(2,1)S(1)}, u32[]{:S(2)}, u32[]{:S(2)}) async-start(bf16[8,2,272,128]{3,2,1,0:T(8,128)(2,1)} %gather_small.1), calls=%async_computation | async-start | bytes 2228224 | tf_op jit(solution)/shard_map/all_to_all | solution.py:691
  8.3 3.2 %cut.2 = (bf16[256,512]{1,0:T(8,128)(2,1)}, bf16[256,512]{1,0:T(8,128)(2,1)}, bf16[256,512]{1,0:T(8,128)(2,1)}, bf16[256,512]{1,0:T(8,128)(2,1)}, bf16[256,512]{...) custom-call(s32[8]{0:T(128)} %stack.48.dest_ref, ...), custom_call_target="tpu_custom_call" | custom-call | tf_op jit(solution)/shard_map/cut/pallas_call | solution.py:179
  13.8 13.5 %collective-permute-done.rest_0_ = bf16[256,512]{1,0:T(8,128)(2,1)S(1)} collective-permute-done((bf16[256,512]{1,0:T(8,128)(2,1)}, bf16[256,512]{1,0:T(8,128)(2,1)S(1)}, u32[]{:S(2)}, u32[]{:S(2)}) %collective-permute-start) | collective-permute-done | bytes 262176 | tf_op jit(solution)/shard_map/ppermute | solution.py:698
  29.1 7.5 %all-to-all-start.1 = ((bf16[32,288,128]{2,1,0:T(8,128)(2,1)}), bf16[32,288,128]{2,1,0:T(8,128)(2,1)S(1)}, u32[]{:S(2)}, u32[]{:S(2)}) async-start(bf16[32,288,128]{2,1,0:T(8,128)(2,1)} %pack_small.1), calls=%async_computation.1 | async-start | bytes 4718592 | tf_op jit(solution)/shard_map/all_to_all | solution.py:678
  42.1 3.2 %cut.3 = (bf16[256,512]{1,0:T(8,128)(2,1)}, bf16[256,512]{1,0:T(8,128)(2,1)}, bf16[256,512]{1,0:T(8,128)(2,1)}, bf16[256,512]{1,0:T(8,128)(2,1)}, bf16[256,512]{...) custom-call(s32[8]{0:T(128)} %stack.48.dest_ref, ...), custom_call_target="tpu_custom_call" | custom-call | tf_op jit(solution)/shard_map/cut/pallas_call | solution.py:179
  46.5 7.0 %collective-permute-done.4.rest_4_ = bf16[256,512]{1,0:T(8,128)(2,1)} collective-permute-done((bf16[256,512]{1,0:T(8,128)(2,1)}, bf16[256,512]{1,0:T(8,128)(2,1)}, u32[]{:S(2)}, u32[]{:S(2)}) %collective-permute-start.4) | collective-permute-done | bytes 262176 | tf_op jit(solution)/shard_map/ppermute | solution.py:698
  53.5 4.9 %collective-permute-done.5.rest_5_ = bf16[256,512]{1,0:T(8,128)(2,1)} collective-permute-done((bf16[256,512]{1,0:T(8,128)(2,1)}, bf16[256,512]{1,0:T(8,128)(2,1)}, u32[]{:S(2)}, u32[]{:S(2)}) %collective-permute-start.5) | collective-permute-done | bytes 262176 | tf_op jit(solution)/shard_map/ppermute | solution.py:698
  62.1 3.8 %pack_x.2 = bf16[32,128,512]{2,1,0:T(8,128)(2,1)} custom-call(s32[16]{0:T(128)S(1)} %multiply_add_fusion.slot_ref, s32[8]{0:T(128)S(1)} %stack.50.from_ref, bf16[256,512]{1,0:T(8,128)(2,1)S(1)} %copy-done.4, bf16[256,512]{1,0:T(8,128)(2,1)S(1)} %copy-done.6, bf16[256,512]{1,0:T(8,128)(2,1)} %collective-permute-done.2.rest_2_, ...), custom_call_target="tpu_custom_call" | custom-call | tf_op jit(solution)/shard_map/pack_x/pallas_call | solution.py:214
  66.6 7.9 %all-to-all-start.2 = ((bf16[32,128,512]{2,1,0:T(8,128)(2,1)}), bf16[32,128,512]{2,1,0:T(8,128)(2,1)}, u32[]{:S(2)}, u32[]{:S(2)}) async-start(bf16[32,128,512]{2,1,0:T(8,128)(2,1)} %pack_x.2), calls=%async_computation.2 | async-start | bytes 8388608 | tf_op jit(solution)/shard_map/all_to_all | solution.py:678
  77.3 2.9 %collective-permute-start.11 = (bf16[256,512]{1,0:T(8,128)(2,1)}, bf16[256,512]{1,0:T(8,128)(2,1)S(1)}, u32[]{:S(2)}, u32[]{:S(2)}) collective-permute-start(bf16[256,512]{1,0:T(8,128)(2,1)} %get-tuple-element.46), channel_id=1, source_target_pairs={{0,4},{1,5},{2,6},{3,7},{4,0},{5,1},{6,2},{7,3},{8,12},{9,13},{10,... | collective-permute-start | bytes 786440 | tf_op jit(solution)/shard_map/ppermute | solution.py:698
  80.6 4.5 %collective-permute-done.8.rest_1_ = bf16[256,512]{1,0:T(8,128)(2,1)S(1)} collective-permute-done((bf16[256,512]{1,0:T(8,128)(2,1)}, bf16[256,512]{1,0:T(8,128)(2,1)S(1)}, u32[]{:S(2)}, u32[]{:S(2)}) %collective-permute-start.8) | collective-permute-done | bytes 262176 | tf_op jit(solution)/shard_map/ppermute | solution.py:698
  85.1 12.8 %collective-permute-start.7 = (bf16[256,512]{1,0:T(8,128)(2,1)S(1)}, bf16[256,512]{1,0:T(8,128)(2,1)S(1)}, u32[]{:S(2)}, u32[]{:S(2)}) collective-permute-start(bf16[256,512]{1,0:T(8,128)(2,1)S(1)} %copy-done.10), channel_id=1, source_target_pairs={{0,2},{1,3},{2,4},{3,5},{4,6},{5,7},{6,0},{7,1},{8,10},{9,11},{10,... | collective-permute-start | bytes 786440 | tf_op jit(solution)/shard_map/ppermute | solution.py:698
  98.6 7.2 %decays.1 = (bf16[16,128,128]{2,1,0:T(8,128)(2,1)}, bf16[16,128,128]{2,1,0:T(8,128)(2,1)}, bf16[16,128,128]{2,1,0:T(8,128)(2,1)}, bf16[16,128,128]{2,1,0:T(8,128...) custom-call(s32[1,128]{1,0:T(1,128)} %copy-done.15, ...), custom_call_target="tpu_custom_call" | custom-call | tf_op jit(solution)/shard_map/decays/pallas_call | solution.py:336
  105.8 6.3 %leaving_gradient.1.rest_8_.refs_9_.g_ref = bf16[128,1024]{1,0:T(8,128)(2,1)} custom-call(bf16[2048,1024]{1,0:T(8,128)(2,1)} %refs_2_.1, bf16[16,128,128]{2,1,0:T(8,128)(2,1)} %get-tuple-element.50.keys_ref.refs_1_, bf16[16,128,128]{2,1,0:T(8,128)(2,1)} %get-tuple-element.41.scale_ref.refs_5_.refs_8_, bf16[4,128,1024]{2,1,0:T(8,128)(2,1)} %copy-done), custom_call_target="tpu_custom_call" | custom-call | tf_op jit(solution)/shard_map/leaving_gradient/pallas_call | solution.py:547
  112.2 15.8 %backward_local.1.rest_0_.g_ref = bf16[16,128,1024]{2,1,0:T(8,128)(2,1)} custom-call(s32[1,128]{1,0:T(1,128)} %copy-done.15, bf16[16,128,128]{2,1,0:T(8,128)(2,1)} %get-tuple-element.29.refs_0_.b_ref, bf16[16,128,128]{2,1,0:T(8,128)(2,1)} %get-tuple-element.50.keys_ref.refs_1_, bf16[2048,1024]{1,0:T(8,128)(2,1)} %refs_2_.1, ...), custom_call_target="tpu_custom_call" | custom-call | tf_op jit(solution)/shard_map/backward_local/pallas_call | solution.py:457
  128.1 4.8 %pack_x.3.value_ref = bf16[32,128,512]{2,1,0:T(8,128)(2,1)} custom-call(s32[16]{0:T(128)S(1)} %multiply_add_fusion.slot_ref, s32[8]{0:T(128)S(1)} %stack.50.from_ref, bf16[256,512]{1,0:T(8,128)(2,1)S(1)} %collective-permute-done.7.rest_0_, bf16[256,512]{1,0:T(8,128)(2,1)S(1)} %collective-permute-done.8.rest_1_, ...), custom_call_target="tpu_custom_call" | custom-call | tf_op jit(solution)/shard_map/pack_x/pallas_call | solution.py:214
  133.0 60.9 %all_to_all.30.xb_ref.refs_2_.refs_3_.refs_4_.refs_5_ = bf16[32,128,512]{2,1,0:T(8,128)(2,1)} all-to-all(bf16[32,128,512]{2,1,0:T(8,128)(2,1)} %hold.1), channel_id=1, replica_groups=mesh['ctx'=16,'head'=8] {'ctx'}, dimensions={0} | all-to-all | bytes 8388608 | tf_op jit(solution)/shard_map/all_to_all | solution.py:678
  193.9 6.8 %leaving.1.refs_12_ = bf16[16,16,1152]{2,1,0:T(8,128)(2,1)} custom-call(s32[1,128]{1,0:T(1,128)} %copy-done.15, bf16[32,128,512]{2,1,0:T(8,128)(2,1)} %all-to-all-done.2.xa_ref.refs_2_.refs_3_.refs_4_.refs_5_, bf16[32,128,512]{2,1,0:T(8,128)(2,1)} %all_to_all.30.xb_ref.refs_2_.refs_3_.refs_4_.refs_5_, ...), custom_call_target="tpu_custom_call" | custom-call | tf_op jit(solution)/shard_map/leaving/pallas_call | solution.py:587
  200.7 5.5 %all-to-all-start.4 = ((bf16[16,16,1152]{2,1,0:T(8,128)(2,1)}), bf16[16,16,1152]{2,1,0:T(8,128)(2,1)S(1)}, u32[]{:S(2)}, u32[]{:S(2)}) async-start(bf16[16,16,1152]{2,1,0:T(8,128)(2,1)} %leaving.1.refs_12_), calls=%async_computation.4 | async-start | bytes 1179648 | tf_op jit(solution)/shard_map/all_to_all | solution.py:678
  206.1 10.3 %forward_local.2.after_ref.ya_ref = bf16[16,128,512]{2,1,0:T(8,128)(2,1)} custom-call(s32[1,128]{1,0:T(1,128)} %copy-done.15, bf16[16,128,128]{2,1,0:T(8,128)(2,1)} %get-tuple-element.30.refs_0_.c_ref, bf16[16,128,128]{2,1,0:T(8,128)(2,1)} %get-tuple-element.31.keys_ref.refs_1_, bf16[32,128,512]{2,1,0:T(8,128)(2,1)} %all-to-all-done.2.xa_ref.refs_2_.refs_3_.refs_4_.refs_5_, ...), custom_call_target="tpu_custom_call" | custom-call | tf_op jit(solution)/shard_map/forward_local/pallas_call | solution.py:457
  219.5 7.2 %all-to-all-start.5 = ((bf16[16,16,1024]{2,1,0:T(8,128)(2,1)}), bf16[16,16,1024]{2,1,0:T(8,128)(2,1)S(1)}, u32[]{:S(2)}, u32[]{:S(2)}) async-start(bf16[16,16,1024]{2,1,0:T(8,128)(2,1)} %scan_owners.1.refs_12_), calls=%async_computation.5 | async-start | bytes 1048576 | tf_op jit(solution)/shard_map/all_to_all | solution.py:678
  226.7 10.3 %forward_local.3.yb_ref = bf16[16,128,512]{2,1,0:T(8,128)(2,1)} custom-call(s32[1,128]{1,0:T(1,128)} %copy-done.15, bf16[16,128,128]{2,1,0:T(8,128)(2,1)} %get-tuple-element.30.refs_0_.c_ref, bf16[16,128,128]{2,1,0:T(8,128)(2,1)} %get-tuple-element.31.keys_ref.refs_1_, bf16[32,128,512]{2,1,0:T(8,128)(2,1)} %all_to_all.30.xb_ref.refs_2_.refs_3_.refs_4_.refs_5_, ...), custom_call_target="tpu_custom_call" | custom-call | tf_op jit(solution)/shard_map/forward_local/pallas_call | solution.py:457
  237.8 10.0 %finish.1 = (bf16[2048,1024]{1,0:T(8,128)(2,1)}, bf16[2048,1024]{1,0:T(8,128)(2,1)}) custom-call(bf16[16,128,128]{2,1,0:T(8,128)(2,1)} %get-tuple-element.29.refs_0_.b_ref, bf16[16,128,128]{2,1,0:T(8,128)(2,1)} %get-tuple-element.30.refs_0_.c_ref, bf16[16,128,512]{2,1,0:T(8,128)(2,1)} %forward_local.2.after_ref.ya_ref, ...), custom_call_target="tpu_custom_call" | custom-call | tf_op jit(solution)/shard_map/finish/pallas_call | solution.py:649
  (94 shorter events, 23.4 us)
Async XLA Ops:
  3.1 24.2 %all-to-all-start = ((bf16[8,2,272,128]{3,2,1,0:T(8,128)(2,1)}), bf16[8,2,272,128]{3,2,1,0:T(8,128)(2,1)S(1)}, u32[]{:S(2)}, u32[]{:S(2)}) async-start(bf16[8,2,272,128]{3,2,1,0:T(8,128)(2,1)} %gather_small.1), calls=%async_computation | async-start | bytes 2228224 | tf_op jit(solution)/shard_map/all_to_all | solution.py:691
  11.5 15.8 %collective-permute-start = (bf16[256,512]{1,0:T(8,128)(2,1)}, bf16[256,512]{1,0:T(8,128)(2,1)S(1)}, u32[]{:S(2)}, u32[]{:S(2)}) collective-permute-start(bf16[256,512]{1,0:T(8,128)(2,1)} %get-tuple-element.27), channel_id=1, source_target_pairs={{0,2},{1,3},{2,4},{3,5},{4,6},{5,7},{6,0},{7,1},{8,10},{9,11},{10,... | collective-permute-start | bytes 786440 | tf_op jit(solution)/shard_map/ppermute | solution.py:698
  11.6 15.7 %collective-permute-start.1 = (bf16[256,512]{1,0:T(8,128)(2,1)}, bf16[256,512]{1,0:T(8,128)(2,1)S(1)}, u32[]{:S(2)}, u32[]{:S(2)}) collective-permute-start(bf16[256,512]{1,0:T(8,128)(2,1)} %get-tuple-element.28), channel_id=1, source_target_pairs={{0,6},{1,7},{2,0},{3,1},{4,2},{5,3},{6,4},{7,5},{8,14},{9,15},{10,... | collective-permute-start | bytes 786440 | tf_op jit(solution)/shard_map/ppermute | solution.py:698
  29.1 37.5 %all-to-all-start.1 = ((bf16[32,288,128]{2,1,0:T(8,128)(2,1)}), bf16[32,288,128]{2,1,0:T(8,128)(2,1)S(1)}, u32[]{:S(2)}, u32[]{:S(2)}) async-start(bf16[32,288,128]{2,1,0:T(8,128)(2,1)} %pack_small.1), calls=%async_computation.1 | async-start | bytes 4718592 | tf_op jit(solution)/shard_map/all_to_all | solution.py:678
  36.6 9.8 %collective-permute-start.2 = (bf16[256,512]{1,0:T(8,128)(2,1)}, bf16[256,512]{1,0:T(8,128)(2,1)}, u32[]{:S(2)}, u32[]{:S(2)}) collective-permute-start(bf16[256,512]{1,0:T(8,128)(2,1)} %get-tuple-element.32), channel_id=1, source_target_pairs={{0,3},{1,2},{2,5},{3,4},{4,7},{5,6},{6,1},{7,0},{8,11},{9,10},{10,... | collective-permute-start | bytes 786440 | tf_op jit(solution)/shard_map/ppermute | solution.py:698
  37.8 8.7 %collective-permute-start.3 = (bf16[256,512]{1,0:T(8,128)(2,1)}, bf16[256,512]{1,0:T(8,128)(2,1)}, u32[]{:S(2)}, u32[]{:S(2)}) collective-permute-start(bf16[256,512]{1,0:T(8,128)(2,1)} %get-tuple-element.33), channel_id=1, source_target_pairs={{0,7},{1,6},{2,1},{3,0},{4,3},{5,2},{6,5},{7,4},{8,15},{9,14},{10,... | collective-permute-start | bytes 786440 | tf_op jit(solution)/shard_map/ppermute | solution.py:698
  38.3 15.1 %collective-permute-start.4 = (bf16[256,512]{1,0:T(8,128)(2,1)}, bf16[256,512]{1,0:T(8,128)(2,1)}, u32[]{:S(2)}, u32[]{:S(2)}) collective-permute-start(bf16[256,512]{1,0:T(8,128)(2,1)} %get-tuple-element.34), channel_id=1, source_target_pairs={{0,4},{1,5},{2,6},{3,7},{4,0},{5,1},{6,2},{7,3},{8,12},{9,13},{10,... | collective-permute-start | bytes 786440 | tf_op jit(solution)/shard_map/ppermute | solution.py:698
  40.4 18.0 %collective-permute-start.5 = (bf16[256,512]{1,0:T(8,128)(2,1)}, bf16[256,512]{1,0:T(8,128)(2,1)}, u32[]{:S(2)}, u32[]{:S(2)}) collective-permute-start(bf16[256,512]{1,0:T(8,128)(2,1)} %get-tuple-element.35), channel_id=1, source_target_pairs={{0,5},{1,4},{2,7},{3,6},{4,1},{5,0},{6,3},{7,2},{8,13},{9,12},{10,... | collective-permute-start | bytes 786440 | tf_op jit(solution)/shard_map/ppermute | solution.py:698
  41.9 16.4 %collective-permute-start.6 = (bf16[256,512]{1,0:T(8,128)(2,1)}, bf16[256,512]{1,0:T(8,128)(2,1)}, u32[]{:S(2)}, u32[]{:S(2)}) collective-permute-start(bf16[256,512]{1,0:T(8,128)(2,1)} %get-tuple-element.36), channel_id=1, source_target_pairs={{0,1},{1,0},{2,3},{3,2},{4,5},{5,4},{6,7},{7,6},{8,9},{9,8},{10,11... | collective-permute-start | bytes 786440 | tf_op jit(solution)/shard_map/ppermute | solution.py:698
  45.5 20.4 %copy-start.12 = (f32[16,1]{1,0:T(8,128)}, f32[16,1]{1,0:T(8,128)S(1)}, u32[]{:S(2)}) copy-start(f32[16,1]{1,0:T(8,128)S(1)} %copy.20.alog_ref.rest_10_) | copy-start | bytes 196
  45.6 20.3 %copy-start.13 = (f32[16,1]{1,0:T(8,128)}, f32[16,1]{1,0:T(8,128)S(1)}, u32[]{:S(2)}) copy-start(f32[16,1]{1,0:T(8,128)S(1)} %copy.19.bias_ref.rest_9_) | copy-start | bytes 196
  45.9 20.0 %copy-start.14 = (f32[16,1,128]{2,1,0:T(1,128)}, f32[16,1,128]{2,1,0:T(1,128)S(1)}, u32[]{:S(2)}) copy-start(f32[16,1,128]{2,1,0:T(1,128)S(1)} %convert_element_type.30.seg_ref.rest_8_) | copy-start | bytes 24580
  46.1 19.9 %copy-start.11 = (f32[1,1024]{1,0:T(1,128)}, f32[1,1024]{1,0:T(1,128)S(1)}, u32[]{:S(2)}) copy-start(f32[1,1024]{1,0:T(1,128)S(1)} %reshape_reshape.3.rest_11_.refs_8_.refs_11_) | copy-start | bytes 12292
  66.6 31.4 %copy-start.1 = (bf16[32,288,128]{2,1,0:T(8,128)(2,1)}, bf16[32,288,128]{2,1,0:T(8,128)(2,1)S(1)}, u32[]{:S(2)}) copy-start(bf16[32,288,128]{2,1,0:T(8,128)(2,1)S(1)} %all-to-all-done.1.small_ref) | copy-start | bytes 7077892
  66.6 66.4 %all-to-all-start.2 = ((bf16[32,128,512]{2,1,0:T(8,128)(2,1)}), bf16[32,128,512]{2,1,0:T(8,128)(2,1)}, u32[]{:S(2)}, u32[]{:S(2)}) async-start(bf16[32,128,512]{2,1,0:T(8,128)(2,1)} %pack_x.2), calls=%async_computation.2 | async-start | bytes 8388608 | tf_op jit(solution)/shard_map/all_to_all | solution.py:678
  74.4 10.7 %collective-permute-start.8 = (bf16[256,512]{1,0:T(8,128)(2,1)}, bf16[256,512]{1,0:T(8,128)(2,1)S(1)}, u32[]{:S(2)}, u32[]{:S(2)}) collective-permute-start(bf16[256,512]{1,0:T(8,128)(2,1)} %get-tuple-element.43), channel_id=1, source_target_pairs={{0,6},{1,7},{2,0},{3,1},{4,2},{5,3},{6,4},{7,5},{8,14},{9,15},{10,... | collective-permute-start | bytes 786440 | tf_op jit(solution)/shard_map/ppermute | solution.py:698
  75.6 9.5 %collective-permute-start.9 = (bf16[256,512]{1,0:T(8,128)(2,1)}, bf16[256,512]{1,0:T(8,128)(2,1)S(1)}, u32[]{:S(2)}, u32[]{:S(2)}) collective-permute-start(bf16[256,512]{1,0:T(8,128)(2,1)} %get-tuple-element.44), channel_id=1, source_target_pairs={{0,3},{1,2},{2,5},{3,4},{4,7},{5,6},{6,1},{7,0},{8,11},{9,10},{10,... | collective-permute-start | bytes 786440 | tf_op jit(solution)/shard_map/ppermute | solution.py:698
  76.2 51.8 %collective-permute-start.10 = (bf16[256,512]{1,0:T(8,128)(2,1)}, bf16[256,512]{1,0:T(8,128)(2,1)S(1)}, u32[]{:S(2)}, u32[]{:S(2)}) collective-permute-start(bf16[256,512]{1,0:T(8,128)(2,1)} %get-tuple-element.45), channel_id=1, source_target_pairs={{0,7},{1,6},{2,1},{3,0},{4,3},{5,2},{6,5},{7,4},{8,15},{9,14},{10,... | collective-permute-start | bytes 786440 | tf_op jit(solution)/shard_map/ppermute | solution.py:698
  77.3 50.7 %collective-permute-start.11 = (bf16[256,512]{1,0:T(8,128)(2,1)}, bf16[256,512]{1,0:T(8,128)(2,1)S(1)}, u32[]{:S(2)}, u32[]{:S(2)}) collective-permute-start(bf16[256,512]{1,0:T(8,128)(2,1)} %get-tuple-element.46), channel_id=1, source_target_pairs={{0,4},{1,5},{2,6},{3,7},{4,0},{5,1},{6,2},{7,3},{8,12},{9,13},{10,... | collective-permute-start | bytes 786440 | tf_op jit(solution)/shard_map/ppermute | solution.py:698
  80.2 47.8 %collective-permute-start.12 = (bf16[256,512]{1,0:T(8,128)(2,1)}, bf16[256,512]{1,0:T(8,128)(2,1)S(1)}, u32[]{:S(2)}, u32[]{:S(2)}) collective-permute-start(bf16[256,512]{1,0:T(8,128)(2,1)} %get-tuple-element.47), channel_id=1, source_target_pairs={{0,5},{1,4},{2,7},{3,6},{4,1},{5,0},{6,3},{7,2},{8,13},{9,12},{10,... | collective-permute-start | bytes 786440 | tf_op jit(solution)/shard_map/ppermute | solution.py:698
  85.1 42.9 %collective-permute-start.13 = (bf16[256,512]{1,0:T(8,128)(2,1)}, bf16[256,512]{1,0:T(8,128)(2,1)S(1)}, u32[]{:S(2)}, u32[]{:S(2)}) collective-permute-start(bf16[256,512]{1,0:T(8,128)(2,1)} %get-tuple-element.48), channel_id=1, source_target_pairs={{0,1},{1,0},{2,3},{3,2},{4,5},{5,4},{6,7},{7,6},{8,9},{9,8},{10,11... | collective-permute-start | bytes 786440 | tf_op jit(solution)/shard_map/ppermute | solution.py:698
  85.1 42.9 %collective-permute-start.7 = (bf16[256,512]{1,0:T(8,128)(2,1)S(1)}, bf16[256,512]{1,0:T(8,128)(2,1)S(1)}, u32[]{:S(2)}, u32[]{:S(2)}) collective-permute-start(bf16[256,512]{1,0:T(8,128)(2,1)S(1)} %copy-done.10), channel_id=1, source_target_pairs={{0,2},{1,3},{2,4},{3,5},{4,6},{5,7},{6,0},{7,1},{8,10},{9,11},{10,... | collective-permute-start | bytes 786440 | tf_op jit(solution)/shard_map/ppermute | solution.py:698
  200.7 15.7 %all-to-all-start.4 = ((bf16[16,16,1152]{2,1,0:T(8,128)(2,1)}), bf16[16,16,1152]{2,1,0:T(8,128)(2,1)S(1)}, u32[]{:S(2)}, u32[]{:S(2)}) async-start(bf16[16,16,1152]{2,1,0:T(8,128)(2,1)} %leaving.1.refs_12_), calls=%async_computation.4 | async-start | bytes 1179648 | tf_op jit(solution)/shard_map/all_to_all | solution.py:678
  219.5 17.5 %all-to-all-start.5 = ((bf16[16,16,1024]{2,1,0:T(8,128)(2,1)}), bf16[16,16,1024]{2,1,0:T(8,128)(2,1)S(1)}, u32[]{:S(2)}, u32[]{:S(2)}) async-start(bf16[16,16,1024]{2,1,0:T(8,128)(2,1)} %scan_owners.1.refs_12_), calls=%async_computation.5 | async-start | bytes 1048576 | tf_op jit(solution)/shard_map/all_to_all | solution.py:678
  (18 other events, 99.1 us)
